TPU v7x, 128 devices: a whole 4x4x4 slice. The times are simulated.
128 devices in a mesh: blk: 32 (over y, x, z_hi), occ: 4 (over z_lo, core).
Axes of the slice: x: 4, y: 4, z: 4 (z_hi: 2, z_lo: 2; z = z_hi * 2 + z_lo), core: 2. Of those that a mesh axis runs over, the one named last changes fastest.
Arguments:
- amplitudes: bfloat16 [64, 64, 49152], P('occ', None, 'blk'), may hold values from -6 to 6
- integrals: bfloat16 [49152, 4608], P('blk'), may hold values from -0.25 to 0.25
- pair_irrep: int32 [49152], replicated, may hold values from 0 to 7, as said below
- pair_energy: float32 [49152], P('blk'), may hold values from 0.5 to 3
- occ_energy: float32 [64], replicated, may hold values from -1.5 to -0.3
Outputs:
- update: float32 [64, 64, 49152], P('occ', None, 'blk')
Inputs may be any that keep to these rules, and one draw needn't show every extreme that they name: `pair_irrep`: labels are constant over aligned runs of 128 pairs and are non-decreasing within each block of 1536 pairs.
All inputs are finite; a program needn't handle non-finite values.
Results may differ from a plain program's by a relative error of at most 0.0003.
Values may be sent and summed in bfloat16 or wider, within the bound.
No kernel may reach another device: no remote copies, remote signals or barrier semaphores. Data moves between devices by JAX's collectives and lax.ppermute only.
A program may use at most 128 MiB of HBM per device.

v0:
```python
import jax
import jax.numpy as jnp
from jax import lax
from jax.sharding import PartitionSpec as P


def from_behind(value, axis, by):
    length = lax.axis_size(axis)
    return lax.ppermute(value, axis, [(i, (i + by) % length) for i in range(length)])


def masked(slab, labels, row_block, col_block, width):
    rows = lax.dynamic_slice_in_dim(labels, row_block * width, width)
    cols = lax.dynamic_slice_in_dim(labels, col_block * width, width)
    return jnp.where(rows[:, None] == cols[None, :], slab, jnp.zeros((), slab.dtype))


def per_device(amplitudes, integrals, pair_irrep, pair_energy, occ_energy):
    width = amplitudes.shape[2]
    nocc = amplitudes.shape[1]
    i_local = amplitudes.shape[0]
    count = lax.axis_size("blk")
    here = lax.axis_index("blk")
    left = amplitudes.reshape(i_local * nocc, width)
    ladder = jnp.dot(
        left,
        masked(integrals[:, :width], pair_irrep, here, here, width),
        preferred_element_type=jnp.float32,
    )
    carried = (left, integrals[:, width:])
    for step in range(1, 3):
        got_left, got_slab = from_behind((carried[0], carried[1]), "blk", 1)
        source = (here - step) % count
        ladder = ladder + jnp.dot(
            got_left,
            masked(got_slab[:, :width], pair_irrep, source, here, width),
            preferred_element_type=jnp.float32,
        )
        carried = (got_left, got_slab[:, width:])
    ladder = ladder.reshape(i_local, nocc, width)
    received = lax.all_to_all(ladder, "occ", split_axis=1, concat_axis=0, tiled=True)
    swapped = ladder - received.transpose(1, 0, 2)
    own_energy = lax.dynamic_slice_in_dim(occ_energy, lax.axis_index("occ") * i_local, i_local)
    denominator = pair_energy[None, None, :] - own_energy[:, None, None] - occ_energy[None, :, None]
    return swapped / denominator


def solution(mesh):
    placed = (P("occ", None, "blk"), P("blk", None), P(), P("blk"), P())
    return jax.shard_map(
        per_device, mesh=mesh, in_specs=placed, out_specs=P("occ", None, "blk"), check_vma=False
    )
```

profile of v0, /device:TPU:1, one launch (start us, length us, event | category | flops | bytes accessed | tf_op | source)
XLA Modules:
  0.0 559.4 jit_solution(2184772412386598489)
XLA Ops:
  0.0 0.0 copy-start.6
  0.0 8.3 %slice.13 = bf16[1536,3072]{1,0:T(8,128)(2,1)} slice(bf16[1536,4608]{1,0:T(8,128)(2,1)} %param.6), slice={[0:1536], [1536:4608]} | slice | bytes 18874368 | tf_op jit(solution)/shard_map/slice | solution.py:30
  8.3 4.4 collective-permute-start
  12.8 0.0 copy-done.6
  12.8 0.3 collective-permute-start.1
  13.1 207.2 %collective-permute-done = bf16[1536,3072]{1,0:T(8,128)(2,1)S(1)} collective-permute-done((bf16[1536,3072]{1,0:T(8,128)(2,1)}, bf16[1536,3072]{1,0:T(8,128)(2,1)S(1)}, u32[]{:S(2)}, u32[]{:S(2)}) %collective-permute-start) | collective-permute-done | bytes 9437216 | tf_op jit(solution)/shard_map/ppermute | solution.py:9
  220.3 0.0 copy-start.2
  220.3 3.6 copy-done.2
  223.9 2.6 slice.17
  226.5 0.0 collective-permute-start.2
  226.5 61.2 %collective-permute-done.1 = bf16[1024,1536]{1,0:T(8,128)(2,1)} collective-permute-done((bf16[1024,1536]{1,0:T(8,128)(2,1)S(1)}, bf16[1024,1536]{1,0:T(8,128)(2,1)}, u32[]{:S(2)}, u32[]{:S(2)}) %collective-permute-start.1) | collective-permute-done | bytes 3145760 | tf_op jit(solution)/shard_map/ppermute | solution.py:9
  287.8 0.0 collective-permute-start.3
  287.8 0.9 fusion.18
  288.6 0.0 copy-start.3
  288.6 7.5 %fusion.1 = f32[1536,1024]{0,1:T(8,128)S(1)} fusion(bf16[1024,1536]{1,0:T(8,128)(2,1)S(1)} %bitcast.19, bf16[1536,4608]{1,0:T(8,128)(2,1)} %param.6, s32[1536]{0:T(1024)S(1)} %get-tuple-element.6), kind=kOutput, calls=%fused_computation.6 | convolution fusion | flops 4836556800 | bytes 14172160 | tf_op jit(solution)/shard_map/dot_general | solution.py:25
  296.1 0.0 copy-done.3
  296.1 7.0 %fusion.2 = f32[1536,1024]{0,1:T(8,128)S(1)} fusion(bf16[1024,1536]{1,0:T(8,128)(2,1)} %collective-permute-done.1, bf16[1536,3072]{1,0:T(8,128)(2,1)S(1)} %copy-done.3, s32[1536]{0:T(1024)S(1)} %get-tuple-element.6, s32[1536]{0:T(1024)S(1)} %get-tuple-element.7), kind=kOutput, calls=%fused_computation.7 | convolution fusion | flops 4836556800 | bytes 14172160 | tf_op jit(solution)/shard_map/dot_general | solution.py:34
  303.2 153.1 %collective-permute-done.3 = bf16[1024,1536]{1,0:T(8,128)(2,1)} collective-permute-done((bf16[1024,1536]{1,0:T(8,128)(2,1)}, bf16[1024,1536]{1,0:T(8,128)(2,1)}, u32[]{:S(2)}, u32[]{:S(2)}) %collective-permute-start.3) | collective-permute-done | bytes 3145760 | tf_op jit(solution)/shard_map/ppermute | solution.py:9
  456.3 0.0 collective-permute-done.2
  456.3 8.6 %add_add_fusion = f32[1536,1024]{0,1:T(8,128)S(1)} fusion(f32[1536,1024]{0,1:T(8,128)S(1)} %fusion.1, f32[1536,1024]{0,1:T(8,128)S(1)} %fusion.2, bf16[1024,1536]{1,0:T(8,128)(2,1)} %collective-permute-done.3, bf16[1536,1536]{1,0:T(8,128)(2,1)} %collective-permute-done.2, s32[1536]{0:T(1024)S(1)} %get-tuple-element.6, s32[1536]{0:T(1024)S(1)} %get-tuple-element.5), kind=kOutput, calls=%fused_computation.5 | convolution fusion | flops 4839702528 | bytes 26750976 | tf_op jit(solution)/shard_map/dot_general | solution.py:34
  465.0 0.0 copy-start
  465.0 2.7 copy-done
  467.7 6.3 %copy.7 = f32[16,64,1536]{2,0,1:T(8,128)} copy(f32[16,64,1536]{2,1,0:T(8,128)S(1)} %bitcast.16) | data formatting | bytes 12582912 | tf_op jit(solution)/shard_map/reshape | solution.py:40
  474.0 0.0 copy-start.5
  474.0 0.0 copy-start.4
  474.0 6.6 %all-to-all-start = ((f32[16,64,1536]{2,0,1:T(8,128)}), f32[16,64,1536]{2,0,1:T(8,128)}, u32[]{:S(2)}, u32[]{:S(2)}) async-start(f32[16,64,1536]{2,0,1:T(8,128)} %copy.7), calls=%async_computation | async-start | bytes 12582912 | tf_op jit(solution)/shard_map/all_to_all | solution.py:41
  480.5 0.0 copy-done.5
  480.5 0.1 dynamic_slice.18
  480.6 0.0 copy-done.4
  480.6 0.1 broadcast_subtract_fusion
  480.7 69.7 %all-to-all-done = f32[16,64,1536]{2,0,1:T(8,128)} async-done(((f32[16,64,1536]{2,0,1:T(8,128)}), f32[16,64,1536]{2,0,1:T(8,128)}, u32[]{:S(2)}, u32[]{:S(2)}) %all-to-all-start) | async-done | bytes 6291488 | tf_op jit(solution)/shard_map/all_to_all | solution.py:41
  550.4 0.0 copy-start.1
  550.4 3.7 copy.8
  554.1 0.9 copy-done.1
  555.0 4.4 fusion
Async XLA Ops:
  0.0 12.8 %copy-start.6 = (bf16[16,64,1536]{2,1,0:T(8,128)(2,1)S(1)}, bf16[16,64,1536]{2,1,0:T(8,128)(2,1)}, u32[]{:S(2)}) copy-start(bf16[16,64,1536]{2,1,0:T(8,128)(2,1)} %param.5) | copy-start | bytes 9437188
  8.3 211.9 %collective-permute-start = (bf16[1536,3072]{1,0:T(8,128)(2,1)}, bf16[1536,3072]{1,0:T(8,128)(2,1)S(1)}, u32[]{:S(2)}, u32[]{:S(2)}) collective-permute-start(bf16[1536,3072]{1,0:T(8,128)(2,1)} %slice.13), channel_id=1, source_target_pairs={{0,4},{4,8},{8,12},{12,16},{16,20},{20,24},{24,28},{28,32},{32,36}... | collective-permute-start | bytes 28311560 | tf_op jit(solution)/shard_map/ppermute | solution.py:9
  12.8 275.0 %collective-permute-start.1 = (bf16[1024,1536]{1,0:T(8,128)(2,1)S(1)}, bf16[1024,1536]{1,0:T(8,128)(2,1)}, u32[]{:S(2)}, u32[]{:S(2)}) collective-permute-start(bf16[1024,1536]{1,0:T(8,128)(2,1)S(1)} %bitcast.18), channel_id=1, source_target_pairs={{0,4},{4,8},{8,12},{12,16},{16,20},{20,24},{24,28},{28,32},{32,36}... | collective-permute-start | bytes 9437192 | tf_op jit(solution)/shard_map/ppermute | solution.py:9
  220.3 3.6 copy-start.2
  226.5 229.8 %collective-permute-start.2 = (bf16[1536,1536]{1,0:T(8,128)(2,1)}, bf16[1536,1536]{1,0:T(8,128)(2,1)}, u32[]{:S(2)}, u32[]{:S(2)}) collective-permute-start(bf16[1536,1536]{1,0:T(8,128)(2,1)} %slice.17), channel_id=1, source_target_pairs={{0,4},{4,8},{8,12},{12,16},{16,20},{20,24},{24,28},{28,32},{32,36}... | collective-permute-start | bytes 14155784 | tf_op jit(solution)/shard_map/ppermute | solution.py:9
  287.8 168.5 %collective-permute-start.3 = (bf16[1024,1536]{1,0:T(8,128)(2,1)}, bf16[1024,1536]{1,0:T(8,128)(2,1)}, u32[]{:S(2)}, u32[]{:S(2)}) collective-permute-start(bf16[1024,1536]{1,0:T(8,128)(2,1)} %collective-permute-done.1), channel_id=1, source_target_pairs={{0,4},{4,8},{8,12},{12,16},{16,20},{20,24},{24,28},{28,32},{32,36}... | collective-permute-start | bytes 9437192 | tf_op jit(solution)/shard_map/ppermute | solution.py:9
  288.6 7.5 %copy-start.3 = (bf16[1536,3072]{1,0:T(8,128)(2,1)S(1)}, bf16[1536,3072]{1,0:T(8,128)(2,1)}, u32[]{:S(2)}) copy-start(bf16[1536,3072]{1,0:T(8,128)(2,1)} %copy-done.2) | copy-start | bytes 28311556
  465.0 2.7 copy-start
  474.0 6.6 %copy-start.5 = (f32[64]{0:T(128)S(1)}, f32[64]{0:T(128)}, u32[]{:S(2)}) copy-start(f32[64]{0:T(128)} %param.9) | copy-start | bytes 772
  474.0 6.6 %copy-start.4 = (f32[1536]{0:T(1024)S(1)}, f32[1536]{0:T(1024)}, u32[]{:S(2)}) copy-start(f32[1536]{0:T(1024)} %param.8) | copy-start | bytes 18436
  474.0 76.4 %all-to-all-start = ((f32[16,64,1536]{2,0,1:T(8,128)}), f32[16,64,1536]{2,0,1:T(8,128)}, u32[]{:S(2)}, u32[]{:S(2)}) async-start(f32[16,64,1536]{2,0,1:T(8,128)} %copy.7), calls=%async_computation | async-start | bytes 12582912 | tf_op jit(solution)/shard_map/all_to_all | solution.py:41
  550.4 4.6 copy-start.1
where the time goes:
time: 560 us; the launch traced here: 559 us
  waiting for transfers between devices  491 us (88%)
  local copies, waits for them, and re-layouts  29.1 us (5%)
  matrix products  23.2 us (4%)
  starting transfers between devices  11.3 us (2%)
    ppermute x4, waiting for transfers between devices, from_behind(): lax.ppermute(value, axis, [(i, (i + by) % length) for i in range(length)])  422 us
    all_to_all x1, waiting for transfers between devices, per_device(): lax.all_to_all(ladder, 'occ', split_axis=1, concat_axis=0, tiled=True)  69.7 us
    dot_general x2, matrix products, per_device(): jnp.dot(got_left, masked(got_slab[:, :width], pair_irrep, source, here, w...  15.7 us
  transfers between devices with their start and end apart: 5, of which 4 were waited for; matrix products, arithmetic and copies ran while one was open for 3% of the time, Pallas kernels for 0%

commit v1 on v0

v1 whole, which is shorter than its diff:
```python
import functools

import jax
import jax.numpy as jnp
from jax import lax
from jax.experimental import pallas as pl
from jax.experimental.pallas import tpu as pltpu
from jax.sharding import PartitionSpec as P

BOTH = ("blk", "occ")
RUN = 128
OCT = 8
G = 128
PAD = 16
LEVELS = 32000.0
STEPS = 256.0
VMEM = 60 * 1024 * 1024


def routes(where):
    pairs = []
    for blk in range(32):
        for occ in range(4):
            to_blk, to_occ = where(blk, occ)
            pairs.append((blk * 4 + occ, (to_blk % 32) * 4 + to_occ))
    return pairs


def send(value, where):
    return lax.ppermute(value, BOTH, routes(where))


def encode(value, out_ref):
    rows = value.shape[0]
    most = jnp.max(jnp.abs(value), axis=0, keepdims=True)
    code = jnp.ceil(jnp.log2(jnp.maximum(most, 2.0**-120)) * STEPS)
    up = jnp.exp2(code * (-1.0 / STEPS)) * LEVELS
    coded = jnp.clip(jnp.round(value * up), -32767.0, 32767.0)
    out_ref[:rows, :] = coded.astype(jnp.int32).astype(jnp.int16)
    scale = jnp.broadcast_to(code.astype(jnp.int32), (PAD, value.shape[1]))
    out_ref[rows:, :] = scale.astype(jnp.int16)


def decode(ref):
    rows = ref.shape[0] - PAD
    code = ref[rows:, :].astype(jnp.int32).astype(jnp.float32)[:1]
    down = jnp.exp2(code * (1.0 / STEPS)) * (1.0 / LEVELS)
    return ref[:rows, :].astype(jnp.int32).astype(jnp.float32) * down


def iotas(rows, cols):
    return (
        lax.broadcasted_iota(jnp.int32, (rows, cols), 0),
        lax.broadcasted_iota(jnp.int32, (rows, cols), 1),
    )


def flip_matrix(octet_flip):
    row, col = iotas(G, G)
    a, x, y = row >> 6, (row >> 3) & 7, row & 7
    source = ((a ^ octet_flip) << 6) | (y << 3) | x
    return (col == source).astype(jnp.float32).astype(jnp.bfloat16)


def own_pairs():
    row, col = iotas(G, 256)
    q = row - 64
    octet, d, x = q >> 5, ((q >> 3) & 3) + 1, q & 7
    low = row < 64
    i = jnp.where(low, row >> 3, octet * 8 + x)
    j = jnp.where(low, 8 + (row & 7), octet * 8 + ((x + d) & 7))
    return i, j, col


def dot(a, b):
    return jnp.dot(a, b, preferred_element_type=jnp.float32)


def split_kernel(meta, t_ref, *outs):
    g, zh = meta[1], meta[2]
    for d in (1, 2, 3):
        stay, go = outs[2 * (d - 1)], outs[2 * (d - 1) + 1]
        p = g ^ d
        s = meta[2 + d]
        for a in range(2):
            for x in range(OCT):
                both = t_ref[a * OCT + x, pl.ds(pl.multiple_of(p * 16, 16), 16), :].astype(jnp.float32)
                first, second = both[:OCT], both[OCT:]
                take = (a ^ s) == 0
                keep = jnp.where(take, first, second)
                other = jnp.where(take, second, first)
                at = a * 64 + x * OCT
                if x % 2 == 0:
                    keep0, other0 = keep, other
                else:
                    stay[at - OCT : at + OCT, :] = jnp.concatenate([keep0, keep]).astype(jnp.bfloat16)
                    go[at - OCT : at + OCT, :] = jnp.concatenate([other0, other]).astype(jnp.bfloat16)
    own = t_ref[:, pl.ds(pl.multiple_of(g * 16, 16), 16), :].reshape(256, t_ref.shape[2])
    i, j, col = own_pairs()
    for out, source in ((outs[6], i * 16 + j), (outs[7], j * 16 + i)):
        pick = (col == source).astype(jnp.float32).astype(jnp.bfloat16)
        out[...] = dot(pick, own).astype(jnp.bfloat16)


def partial_kernel(groups, kinds, meta, lab, *refs):
    n = len(groups)
    xs, ys, v_ref = refs[:n], refs[n : 2 * n], refs[2 * n]
    outs = refs[2 * n + 1 : 2 * n + 4]
    lhs, vbuf, acc, todo, sems = refs[2 * n + 4 :]
    width = v_ref.shape[0]
    runs = width // RUN
    k = meta[0]
    zh = meta[2]
    rows = [lab[k * runs + r] for r in range(runs)]

    def tile(s, c, r):
        at = (pl.ds(pl.multiple_of(r * RUN, RUN), RUN), pl.ds(pl.multiple_of(s * width + c * RUN, RUN), RUN))
        return pltpu.make_async_copy(v_ref.at[at], vbuf.at[at], sems.at[s])

    ends = [jnp.int32(0)]
    for s in range(3):
        block = lax.rem(k + s, 32)

        def column(c, count, s=s, block=block):
            label = lab[block * runs + c]
            first = sum((row < label).astype(jnp.int32) for row in rows)
            last = first + sum((row == label).astype(jnp.int32) for row in rows)

            def one(r, count):
                tile(s, c, r).start()
                todo[count] = c * 16 + r
                return count + 1

            return lax.fori_loop(first, last, one, count)

        ends.append(lax.fori_loop(0, runs, column, ends[-1]))

    for at, d in enumerate(groups):
        x, y = xs[at][...], ys[at][...]
        if d >= 2:
            x, y = jnp.where(zh == 1, y, x), jnp.where(zh == 1, x, y)
        if d >= 1:
            y = dot(flip_matrix(meta[2 + d]), y).astype(jnp.bfloat16)
        y = -y
        for r in range(runs):
            lhs[at * G : (at + 1) * G, 2 * r * RUN : (2 * r + 1) * RUN] = x[:, r * RUN : (r + 1) * RUN]
            lhs[at * G : (at + 1) * G, (2 * r + 1) * RUN : (2 * r + 2) * RUN] = y[:, r * RUN : (r + 1) * RUN]
    acc[...] = jnp.zeros_like(acc)

    for s in range(3):
        start, end = ends[s], ends[s + 1]

        def arrived(_, c, s=s):
            tile(s, 0, 0).wait()
            return c

        lax.fori_loop(start, end, arrived, 0)

        def several(base, many, s=s):
            got = []
            for u in range(many):
                entry = todo[base + u]
                c, r = entry >> 4, entry & 15
                right = vbuf[
                    pl.ds(pl.multiple_of(r * RUN, RUN), RUN), pl.ds(pl.multiple_of(s * width + c * RUN, RUN), RUN)
                ]
                left = lhs[:, pl.ds(pl.multiple_of(r * 2 * RUN, 2 * RUN), 2 * RUN)]
                got.append((c, dot(left, jnp.concatenate([right, right], axis=0))))
            for c, value in got:
                acc[s, :, pl.ds(pl.multiple_of(c * RUN, RUN), RUN)] += value

        fours = (end - start) >> 2

        def four(at, carry, start=start):
            several(start + at * 4, 4)
            return carry

        def single(at, carry):
            several(at, 1)
            return carry

        lax.fori_loop(0, fours, four, 0)
        lax.fori_loop(start + fours * 4, end, single, 0)
        if kinds[s]:
            encode(acc[s], outs[s])
        else:
            outs[s][...] = acc[s]


def merge_kernel(meta, mine_ref, got_ref, out_ref):
    encode(mine_ref[...] + jnp.where(meta[2] == 0, decode(got_ref), 0.0), out_ref)


def finish_kernel(sent, meta, mine_ref, one_ref, two_ref, energy_ref, sums_ref, *outs):
    one = decode(one_ref)
    if sent == "cross":
        one = jnp.where(meta[2] == 1, one, 0.0)
    value = mine_ref[...] + one + decode(two_ref)
    below = energy_ref[...] - sums_ref[:, :1]
    value = value / below
    outs[0][...] = value
    if sent == "cross":
        encode(value, outs[1])
    else:
        encode(value[G:], outs[1])


def thirds(value):
    high = value.astype(jnp.bfloat16)
    rest = value - high.astype(jnp.float32)
    middle = rest.astype(jnp.bfloat16)
    low = (rest - middle.astype(jnp.float32)).astype(jnp.bfloat16)
    return jnp.concatenate([high, middle, low], axis=0)


def assemble_kernel(meta, near_ref, second_ref, third_ref, got1, got2, got3, out_ref):
    g, zh = meta[1], meta[2]
    near = near_ref[:G]
    row, col = iotas(256, G)
    i, j = row >> 4, row & 15
    oi, oj, xi, xj = i >> 3, j >> 3, i & 7, j & 7
    gap = (xj - xi) & 7
    up = 64 + oi * 32 + (gap - 1) * 8 + xi
    down = 64 + oi * 32 + (7 - gap) * 8 + xj
    same = oi == oj
    plus = jnp.where(same, jnp.where((gap >= 1) & (gap <= 4), up, -1), jnp.where(oi < oj, xi * 8 + xj, -1))
    minus = jnp.where(same, jnp.where(gap >= 5, down, -1), jnp.where(oi > oj, xj * 8 + xi, -1))
    pick = (col == plus).astype(jnp.float32) - (col == minus).astype(jnp.float32)
    pick = pick.astype(jnp.bfloat16)
    pick = jnp.concatenate([pick, pick, pick], axis=1)
    out_ref[:, pl.ds(pl.multiple_of(g * 16, 16), 16), :] = dot(pick, thirds(near)).reshape(16, 16, -1)
    for d, mine, got in ((1, near_ref[G:], got1), (2, second_ref[...], got2), (3, third_ref[...], got3)):
        p = g ^ d
        w = meta[5 + d]
        got = decode(got)
        straight, turned = mine, got
        if d >= 2:
            straight, turned = jnp.where(zh == 1, got, mine), jnp.where(zh == 1, mine, got)
        flip = flip_matrix(1 - w)
        turned = -dot(jnp.concatenate([flip, flip, flip], axis=1), thirds(turned))
        for a in range(2):
            for x in range(OCT):
                at = a * 64 + x * OCT
                o = a ^ w
                out_ref[a * OCT + x, pl.ds(pl.multiple_of(p * 16 + o * OCT, OCT), OCT), :] = straight[at : at + OCT]
                out_ref[a * OCT + x, pl.ds(pl.multiple_of(p * 16 + (1 - o) * OCT, OCT), OCT), :] = turned[at : at + OCT]


def call(kernel, name, outs, args, scratch=(), anywhere=(), flops=0, moved=0):
    specs = []
    for at, arg in enumerate(args):
        if at in anywhere:
            specs.append(pl.BlockSpec(memory_space=pl.ANY))
        elif arg.dtype == jnp.int32:
            specs.append(pl.BlockSpec(memory_space=pltpu.SMEM))
        else:
            specs.append(pl.BlockSpec(memory_space=pltpu.VMEM))
    return pl.pallas_call(
        kernel,
        out_shape=outs,
        in_specs=specs,
        out_specs=[pl.BlockSpec(memory_space=pltpu.VMEM)] * len(outs),
        scratch_shapes=scratch,
        compiler_params=pltpu.CompilerParams(vmem_limit_bytes=VMEM),
        cost_estimate=pl.CostEstimate(flops=flops, bytes_accessed=moved, transcendentals=0),
        name=name,
    )(*args)


def partials(name, groups, kinds, meta, labels, xs, ys, integrals):
    rows, width = G * len(groups), integrals.shape[0]
    outs = [
        jax.ShapeDtypeStruct((rows + PAD, width), jnp.int16) if kind else jax.ShapeDtypeStruct((rows, width), jnp.float32)
        for kind in kinds
    ]
    return call(
        functools.partial(partial_kernel, groups, kinds),
        name,
        outs,
        (meta, labels, *xs, *ys, integrals),
        scratch=[
            pltpu.VMEM((rows, 2 * width), jnp.bfloat16),
            pltpu.VMEM(integrals.shape, jnp.bfloat16),
            pltpu.VMEM((3, rows, width), jnp.float32),
            pltpu.SMEM((448,), jnp.int32),
            pltpu.SemaphoreType.DMA((3,)),
        ],
        anywhere=(2 + 2 * len(groups),),
        flops=2 * rows * width * width,
        moved=16 * 1024 * 1024,
    )


def per_device(amplitudes, integrals, pair_irrep, pair_energy, occ_energy):
    i_local, nocc, width = amplitudes.shape
    k = lax.axis_index("blk")
    g = lax.axis_index("occ")
    zh = k & 1
    w = [g & 1, g >> 1, g >> 1]
    s = [w[0], w[1] ^ zh, w[2] ^ zh]
    meta = jnp.stack([k, g, zh, *s, *w]).astype(jnp.int32)
    labels = pair_irrep.reshape(-1, RUN)[:, 0]

    own = occ_energy.reshape(4, 16)
    mine = lax.dynamic_index_in_dim(own, g, 0, keepdims=False)
    sums = []
    ii = jnp.array([i for i in range(8) for j in range(8)] + [a * 8 + x for a in range(2) for d in range(1, 5) for x in range(8)])
    jj = jnp.array([8 + j for i in range(8) for j in range(8)] + [a * 8 + (x + d) % 8 for a in range(2) for d in range(1, 5) for x in range(8)])
    sums.append(mine[ii] + mine[jj])
    for d in (1, 2, 3):
        theirs = lax.dynamic_index_in_dim(own, g ^ d, 0, keepdims=False)
        turn = zh if d >= 2 else 0
        x = jnp.where(turn == 1, theirs, mine).reshape(2, 8)
        y = jnp.where(turn == 1, mine, theirs).reshape(2, 8)
        y = jnp.where(s[d - 1] == 1, y[::-1], y)
        sums.append((x[:, :, None] + y[:, None, :]).reshape(G))
    sums = [jnp.broadcast_to(one[:, None], (G, RUN)) for one in sums]
    energy = pair_energy.reshape(1, width)

    slab = jax.ShapeDtypeStruct((G, width), jnp.bfloat16)
    stay1, go1, stay2, go2, stay3, go3, own_x, own_y = call(
        split_kernel, "split", [slab] * 8, (meta, amplitudes), moved=6 * 1024 * 1024
    )
    got2 = send(go2, lambda b, o: (b, o ^ 2))
    got3 = send(go3, lambda b, o: (b, o ^ 3))
    got1 = send(go1, lambda b, o: (b, o ^ 1))

    near0, near1, near2 = partials("near", (0, 1), (0, 1, 1), meta, labels, (own_x, stay1), (own_y, got1), integrals)
    near1 = send(near1, lambda b, o: (b + 1, o))
    near2 = send(near2, lambda b, o: (b + 2, o))

    coded = [jax.ShapeDtypeStruct((G + PAD, width), jnp.int16)]
    crossed = []
    for d, stay, got in ((2, stay2, got2), (3, stay3, got3)):
        far0, far1, far2 = partials("far%d" % d, (d,), (0, 1, 0), meta, labels, (stay,), (got,), integrals)
        far1 = send(far1, lambda b, o, d=d: (b ^ 1, o ^ d))
        (far2,) = call(merge_kernel, "merge%d" % d, coded, (meta, far2, far1), moved=2 * 1024 * 1024)
        far2 = send(far2, lambda b, o: (b + 2, o))
        crossed.append((far0, far1, far2))

    done, back = [], []
    for d, (far0, far1, far2) in ((2, crossed[0]), (3, crossed[1])):
        value, code = call(
            functools.partial(finish_kernel, "cross"),
            "finish%d" % d,
            [jax.ShapeDtypeStruct((G, width), jnp.float32)] + coded,
            (meta, far0, far1, far2, energy, sums[d]),
            moved=4 * 1024 * 1024,
        )
        done.append(value)
        back.append(send(code, lambda b, o, d=d: (b, o ^ d)))
    near, code = call(
        functools.partial(finish_kernel, "near"),
        "finish1",
        [jax.ShapeDtypeStruct((2 * G, width), jnp.float32)] + coded,
        (meta, near0, near1, near2, energy, jnp.concatenate(sums[:2])),
        moved=6 * 1024 * 1024,
    )
    back1 = send(code, lambda b, o: (b, o ^ 1))
    (out,) = call(
        assemble_kernel,
        "assemble",
        [jax.ShapeDtypeStruct((i_local, nocc, width), jnp.float32)],
        (meta, near, done[0], done[1], back1, back[0], back[1]),
        moved=12 * 1024 * 1024,
    )
    return out


def solution(mesh):
    placed = (P("occ", None, "blk"), P("blk", None), P(), P("blk"), P())
    return jax.shard_map(
        per_device, mesh=mesh, in_specs=placed, out_specs=P("occ", None, "blk"), check_vma=False
    )
```

time: 560 us -> 148 us (0.26)
  the two profiles are of different devices: /device:TPU:1 before, /device:TPU:64 now
where the time goes in v1:
time: 148 us
  Pallas kernels  55.7 us (38%)
  waiting for transfers between devices  55.2 us (37%)
  starting transfers between devices  14.8 us (10%)
  local copies, waits for them, and re-layouts  11.8 us (8%)
  other arithmetic  10.1 us (7%)
    pallas_call x10, Pallas kernels, call(): pl.pallas_call(kernel, out_shape=outs, in_specs=specs, out_specs=[pl.Bloc...  55.7 us
    ppermute x12, waiting for transfers between devices, send(): return lax.ppermute(value, BOTH, routes(where))  55.2 us
    ppermute x12, starting transfers between devices, send(): return lax.ppermute(value, BOTH, routes(where))  14.8 us
    add x1, other arithmetic, per_device(): sums.append(mine[ii] + mine[jj])  9.92 us
    unnamed x90, local copies, waits for them, and re-layouts  4.88 us
  transfers between devices with their start and end apart: 12, of which 5 were waited for; matrix products, arithmetic and copies ran while one was open for 11% of the time, Pallas kernels for 30%

profile of v1, /device:TPU:64, one launch (start us, length us, event | category | flops | bytes accessed | tf_op | source)
XLA Modules:
  0.0 148.2 jit_solution(15771320203985107110)
XLA Ops:
  0.0 0.6 stack.30.meta
  0.6 4.0 %split.1 = (bf16[128,1536]{1,0:T(8,128)(2,1)}, bf16[128,1536]{1,0:T(8,128)(2,1)}, bf16[128,1536]{1,0:T(8,128)(2,1)}, bf16[128,1536]{1,0:T(8,128)(2,1)}, bf16[128...) custom-call(s32[9]{0:T(128)} %stack.30.meta, ...), custom_call_target="tpu_custom_call" | custom-call | bytes 6291456 | tf_op jit(solution)/shard_map/split/pallas_call | solution.py:258
  4.6 1.7 %collective-permute-start.3 = (bf16[128,1536]{1,0:T(8,128)(2,1)}, bf16[128,1536]{1,0:T(8,128)(2,1)S(1)}, u32[]{:S(2)}, u32[]{:S(2)}) collective-permute-start(bf16[128,1536]{1,0:T(8,128)(2,1)} %get-tuple-element.37), channel_id=1, source_target_pairs={{0,2},{1,3},{2,0},{3,1},{4,6},{5,7},{6,4},{7,5},{8,10},{9,11},{10,... | collective-permute-start | bytes 1179656 | tf_op jit(solution)/shard_map/ppermute | solution.py:30
  6.3 0.2 collective-permute-start.6
  6.5 0.1 reshape.91
  6.6 0.5 broadcast.136
  7.1 0.7 fusion.3
  7.8 0.1 add.92
  7.8 0.1 reshape.92
  8.0 0.1 squeeze.16
  8.0 0.1 squeeze.17
  8.1 0.1 broadcast_add_fusion.2
  8.2 0.7 slice_reduce_fusion.lab
  9.0 0.6 reshape.90.energy_ref
  9.6 0.1 reshape.230
  9.7 14.6 %collective-permute-done.6.refs_1_ = bf16[128,1536]{1,0:T(8,128)(2,1)S(1)} collective-permute-done((bf16[128,1536]{1,0:T(8,128)(2,1)}, bf16[128,1536]{1,0:T(8,128)(2,1)S(1)}, u32[]{:S(2)}, u32[]{:S(2)}) %collective-permute-start.6) | collective-permute-done | bytes 393248 | tf_op jit(solution)/shard_map/ppermute | solution.py:30
  24.3 0.7 copy-done.11
  25.1 9.4 %far3.1 = (f32[128,1536]{1,0:T(8,128)}, s16[144,1536]{1,0:T(8,128)(2,1)}, f32[128,1536]{1,0:T(8,128)}) custom-call(s32[9]{0:T(128)} %stack.30.meta, s32[384]{0:T(512)} %slice_reduce_fusion.lab, bf16[128,1536]{1,0:T(8,128)(2,1)} %get-tuple-element.42.refs_0_, bf16[128,1536]{1,0:T(8,128)(2,1)} %copy-done.11, bf16[1536,4608]{1,0:T(8,128)(2,1)} %refs_2_.3), custom_call_target="tpu_custom_call" | custom-call | flops 603979776 | bytes 16777216 | tf_op jit(solution)/shard_map/far3/pallas_call | solution.py:258
  34.4 0.6 collective-permute-start.7
  35.0 0.8 copy-done.10
  35.8 9.4 %far2.1 = (f32[128,1536]{1,0:T(8,128)}, s16[144,1536]{1,0:T(8,128)(2,1)}, f32[128,1536]{1,0:T(8,128)}) custom-call(s32[9]{0:T(128)} %stack.30.meta, s32[384]{0:T(512)} %slice_reduce_fusion.lab, bf16[128,1536]{1,0:T(8,128)(2,1)} %get-tuple-element.36.refs_0_, bf16[128,1536]{1,0:T(8,128)(2,1)} %copy-done.10, bf16[1536,4608]{1,0:T(8,128)(2,1)} %refs_2_.3), custom_call_target="tpu_custom_call" | custom-call | flops 603979776 | bytes 16777216 | tf_op jit(solution)/shard_map/far2/pallas_call | solution.py:258
  45.1 2.0 %collective-permute-start.4 = (s16[144,1536]{1,0:T(8,128)(2,1)}, s16[144,1536]{1,0:T(8,128)(2,1)S(1)}, u32[]{:S(2)}, u32[]{:S(2)}) collective-permute-start(s16[144,1536]{1,0:T(8,128)(2,1)} %get-tuple-element.39), channel_id=1, source_target_pairs={{0,6},{1,7},{2,4},{3,5},{4,2},{5,3},{6,0},{7,1},{8,14},{9,15},{10,... | collective-permute-start | bytes 1327112 | tf_op jit(solution)/shard_map/ppermute | solution.py:30
  47.1 0.8 copy-done.9
  47.9 11.7 %near.1 = (f32[256,1536]{1,0:T(8,128)}, s16[272,1536]{1,0:T(8,128)(2,1)}, s16[272,1536]{1,0:T(8,128)(2,1)}) custom-call(s32[9]{0:T(128)} %stack.30.meta, s32[384]{0:T(512)} %slice_reduce_fusion.lab, bf16[128,1536]{1,0:T(8,128)(2,1)} %get-tuple-element.28.refs_0_, bf16[128,1536]{1,0:T(8,128)(2,1)} %get-tuple-element.29.refs_1_, ...), custom_call_target="tpu_custom_call" | custom-call | flops 1207959552 | bytes 16777216 | tf_op jit(solution)/shard_map/near/pallas_call | solution.py:258
  59.6 0.0 copy-start.15
  59.6 0.0 copy-start.16
  59.6 0.0 copy-start.18
  59.6 0.0 copy-start.19
  59.6 0.0 copy-start.20
  59.7 0.0 copy-start.21
  59.7 0.0 copy-start.23
  59.7 0.0 copy-start.24
  59.7 0.0 copy-start.25
  59.7 0.0 copy-start.26
  59.7 0.0 copy-start.27
  59.7 0.0 copy-start.28
  60.0 3.0 %collective-permute-start.1 = (s16[272,1536]{1,0:T(8,128)(2,1)}, s16[272,1536]{1,0:T(8,128)(2,1)S(1)}, u32[]{:S(2)}, u32[]{:S(2)}) collective-permute-start(s16[272,1536]{1,0:T(8,128)(2,1)} %get-tuple-element.33), channel_id=1, source_target_pairs={{0,4},{1,5},{2,6},{3,7},{4,8},{5,9},{6,10},{7,11},{8,12},{9,13},{1... | collective-permute-start | bytes 2506760 | tf_op jit(solution)/shard_map/ppermute | solution.py:30
  62.9 0.7 collective-permute-start.2
  63.7 0.1 broadcast_add_fusion
  63.8 0.1 add.107
  63.9 0.1 add.102
  64.0 0.8 copy-done.1
  64.7 2.3 %merge3.1 = s16[144,1536]{1,0:T(8,128)(2,1)} custom-call(s32[9]{0:T(128)} %stack.30.meta, f32[128,1536]{1,0:T(8,128)} %get-tuple-element.46.mine_ref, s16[144,1536]{1,0:T(8,128)(2,1)} %copy-done.1), custom_call_target="tpu_custom_call" | custom-call | bytes 2097152 | tf_op jit(solution)/shard_map/merge3/pallas_call | solution.py:258
  67.1 1.5 collective-permute-start.8
  68.5 0.8 copy-done
  69.3 2.3 %merge2.1 = s16[144,1536]{1,0:T(8,128)(2,1)} custom-call(s32[9]{0:T(128)} %stack.30.meta, f32[128,1536]{1,0:T(8,128)} %get-tuple-element.40.mine_ref, s16[144,1536]{1,0:T(8,128)(2,1)} %copy-done), custom_call_target="tpu_custom_call" | custom-call | bytes 2097152 | tf_op jit(solution)/shard_map/merge2/pallas_call | solution.py:258
  71.6 1.2 collective-permute-start.5
  72.8 0.7 fusion.4
  73.8 9.9 %select_add_fusion = f32[128]{0:T(128)S(1)} fusion(pred[128]{0:T(512)(128)(4,1)S(1)} %copy-done.29, pred[128]{0:T(512)(128)(4,1)S(1)} %copy-done.28, pred[128]{0:T(512)(128)(4,1)S(1)} %copy-done.27, pred[128]{0:T(512)(128)(4,1)S(1)} %copy-done.26, pred[128]{0:T(512)(128)(4,1)S(1)} %copy-done.25, pred[128]{0:T(512)(128)(4,1)S(1)} %copy-done.24, ...), kind=kLoop, calls=%fused_computation.19 | loop fusion | flops 3968 | bytes 4416 | tf_op jit(solution)/shard_map/add | solution.py:309
  83.8 21.3 %collective-permute-done.2.two_ref = s16[272,1536]{1,0:T(8,128)(2,1)S(1)} collective-permute-done((s16[272,1536]{1,0:T(8,128)(2,1)}, s16[272,1536]{1,0:T(8,128)(2,1)S(1)}, u32[]{:S(2)}, u32[]{:S(2)}) %collective-permute-start.2) | collective-permute-done | bytes 835616 | tf_op jit(solution)/shard_map/ppermute | solution.py:30
  105.1 0.9 broadcast.115.sums_ref
  106.0 0.1 copy-done.3
  106.1 3.9 %finish1.1 = (f32[256,1536]{1,0:T(8,128)}, s16[144,1536]{1,0:T(8,128)(2,1)}) custom-call(s32[9]{0:T(128)} %stack.30.meta, f32[256,1536]{1,0:T(8,128)} %get-tuple-element.32.mine_ref, s16[272,1536]{1,0:T(8,128)(2,1)} %copy-done.2, s16[272,1536]{1,0:T(8,128)(2,1)} %copy-done.3, f32[1,1536]{1,0:T(1,128)} %reshape.90.energy_ref, f32[256,128]{1,0:T(8,128)} %broadcast.115.sums_ref), custom_call_target="tpu_custom_call" | custom-call | bytes 6291456 | tf_op jit(solution)/shard_map/finish1/pallas_call | solution.py:258
  110.0 4.6 %collective-permute-done.8.two_ref = s16[144,1536]{1,0:T(8,128)(2,1)S(1)} collective-permute-done((s16[144,1536]{1,0:T(8,128)(2,1)}, s16[144,1536]{1,0:T(8,128)(2,1)S(1)}, u32[]{:S(2)}, u32[]{:S(2)}) %collective-permute-start.8) | collective-permute-done | bytes 442400 | tf_op jit(solution)/shard_map/ppermute | solution.py:30
  114.6 0.8 broadcast_in_dim.17.sums_ref
  115.4 2.8 %finish3.1 = (f32[128,1536]{1,0:T(8,128)}, s16[144,1536]{1,0:T(8,128)(2,1)}) custom-call(s32[9]{0:T(128)} %stack.30.meta, f32[128,1536]{1,0:T(8,128)} %get-tuple-element.44.mine_ref, s16[144,1536]{1,0:T(8,128)(2,1)} %copy-done.1, s16[144,1536]{1,0:T(8,128)(2,1)} %copy-done.5, f32[1,1536]{1,0:T(1,128)} %reshape.90.energy_ref, ...), custom_call_target="tpu_custom_call" | custom-call | bytes 4194304 | tf_op jit(solution)/shard_map/finish3/pallas_call | solution.py:258
  118.2 1.1 collective-permute-start.11
  119.3 4.0 %collective-permute-done.5.two_ref = s16[144,1536]{1,0:T(8,128)(2,1)S(1)} collective-permute-done((s16[144,1536]{1,0:T(8,128)(2,1)}, s16[144,1536]{1,0:T(8,128)(2,1)S(1)}, u32[]{:S(2)}, u32[]{:S(2)}) %collective-permute-start.5) | collective-permute-done | bytes 442400 | tf_op jit(solution)/shard_map/ppermute | solution.py:30
  123.4 0.8 broadcast_in_dim.16.sums_ref
  124.1 2.9 %finish2.1 = (f32[128,1536]{1,0:T(8,128)}, s16[144,1536]{1,0:T(8,128)(2,1)}) custom-call(s32[9]{0:T(128)} %stack.30.meta, f32[128,1536]{1,0:T(8,128)} %get-tuple-element.38.mine_ref, s16[144,1536]{1,0:T(8,128)(2,1)} %copy-done, s16[144,1536]{1,0:T(8,128)(2,1)} %copy-done.4, f32[1,1536]{1,0:T(1,128)} %reshape.90.energy_ref, f32[128,128]{1,0:T(8,128)} %broadcast_in_dim.16.sums_ref), custom_call_target="tpu_custom_call" | custom-call | bytes 4194304 | tf_op jit(solution)/shard_map/finish2/pallas_call | solution.py:258
  127.0 2.8 %collective-permute-start.10 = (s16[144,1536]{1,0:T(8,128)(2,1)}, s16[144,1536]{1,0:T(8,128)(2,1)S(1)}, u32[]{:S(2)}, u32[]{:S(2)}) collective-permute-start(s16[144,1536]{1,0:T(8,128)(2,1)} %get-tuple-element.49), channel_id=1, source_target_pairs={{0,2},{1,3},{2,0},{3,1},{4,6},{5,7},{6,4},{7,5},{8,10},{9,11},{10,... | collective-permute-start | bytes 1327112 | tf_op jit(solution)/shard_map/ppermute | solution.py:30
  129.9 10.5 %collective-permute-done.10.got2 = s16[144,1536]{1,0:T(8,128)(2,1)S(1)} collective-permute-done((s16[144,1536]{1,0:T(8,128)(2,1)}, s16[144,1536]{1,0:T(8,128)(2,1)S(1)}, u32[]{:S(2)}, u32[]{:S(2)}) %collective-permute-start.10) | collective-permute-done | bytes 442400 | tf_op jit(solution)/shard_map/ppermute | solution.py:30
  140.4 0.8 copy-done.8
  141.1 7.0 %assemble.1 = f32[16,64,1536]{2,1,0:T(8,128)} custom-call(s32[9]{0:T(128)} %stack.30.meta, f32[256,1536]{1,0:T(8,128)} %get-tuple-element.35.near_ref, f32[128,1536]{1,0:T(8,128)} %get-tuple-element.41.second_ref, f32[128,1536]{1,0:T(8,128)} %get-tuple-element.47.third_ref, s16[144,1536]{1,0:T(8,128)(2,1)} %copy-done.6, s16[144,1536]{1,0:T(8,128)(2,1)} %copy-done.8, ...), custom_call_target="tpu_custom_call" | custom-call | bytes 12582912 | tf_op jit(solution)/shard_map/assemble/pallas_call | solution.py:258
  (88 shorter events, 0.3 us)
Async XLA Ops:
  0.0 6.5 %copy-start.14 = (f32[64]{0:T(128)S(1)}, f32[64]{0:T(128)}, u32[]{:S(2)}) copy-start(f32[64]{0:T(128)} %param.11) | copy-start | bytes 772
  0.0 8.2 %copy-start.12 = (s32[49152]{0:T(1024)S(1)}, s32[49152]{0:T(1024)}, u32[]{:S(2)}) copy-start(s32[49152]{0:T(1024)} %param.9) | copy-start | bytes 589828
  0.0 9.0 %copy-start.13 = (f32[1536]{0:T(1024)S(1)}, f32[1536]{0:T(1024)}, u32[]{:S(2)}) copy-start(f32[1536]{0:T(1024)} %param.10) | copy-start | bytes 18436
  4.6 42.5 %collective-permute-start = (bf16[128,1536]{1,0:T(8,128)(2,1)}, bf16[128,1536]{1,0:T(8,128)(2,1)S(1)}, u32[]{:S(2)}, u32[]{:S(2)}) collective-permute-start(bf16[128,1536]{1,0:T(8,128)(2,1)} %get-tuple-element.31), channel_id=1, source_target_pairs={{0,1},{1,0},{2,3},{3,2},{4,5},{5,4},{6,7},{7,6},{8,9},{9,8},{10,11... | collective-permute-start | bytes 1179656 | tf_op jit(solution)/shard_map/ppermute | solution.py:30
  4.6 30.4 %collective-permute-start.3 = (bf16[128,1536]{1,0:T(8,128)(2,1)}, bf16[128,1536]{1,0:T(8,128)(2,1)S(1)}, u32[]{:S(2)}, u32[]{:S(2)}) collective-permute-start(bf16[128,1536]{1,0:T(8,128)(2,1)} %get-tuple-element.37), channel_id=1, source_target_pairs={{0,2},{1,3},{2,0},{3,1},{4,6},{5,7},{6,4},{7,5},{8,10},{9,11},{10,... | collective-permute-start | bytes 1179656 | tf_op jit(solution)/shard_map/ppermute | solution.py:30
  6.3 18.0 %collective-permute-start.6 = (bf16[128,1536]{1,0:T(8,128)(2,1)}, bf16[128,1536]{1,0:T(8,128)(2,1)S(1)}, u32[]{:S(2)}, u32[]{:S(2)}) collective-permute-start(bf16[128,1536]{1,0:T(8,128)(2,1)} %get-tuple-element.43), channel_id=1, source_target_pairs={{0,3},{1,2},{2,1},{3,0},{4,7},{5,6},{6,5},{7,4},{8,11},{9,10},{10,... | collective-permute-start | bytes 1179656 | tf_op jit(solution)/shard_map/ppermute | solution.py:30
  24.3 0.7 copy-start.11
  34.4 29.5 %collective-permute-start.7 = (s16[144,1536]{1,0:T(8,128)(2,1)}, s16[144,1536]{1,0:T(8,128)(2,1)S(1)}, u32[]{:S(2)}, u32[]{:S(2)}) collective-permute-start(s16[144,1536]{1,0:T(8,128)(2,1)} %get-tuple-element.45), channel_id=1, source_target_pairs={{0,7},{1,6},{2,5},{3,4},{4,3},{5,2},{6,1},{7,0},{8,15},{9,14},{10,... | collective-permute-start | bytes 1327112 | tf_op jit(solution)/shard_map/ppermute | solution.py:30
  35.0 0.8 copy-start.10
  45.1 23.4 %collective-permute-start.4 = (s16[144,1536]{1,0:T(8,128)(2,1)}, s16[144,1536]{1,0:T(8,128)(2,1)S(1)}, u32[]{:S(2)}, u32[]{:S(2)}) collective-permute-start(s16[144,1536]{1,0:T(8,128)(2,1)} %get-tuple-element.39), channel_id=1, source_target_pairs={{0,6},{1,7},{2,4},{3,5},{4,2},{5,3},{6,0},{7,1},{8,14},{9,15},{10,... | collective-permute-start | bytes 1327112 | tf_op jit(solution)/shard_map/ppermute | solution.py:30
  47.1 0.8 copy-start.9
  59.6 14.0 %copy-start.15 = (pred[128]{0:T(512)(128)(4,1)S(1)}, pred[128]{0:T(512)(128)(4,1)}, u32[]{:S(2)}) copy-start(pred[128]{0:T(512)(128)(4,1)} %constant.109) | copy-start | bytes 388
  59.6 14.0 %copy-start.16 = (pred[128]{0:T(512)(128)(4,1)S(1)}, pred[128]{0:T(512)(128)(4,1)}, u32[]{:S(2)}) copy-start(pred[128]{0:T(512)(128)(4,1)} %constant.108) | copy-start | bytes 388
  59.6 13.9 %copy-start.17 = (pred[128]{0:T(512)(128)(4,1)S(1)}, pred[128]{0:T(512)(128)(4,1)}, u32[]{:S(2)}) copy-start(pred[128]{0:T(512)(128)(4,1)} %constant.107) | copy-start | bytes 388
  59.6 13.9 %copy-start.18 = (pred[128]{0:T(512)(128)(4,1)S(1)}, pred[128]{0:T(512)(128)(4,1)}, u32[]{:S(2)}) copy-start(pred[128]{0:T(512)(128)(4,1)} %constant.106) | copy-start | bytes 388
  59.6 13.9 %copy-start.19 = (pred[128]{0:T(512)(128)(4,1)S(1)}, pred[128]{0:T(512)(128)(4,1)}, u32[]{:S(2)}) copy-start(pred[128]{0:T(512)(128)(4,1)} %constant.105) | copy-start | bytes 388
  59.6 13.9 %copy-start.20 = (pred[128]{0:T(512)(128)(4,1)S(1)}, pred[128]{0:T(512)(128)(4,1)}, u32[]{:S(2)}) copy-start(pred[128]{0:T(512)(128)(4,1)} %constant.104) | copy-start | bytes 388
  59.7 13.9 %copy-start.21 = (pred[128]{0:T(512)(128)(4,1)S(1)}, pred[128]{0:T(512)(128)(4,1)}, u32[]{:S(2)}) copy-start(pred[128]{0:T(512)(128)(4,1)} %constant.103) | copy-start | bytes 388
  59.7 13.9 %copy-start.22 = (pred[128]{0:T(512)(128)(4,1)S(1)}, pred[128]{0:T(512)(128)(4,1)}, u32[]{:S(2)}) copy-start(pred[128]{0:T(512)(128)(4,1)} %constant.102) | copy-start | bytes 388
  59.7 13.9 %copy-start.23 = (pred[128]{0:T(512)(128)(4,1)S(1)}, pred[128]{0:T(512)(128)(4,1)}, u32[]{:S(2)}) copy-start(pred[128]{0:T(512)(128)(4,1)} %constant.101) | copy-start | bytes 388
  59.7 13.9 %copy-start.24 = (pred[128]{0:T(512)(128)(4,1)S(1)}, pred[128]{0:T(512)(128)(4,1)}, u32[]{:S(2)}) copy-start(pred[128]{0:T(512)(128)(4,1)} %constant.100) | copy-start | bytes 388
  59.7 13.9 %copy-start.25 = (pred[128]{0:T(512)(128)(4,1)S(1)}, pred[128]{0:T(512)(128)(4,1)}, u32[]{:S(2)}) copy-start(pred[128]{0:T(512)(128)(4,1)} %constant.99) | copy-start | bytes 388
  59.7 13.9 %copy-start.26 = (pred[128]{0:T(512)(128)(4,1)S(1)}, pred[128]{0:T(512)(128)(4,1)}, u32[]{:S(2)}) copy-start(pred[128]{0:T(512)(128)(4,1)} %constant.98) | copy-start | bytes 388
  59.7 13.9 %copy-start.27 = (pred[128]{0:T(512)(128)(4,1)S(1)}, pred[128]{0:T(512)(128)(4,1)}, u32[]{:S(2)}) copy-start(pred[128]{0:T(512)(128)(4,1)} %constant.97) | copy-start | bytes 388
  59.7 13.9 %copy-start.28 = (pred[128]{0:T(512)(128)(4,1)S(1)}, pred[128]{0:T(512)(128)(4,1)}, u32[]{:S(2)}) copy-start(pred[128]{0:T(512)(128)(4,1)} %constant.96) | copy-start | bytes 388
  59.8 13.9 %copy-start.29 = (pred[128]{0:T(512)(128)(4,1)S(1)}, pred[128]{0:T(512)(128)(4,1)}, u32[]{:S(2)}) copy-start(pred[128]{0:T(512)(128)(4,1)} %constant.95) | copy-start | bytes 388
  59.8 13.9 %copy-start.30 = (pred[128]{0:T(512)(128)(4,1)S(1)}, pred[128]{0:T(512)(128)(4,1)}, u32[]{:S(2)}) copy-start(pred[128]{0:T(512)(128)(4,1)} %constant.92) | copy-start | bytes 388
  59.8 13.9 %copy-start.31 = (pred[128]{0:T(512)(128)(4,1)S(1)}, pred[128]{0:T(512)(128)(4,1)}, u32[]{:S(2)}) copy-start(pred[128]{0:T(512)(128)(4,1)} %constant.91) | copy-start | bytes 388
  59.8 13.9 %copy-start.32 = (pred[128]{0:T(512)(128)(4,1)S(1)}, pred[128]{0:T(512)(128)(4,1)}, u32[]{:S(2)}) copy-start(pred[128]{0:T(512)(128)(4,1)} %constant.90) | copy-start | bytes 388
  59.8 13.9 %copy-start.33 = (pred[128]{0:T(512)(128)(4,1)S(1)}, pred[128]{0:T(512)(128)(4,1)}, u32[]{:S(2)}) copy-start(pred[128]{0:T(512)(128)(4,1)} %constant.89) | copy-start | bytes 388
  59.8 13.9 %copy-start.34 = (pred[128]{0:T(512)(128)(4,1)S(1)}, pred[128]{0:T(512)(128)(4,1)}, u32[]{:S(2)}) copy-start(pred[128]{0:T(512)(128)(4,1)} %constant.88) | copy-start | bytes 388
  59.8 13.9 %copy-start.35 = (pred[128]{0:T(512)(128)(4,1)S(1)}, pred[128]{0:T(512)(128)(4,1)}, u32[]{:S(2)}) copy-start(pred[128]{0:T(512)(128)(4,1)} %constant.87) | copy-start | bytes 388
  59.8 13.9 %copy-start.36 = (pred[128]{0:T(512)(128)(4,1)S(1)}, pred[128]{0:T(512)(128)(4,1)}, u32[]{:S(2)}) copy-start(pred[128]{0:T(512)(128)(4,1)} %constant.86) | copy-start | bytes 388
  59.9 13.9 %copy-start.37 = (pred[128]{0:T(512)(128)(4,1)S(1)}, pred[128]{0:T(512)(128)(4,1)}, u32[]{:S(2)}) copy-start(pred[128]{0:T(512)(128)(4,1)} %constant.85) | copy-start | bytes 388
  59.9 13.9 %copy-start.38 = (pred[128]{0:T(512)(128)(4,1)S(1)}, pred[128]{0:T(512)(128)(4,1)}, u32[]{:S(2)}) copy-start(pred[128]{0:T(512)(128)(4,1)} %constant.84) | copy-start | bytes 388
  59.9 13.9 %copy-start.39 = (pred[128]{0:T(512)(128)(4,1)S(1)}, pred[128]{0:T(512)(128)(4,1)}, u32[]{:S(2)}) copy-start(pred[128]{0:T(512)(128)(4,1)} %constant.83) | copy-start | bytes 388
  59.9 13.9 %copy-start.40 = (pred[128]{0:T(512)(128)(4,1)S(1)}, pred[128]{0:T(512)(128)(4,1)}, u32[]{:S(2)}) copy-start(pred[128]{0:T(512)(128)(4,1)} %constant.82) | copy-start | bytes 388
  59.9 13.9 %copy-start.41 = (pred[128]{0:T(512)(128)(4,1)S(1)}, pred[128]{0:T(512)(128)(4,1)}, u32[]{:S(2)}) copy-start(pred[128]{0:T(512)(128)(4,1)} %constant.81) | copy-start | bytes 388
  59.9 13.9 %copy-start.42 = (pred[128]{0:T(512)(128)(4,1)S(1)}, pred[128]{0:T(512)(128)(4,1)}, u32[]{:S(2)}) copy-start(pred[128]{0:T(512)(128)(4,1)} %constant.80) | copy-start | bytes 388
  59.9 13.9 %copy-start.43 = (pred[128]{0:T(512)(128)(4,1)S(1)}, pred[128]{0:T(512)(128)(4,1)}, u32[]{:S(2)}) copy-start(pred[128]{0:T(512)(128)(4,1)} %constant.79) | copy-start | bytes 388
  59.9 13.9 %copy-start.44 = (pred[128]{0:T(512)(128)(4,1)S(1)}, pred[128]{0:T(512)(128)(4,1)}, u32[]{:S(2)}) copy-start(pred[128]{0:T(512)(128)(4,1)} %constant.78) | copy-start | bytes 388
  60.0 23.8 %collective-permute-start.1 = (s16[272,1536]{1,0:T(8,128)(2,1)}, s16[272,1536]{1,0:T(8,128)(2,1)S(1)}, u32[]{:S(2)}, u32[]{:S(2)}) collective-permute-start(s16[272,1536]{1,0:T(8,128)(2,1)} %get-tuple-element.33), channel_id=1, source_target_pairs={{0,4},{1,5},{2,6},{3,7},{4,8},{5,9},{6,10},{7,11},{8,12},{9,13},{1... | collective-permute-start | bytes 2506760 | tf_op jit(solution)/shard_map/ppermute | solution.py:30
  62.9 42.2 %collective-permute-start.2 = (s16[272,1536]{1,0:T(8,128)(2,1)}, s16[272,1536]{1,0:T(8,128)(2,1)S(1)}, u32[]{:S(2)}, u32[]{:S(2)}) collective-permute-start(s16[272,1536]{1,0:T(8,128)(2,1)} %get-tuple-element.34), channel_id=1, source_target_pairs={{0,8},{1,9},{2,10},{3,11},{4,12},{5,13},{6,14},{7,15},{8,16},{9,17... | collective-permute-start | bytes 2506760 | tf_op jit(solution)/shard_map/ppermute | solution.py:30
  64.0 0.8 copy-start.1
  67.1 47.6 %collective-permute-start.8 = (s16[144,1536]{1,0:T(8,128)(2,1)}, s16[144,1536]{1,0:T(8,128)(2,1)S(1)}, u32[]{:S(2)}, u32[]{:S(2)}) collective-permute-start(s16[144,1536]{1,0:T(8,128)(2,1)} %merge3.1), channel_id=1, source_target_pairs={{0,8},{1,9},{2,10},{3,11},{4,12},{5,13},{6,14},{7,15},{8,16},{9,17... | collective-permute-start | bytes 1327112 | tf_op jit(solution)/shard_map/ppermute | solution.py:30
  68.5 0.8 copy-start
  71.6 51.7 %collective-permute-start.5 = (s16[144,1536]{1,0:T(8,128)(2,1)}, s16[144,1536]{1,0:T(8,128)(2,1)S(1)}, u32[]{:S(2)}, u32[]{:S(2)}) collective-permute-start(s16[144,1536]{1,0:T(8,128)(2,1)} %merge2.1), channel_id=1, source_target_pairs={{0,8},{1,9},{2,10},{3,11},{4,12},{5,13},{6,14},{7,15},{8,16},{9,17... | collective-permute-start | bytes 1327112 | tf_op jit(solution)/shard_map/ppermute | solution.py:30
  83.8 22.2 %copy-start.2 = (s16[272,1536]{1,0:T(8,128)(2,1)}, s16[272,1536]{1,0:T(8,128)(2,1)S(1)}, u32[]{:S(2)}) copy-start(s16[272,1536]{1,0:T(8,128)(2,1)S(1)} %collective-permute-done.1.one_ref) | copy-start | bytes 2506756
  105.1 0.9 copy-start.3
  110.0 19.9 %collective-permute-start.9 = (s16[144,1536]{1,0:T(8,128)(2,1)}, s16[144,1536]{1,0:T(8,128)(2,1)S(1)}, u32[]{:S(2)}, u32[]{:S(2)}) collective-permute-start(s16[144,1536]{1,0:T(8,128)(2,1)} %get-tuple-element.48), channel_id=1, source_target_pairs={{0,1},{1,0},{2,3},{3,2},{4,5},{5,4},{6,7},{7,6},{8,9},{9,8},{10,11... | collective-permute-start | bytes 1327112 | tf_op jit(solution)/shard_map/ppermute | solution.py:30
  114.6 0.8 copy-start.5
  118.2 11.6 %collective-permute-start.11 = (s16[144,1536]{1,0:T(8,128)(2,1)}, s16[144,1536]{1,0:T(8,128)(2,1)S(1)}, u32[]{:S(2)}, u32[]{:S(2)}) collective-permute-start(s16[144,1536]{1,0:T(8,128)(2,1)} %get-tuple-element.50), channel_id=1, source_target_pairs={{0,3},{1,2},{2,1},{3,0},{4,7},{5,6},{6,5},{7,4},{8,11},{9,10},{10,... | collective-permute-start | bytes 1327112 | tf_op jit(solution)/shard_map/ppermute | solution.py:30
  123.4 0.8 copy-start.4
  127.0 13.4 %collective-permute-start.10 = (s16[144,1536]{1,0:T(8,128)(2,1)}, s16[144,1536]{1,0:T(8,128)(2,1)S(1)}, u32[]{:S(2)}, u32[]{:S(2)}) collective-permute-start(s16[144,1536]{1,0:T(8,128)(2,1)} %get-tuple-element.49), channel_id=1, source_target_pairs={{0,2},{1,3},{2,0},{3,1},{4,6},{5,7},{6,4},{7,5},{8,10},{9,11},{10,... | collective-permute-start | bytes 1327112 | tf_op jit(solution)/shard_map/ppermute | solution.py:30
  129.8 10.5 %copy-start.6 = (s16[144,1536]{1,0:T(8,128)(2,1)}, s16[144,1536]{1,0:T(8,128)(2,1)S(1)}, u32[]{:S(2)}) copy-start(s16[144,1536]{1,0:T(8,128)(2,1)S(1)} %collective-permute-done.9.got1) | copy-start | bytes 1327108
  129.8 10.5 %copy-start.7 = (s16[144,1536]{1,0:T(8,128)(2,1)}, s16[144,1536]{1,0:T(8,128)(2,1)S(1)}, u32[]{:S(2)}) copy-start(s16[144,1536]{1,0:T(8,128)(2,1)S(1)} %collective-permute-done.11.got3) | copy-start | bytes 1327108
  140.4 0.8 copy-start.8

commit v2 on v0

v2 whole, which is shorter than its diff:
```python
import functools

import jax
import jax.numpy as jnp
from jax import lax
from jax.experimental import pallas as pl
from jax.experimental.pallas import tpu as pltpu
from jax.sharding import PartitionSpec as P

BOTH = ("blk", "occ")
BLOCKS = 32
RUN = 128
OCT = 8
G = 128
PAD = 16
LEVELS = 32000.0
STEPS = 256.0
MANY = 8
SLOTS = 160
MIB = 1024 * 1024
ANY = pl.BlockSpec(memory_space=pl.ANY)
IN_VMEM = pl.BlockSpec(memory_space=pltpu.VMEM)
IN_SMEM = pl.BlockSpec(memory_space=pltpu.SMEM)
TOKEN = jax.ShapeDtypeStruct((8,), jnp.int32)


def routes(where):
    pairs = []
    for blk in range(BLOCKS):
        for occ in range(4):
            to_blk, to_occ = where(blk, occ)
            pairs.append((blk * 4 + occ, (to_blk % BLOCKS) * 4 + to_occ))
    return pairs


def send(value, where):
    return lax.ppermute(value, BOTH, routes(where))


def place():
    k = lax.axis_index("blk")
    return k, lax.axis_index("occ"), lax.rem(k, 2)


def later(g, d):
    return lax.rem(g, 2) if d == 1 else lax.div(g, 2)


def side(g, zh, d):
    return later(g, d) if d == 1 else lax.rem(later(g, d) + zh, 2)


def apart(g, d):
    low, high = lax.rem(g, 2), lax.div(g, 2)
    low = 1 - low if d & 1 else low
    high = 1 - high if d & 2 else high
    return high * 2 + low


def encode(value, out_ref):
    rows = value.shape[0]
    most = jnp.max(jnp.abs(value), axis=0, keepdims=True)
    code = jnp.ceil(jnp.log2(jnp.maximum(most, 2.0**-120)) * STEPS)
    up = jnp.exp2(code * (-1.0 / STEPS)) * LEVELS
    coded = jnp.clip(jnp.round(value * up), -32767.0, 32767.0)
    out_ref[:rows, :] = coded.astype(jnp.int32).astype(jnp.int16)
    scale = jnp.broadcast_to(code.astype(jnp.int32), (PAD, value.shape[1]))
    out_ref[rows:, :] = scale.astype(jnp.int16)


def scales(ref):
    code = ref[ref.shape[0] - PAD :, :].astype(jnp.int32).astype(jnp.float32)[:1]
    return jnp.exp2(code * (1.0 / STEPS)) * (1.0 / LEVELS)


def codes(ref):
    return ref[: ref.shape[0] - PAD, :].astype(jnp.int32)


def decode(ref):
    return codes(ref).astype(jnp.float32) * scales(ref)


def iotas(rows, cols):
    return (
        lax.broadcasted_iota(jnp.int32, (rows, cols), 0),
        lax.broadcasted_iota(jnp.int32, (rows, cols), 1),
    )


def ones_at(where):
    return where.astype(jnp.float32).astype(jnp.bfloat16)


def flip_matrix(octet_flip):
    row, col = iotas(G, G)
    a, x, y = row >> 6, (row >> 3) & 7, row & 7
    return ones_at(col == (((a ^ octet_flip) << 6) | (y << 3) | x))


def own_pairs(cols):
    row, col = iotas(G, cols)
    q = row - 64
    octet, d, x = q >> 5, ((q >> 3) & 3) + 1, q & 7
    low = row < 64
    i = jnp.where(low, row >> 3, octet * 8 + x)
    j = jnp.where(low, 8 + (row & 7), octet * 8 + ((x + d) & 7))
    return i, j, col


def dot(a, b):
    return jnp.dot(a, b, preferred_element_type=jnp.float32)


def thirds(value):
    high = value.astype(jnp.bfloat16)
    rest = value - high.astype(jnp.float32)
    middle = rest.astype(jnp.bfloat16)
    low = (rest - middle.astype(jnp.float32)).astype(jnp.bfloat16)
    return jnp.concatenate([high, middle, low], axis=0)


def thrice(matrix):
    return jnp.concatenate([matrix, matrix, matrix], axis=1)


def slab(t_ref, group):
    return t_ref.at[:, pl.ds(pl.multiple_of(group * 16, 16), 16), :]


def half(both, s):
    parts = []
    for a in range(2):
        for x in range(OCT):
            one = both[a * OCT + x].astype(jnp.float32)
            parts.append(jnp.where((a ^ s) == 0, one[:OCT], one[OCT:]))
    return jnp.concatenate(parts, axis=0).astype(jnp.bfloat16)


def split_kernel(ds, t_ref, *refs):
    outs, (buf, sems) = refs[: len(ds)], refs[len(ds) :]
    _, g, zh = place()
    loads = [pltpu.make_async_copy(slab(t_ref, apart(g, d)), buf.at[at], sems.at[at]) for at, d in enumerate(ds)]
    for load in loads:
        load.start()
    for at, d in enumerate(ds):
        loads[at].wait()
        outs[at][...] = half(buf[at], 1 - side(g, zh, d))


def plan_kernel(lab, todo):
    k, _, _ = place()
    runs = lab.shape[0] // BLOCKS
    rows = [lab[k * runs + r] for r in range(runs)]
    for s in range(3):
        block = lax.rem(k + s, BLOCKS)
        base = 8 + s * SLOTS

        def column(c, count, block=block, base=base):
            label = lab[block * runs + c]
            first = sum((row < label).astype(jnp.int32) for row in rows)
            last = first + sum((row == label).astype(jnp.int32) for row in rows)

            def one(r, count):
                todo[base + count] = c * 256 + r * 16 + c
                return count + 1

            return lax.fori_loop(first, last, one, count)

        count = lax.fori_loop(0, runs, column, jnp.int32(0))
        todo[s] = count

        def fill(at, carry, base=base, count=count):
            todo[base + at] = runs * 256 + lax.rem(todo[base + count - 1], 256)
            return carry

        lax.fori_loop(count, lax.div(count + MANY - 1, MANY) * MANY, fill, 0)


def partial_kernel(groups, offsets, todo, *refs):
    n = len(groups)
    if n:
        t_ref, *refs = refs
        partners = sum(d > 0 for d in groups)
        got, refs = refs[:partners], refs[partners:]
    else:
        lhs, *refs = refs
    v_ref, _, *refs = refs
    outs, refs = refs[: len(offsets)], refs[len(offsets) :]
    if n:
        lhs, *refs = refs
    token, vbuf, acc, sems, *refs = refs
    width = v_ref.shape[0]
    runs = width // RUN
    k, g, zh = place()
    token[0] = k

    def tile(s, at, entry):
        r, c = lax.rem(lax.div(entry, 16), 16), lax.rem(entry, 16)
        source = v_ref.at[
            pl.ds(pl.multiple_of(r * RUN, RUN), RUN), pl.ds(pl.multiple_of(s * width + c * RUN, RUN), RUN)
        ]
        return source

    for at, (s, _) in enumerate(offsets):

        def begin(e, carry, at=at, s=s):
            source = tile(s, at, todo[8 + s * SLOTS + e])
            pltpu.make_async_copy(source, vbuf.at[at, e], sems.at[at]).start()
            return carry

        lax.fori_loop(0, todo[s], begin, 0)

    if n:
        tbuf, gbuf, load_sems = refs
        loads = []
        take = 0
        for at, d in enumerate(groups):
            load = [pltpu.make_async_copy(slab(t_ref, apart(g, d) if d else g), tbuf.at[at], load_sems.at[2 * at])]
            if d:
                load.append(pltpu.make_async_copy(got[take], gbuf.at[at], load_sems.at[2 * at + 1]))
                take += 1
            for one in load:
                one.start()
            loads.append(load)
        acc[...] = jnp.zeros_like(acc)
        for at, d in enumerate(groups):
            for one in loads[at]:
                one.wait()
            if d:
                s = side(g, zh, d)
                x, y = half(tbuf[at], s), gbuf[at]
                if d >= 2:
                    x, y = jnp.where(zh == 1, y, x), jnp.where(zh == 1, x, y)
                y = -dot(flip_matrix(s), y)
            else:
                own = tbuf[at].reshape(256, width)
                i, j, col = own_pairs(256)
                x = dot(ones_at(col == i * 16 + j), own).astype(jnp.bfloat16)
                y = -dot(ones_at(col == j * 16 + i), own)
            y = y.astype(jnp.bfloat16)
            for r in range(runs):
                lhs[at * G : (at + 1) * G, 2 * r * RUN : (2 * r + 1) * RUN] = x[:, r * RUN : (r + 1) * RUN]
                lhs[at * G : (at + 1) * G, (2 * r + 1) * RUN : (2 * r + 2) * RUN] = y[:, r * RUN : (r + 1) * RUN]
    else:
        acc[...] = jnp.zeros_like(acc)

    for at, (s, coded) in enumerate(offsets):

        def arrived(e, carry, at=at, s=s):
            pltpu.make_async_copy(tile(s, at, 0), vbuf.at[at, e], sems.at[at]).wait()
            return carry

        lax.fori_loop(0, todo[s], arrived, 0)

        def several(step, carry, at=at, s=s):
            products = []
            for u in range(MANY):
                e = step * MANY + u
                entry = todo[8 + s * SLOTS + e]
                c, r = lax.div(entry, 256), lax.rem(lax.div(entry, 16), 16)
                right = vbuf[at, jnp.minimum(e, todo[s] - 1)]
                left = lhs[:, pl.ds(pl.multiple_of(r * 2 * RUN, 2 * RUN), 2 * RUN)]
                products.append((c, dot(left, jnp.concatenate([right, right], axis=0))))
            for c, value in products:
                acc[at, :, pl.ds(pl.multiple_of(c * RUN, RUN), RUN)] += value
            return carry

        lax.fori_loop(0, lax.div(todo[s] + MANY - 1, MANY), several, 0)
        if coded:
            encode(acc[at, :, :width], outs[at])
        else:
            outs[at][...] = acc[at, :, :width]


def fetch(pairs, sems):
    copies = [pltpu.make_async_copy(a, b, sems.at[at]) for at, (a, b) in enumerate(pairs)]
    for copy in copies:
        copy.start()
    for copy in copies:
        copy.wait()


def merge_kernel(mine_ref, got_ref, out_ref, buf, sems):
    fetch([(got_ref, buf)], sems)
    _, _, zh = place()
    encode(mine_ref[...] + jnp.where(zh == 0, decode(buf), 0.0), out_ref)


def finish_kernel(ds, mine_ref, one_ref, two_ref, energy_ref, occ_ref, value_ref, code_ref, one, two, sems):
    fetch([(one_ref, one), (two_ref, two)], sems)
    _, g, zh = place()
    sums = []
    occ = thirds(occ_ref[...])
    for d in ds:
        if d:
            s = side(g, zh, d)
            row, col = iotas(G, 64)
            a, x, y = row >> 6, (row >> 3) & 7, row & 7
            p = apart(g, d)
            first, second = (g, p) if d == 1 else (jnp.where(zh == 1, p, g), jnp.where(zh == 1, g, p))
            i, j = a * OCT + x + first * 16, (a ^ s) * OCT + y + second * 16
        else:
            i, j, col = own_pairs(64)
            i, j = i + g * 16, j + g * 16
        pick = (col == i).astype(jnp.float32) + (col == j).astype(jnp.float32)
        sums.append(dot(thrice(pick.astype(jnp.bfloat16)), occ)[:, :1])
    sums = jnp.concatenate(sums, axis=0) if len(sums) > 1 else sums[0]
    first = decode(one)
    if ds[-1] >= 2:
        first = jnp.where(zh == 1, first, 0.0)
    value = (mine_ref[...] + first + decode(two)) / (energy_ref[...] - sums)
    value_ref[...] = value
    encode(value[-G:], code_ref)


def put(out_ref, buf, value, d, w, turned, g, sems, at):
    p = apart(g, d)
    copies = []
    buf[at] = value.reshape(2, OCT, OCT, value.shape[1])
    for a in range(2):
        o = p * 2 + lax.rem(a + w + turned, 2)
        copy = pltpu.make_async_copy(
            buf.at[at, a],
            out_ref.at[a * OCT : (a + 1) * OCT, pl.ds(pl.multiple_of(o * OCT, OCT), OCT), :],
            sems.at[at, a],
        )
        copy.start()
        copies.append(copy)
    return copies


def returned(ref, d, w, zh):
    code = codes(ref)
    pieces = jnp.concatenate(
        [(code >> 8).astype(jnp.float32).astype(jnp.bfloat16), (code & 255).astype(jnp.float32).astype(jnp.bfloat16)]
    )
    flip = flip_matrix(1 - w).astype(jnp.float32)
    turned = dot(jnp.concatenate([flip * -256.0, -flip], axis=1).astype(jnp.bfloat16), pieces)
    if d == 1:
        return turned * scales(ref), 1
    return jnp.where(zh == 1, code.astype(jnp.float32), turned) * scales(ref), 1 - zh


def own_kernel(near_ref, second_ref, third_ref, got1_ref, out_ref, got1, square, buf, sems, load_sems):
    load = pltpu.make_async_copy(got1_ref, got1, load_sems.at[0])
    load.start()
    _, g, zh = place()
    copies = []
    for at, (d, mine) in enumerate(((2, second_ref[...]), (3, third_ref[...]), (1, near_ref[G:]))):
        w = later(g, d)
        if d == 1:
            copies += put(out_ref, buf, mine, d, w, 0, g, sems, at)
        else:
            turned = -dot(thrice(flip_matrix(1 - w)), thirds(mine))
            copies += put(out_ref, buf, jnp.where(zh == 1, turned, mine), d, w, zh, g, sems, at)
    row, col = iotas(256, G)
    i, j = row >> 4, row & 15
    oi, oj, xi, xj = i >> 3, j >> 3, i & 7, j & 7
    gap = (xj - xi) & 7
    up = 64 + oi * 32 + (gap - 1) * 8 + xi
    down = 64 + oi * 32 + (7 - gap) * 8 + xj
    same = oi == oj
    plus = jnp.where(same, jnp.where((gap >= 1) & (gap <= 4), up, -1), jnp.where(oi < oj, xi * 8 + xj, -1))
    minus = jnp.where(same, jnp.where(gap >= 5, down, -1), jnp.where(oi > oj, xj * 8 + xi, -1))
    pick = (col == plus).astype(jnp.float32) - (col == minus).astype(jnp.float32)
    square[...] = dot(thrice(pick.astype(jnp.bfloat16)), thirds(near_ref[:G])).reshape(square.shape)
    copy = pltpu.make_async_copy(square, slab(out_ref, g), load_sems.at[1])
    copy.start()
    copies.append(copy)
    load.wait()
    w = later(g, 1)
    value, turned = returned(got1, 1, w, zh)
    copies += put(out_ref, buf, value, 1, w, turned, g, sems, 3)
    for copy in copies:
        copy.wait()


def back_kernel(d, got_ref, _, out_ref, got, buf, sems, load_sems):
    fetch([(got_ref, got)], load_sems)
    _, g, zh = place()
    w = later(g, d)
    value, turned = returned(got, d, w, zh)
    for copy in put(out_ref, buf, value, d, w, turned, g, sems, 0):
        copy.wait()


def call(kernel, name, outs, args, in_specs, out_specs, scratch=(), flops=0, moved=0, aliases={}, room=12):
    return pl.pallas_call(
        kernel,
        out_shape=outs,
        in_specs=in_specs,
        out_specs=out_specs,
        scratch_shapes=scratch,
        input_output_aliases=aliases,
        compiler_params=pltpu.CompilerParams(vmem_limit_bytes=room * MIB),
        cost_estimate=pl.CostEstimate(flops=flops, bytes_accessed=moved, transcendentals=0),
        name=name,
    )(*args)


def plain(rows, width):
    return jax.ShapeDtypeStruct((rows, width), jnp.float32)


def coded(rows, width):
    return jax.ShapeDtypeStruct((rows + PAD, width), jnp.int16)


def partials(name, groups, offsets, todo, rows, integrals, token, amplitudes=None, got=(), lhs=None):
    width = integrals.shape[0]
    outs = [coded(rows, width) if as_code else plain(rows, width) for _, as_code in offsets]
    scratch = [
        pltpu.VMEM((len(offsets), 144, RUN, RUN), jnp.bfloat16),
        pltpu.VMEM((len(offsets), rows, width + RUN), jnp.float32),
        pltpu.SemaphoreType.DMA((len(offsets),)),
    ]
    if groups:
        args = (todo, amplitudes, *got, integrals, token)
        specs = [IN_SMEM] + [ANY] * (2 + len(got)) + [IN_SMEM]
        outs.append(jax.ShapeDtypeStruct((rows, 2 * width), jnp.bfloat16))
        scratch += [
            pltpu.VMEM((len(groups), 16, 16, width), jnp.bfloat16),
            pltpu.VMEM((len(groups), G, width), jnp.bfloat16),
            pltpu.SemaphoreType.DMA((2 * len(groups),)),
        ]
    else:
        args = (todo, lhs, integrals, token)
        specs = [IN_SMEM, IN_VMEM, ANY, IN_SMEM]
    return call(
        functools.partial(partial_kernel, groups, offsets),
        name,
        outs + [TOKEN],
        args,
        specs,
        [IN_VMEM] * len(outs) + [IN_SMEM],
        scratch,
        flops=len(offsets) * rows * width * width // 2,
        moved=4 * 1024 * 1024,
        room=26,
    )


def per_device(amplitudes, integrals, pair_irrep, pair_energy, occ_energy):
    i_local, nocc, width = amplitudes.shape
    labels = pair_irrep.reshape(-1, RUN)[:, 0]
    energy = pair_energy.reshape(1, width)
    occ = jnp.broadcast_to(occ_energy[:, None], (nocc, RUN))

    def split(ds):
        return call(
            functools.partial(split_kernel, ds),
            "split" + "".join(map(str, ds)),
            [jax.ShapeDtypeStruct((G, width), jnp.bfloat16)] * len(ds),
            (amplitudes,),
            [ANY],
            [IN_VMEM] * len(ds),
            [pltpu.VMEM((len(ds), 16, 16, width), jnp.bfloat16), pltpu.SemaphoreType.DMA((len(ds),))],
            moved=2 * 1024 * 1024,
        )

    (go2,) = split((2,))
    got2 = send(go2, lambda b, o: (b, o ^ 2))
    go3, go1 = split((3, 1))
    got3 = send(go3, lambda b, o: (b, o ^ 3))
    got1 = send(go1, lambda b, o: (b, o ^ 1))
    (todo,) = call(
        plan_kernel,
        "plan",
        [jax.ShapeDtypeStruct((8 + 3 * SLOTS,), jnp.int32)],
        (labels,),
        [IN_SMEM],
        [IN_SMEM],
        moved=1024 * 1024,
    )

    near1, near2, near_rows, token = partials(
        "near", (0, 1), ((1, 1), (2, 1)), todo, 2 * G, integrals, todo, amplitudes, (got1,)
    )
    near1 = send(near1, lambda b, o: (b + 1, o))
    near2 = send(near2, lambda b, o: (b + 2, o))

    far = {}
    for d, got in ((2, got2), (3, got3)):
        far1, rows, token = partials("far%d" % d, (d,), ((1, 1),), todo, G, integrals, token, amplitudes, (got,))
        far[d] = send(far1, lambda b, o, d=d: (b ^ 1, o ^ d)), rows
    base = {}
    for d in (2, 3):
        far2, far0, token = partials("rest%d" % d, (), ((2, 0), (0, 0)), todo, G, integrals, token, lhs=far[d][1])
        base[d] = far0, far2
    near0, token = partials("rest1", (), ((0, 0),), todo, 2 * G, integrals, token, lhs=near_rows)

    onward = {}
    for d in (2, 3):
        far1, _ = far[d]
        (far2,) = call(
            merge_kernel,
            "merge%d" % d,
            [coded(G, width)],
            (base[d][1], far1),
            [IN_VMEM, ANY],
            [IN_VMEM],
            [pltpu.VMEM((G + PAD, width), jnp.int16), pltpu.SemaphoreType.DMA((1,))],
            moved=2 * 1024 * 1024,
        )
        onward[d] = send(far2, lambda b, o: (b + 2, o))

    def finish(name, ds, mine, one, two):
        rows = G * len(ds)
        return call(
            functools.partial(finish_kernel, ds),
            name,
            [plain(rows, width), coded(G, width)],
            (mine, one, two, energy, occ),
            [IN_VMEM, ANY, ANY, IN_VMEM, IN_VMEM],
            [IN_VMEM] * 2,
            [
                pltpu.VMEM((rows + PAD, width), jnp.int16),
                pltpu.VMEM((rows + PAD, width), jnp.int16),
                pltpu.SemaphoreType.DMA((2,)),
            ],
            moved=2 * 1024 * 1024,
        )

    done, back = {}, {}
    for d in (2, 3):
        done[d], code = finish("finish%d" % d, (d,), base[d][0], far[d][0], onward[d])
        back[d] = send(code, lambda b, o, d=d: (b, o ^ d))
    near, code = finish("finish1", (0, 1), near0, near1, near2)
    back1 = send(code, lambda b, o: (b, o ^ 1))

    out = jax.ShapeDtypeStruct((i_local, nocc, width), jnp.float32)
    landed = pltpu.VMEM((G + PAD, width), jnp.int16)
    (whole,) = call(
        own_kernel,
        "own",
        [out],
        (near, done[2], done[3], back1),
        [IN_VMEM, IN_VMEM, IN_VMEM, ANY],
        [ANY],
        [
            landed,
            pltpu.VMEM((16, 16, width), jnp.float32),
            pltpu.VMEM((4, 2, OCT, OCT, width), jnp.float32),
            pltpu.SemaphoreType.DMA((4, 2)),
            pltpu.SemaphoreType.DMA((2,)),
        ],
        moved=6 * 1024 * 1024,
        room=24,
    )
    for d in (2, 3):
        (whole,) = call(
            functools.partial(back_kernel, d),
            "back%d" % d,
            [out],
            (back[d], whole),
            [ANY, ANY],
            [ANY],
            [
                landed,
                pltpu.VMEM((1, 2, OCT, OCT, width), jnp.float32),
                pltpu.SemaphoreType.DMA((1, 2)),
                pltpu.SemaphoreType.DMA((1,)),
            ],
            moved=2 * 1024 * 1024,
            aliases={1: 0},
        )
    return whole


def solution(mesh):
    placed = (P("occ", None, "blk"), P("blk", None), P(), P("blk"), P())
    return jax.shard_map(
        per_device, mesh=mesh, in_specs=placed, out_specs=P("occ", None, "blk"), check_vma=False
    )
```

time: 560 us -> 107 us (0.19)
  the two profiles are of different devices: /device:TPU:1 before, /device:TPU:64 now
where the time goes in v2:
time: 107 us
  Pallas kernels  46.9 us (44%)
  waiting for transfers between devices  46 us (43%)
  local copies, waits for them, and re-layouts  7.15 us (7%)
  starting transfers between devices  6.83 us (6%)
    pallas_call x17, Pallas kernels, call(): pl.pallas_call(kernel, out_shape=outs, in_specs=in_specs, out_specs=out_s...  46.9 us
    ppermute x12, waiting for transfers between devices, send(): return lax.ppermute(value, BOTH, routes(where))  46 us
    unnamed x14, local copies, waits for them, and re-layouts  6.93 us
    ppermute x12, starting transfers between devices, send(): return lax.ppermute(value, BOTH, routes(where))  6.83 us
  transfers between devices with their start and end apart: 12, of which 6 were waited for; matrix products, arithmetic and copies ran while one was open for 0% of the time, Pallas kernels for 42%

profile of v2, /device:TPU:64, one launch (start us, length us, event | category | flops | bytes accessed | tf_op | source)
XLA Modules:
  0.0 107.3 jit_solution(10098267561166631944)
XLA Ops:
  0.0 0.0 copy-start.2
  0.0 1.9 %copy-done.2 = bf16[16,64,1536]{2,1,0:T(8,128)(2,1)S(1)} copy-done((bf16[16,64,1536]{2,1,0:T(8,128)(2,1)S(1)}, bf16[16,64,1536]{2,1,0:T(8,128)(2,1)}, u32[]{:S(2)}) %copy-start.2) | copy-done | bytes 3145752
  1.9 0.0 copy-start.4
  1.9 0.0 copy-start.3
  1.9 0.3 split31.1
  2.2 0.1 collective-permute-start.2
  2.3 0.2 split2.1
  2.5 1.7 %collective-permute-start.1 = (bf16[128,1536]{1,0:T(8,128)(2,1)S(1)}, bf16[128,1536]{1,0:T(8,128)(2,1)S(1)}, u32[]{:S(2)}, u32[]{:S(2)}) collective-permute-start(bf16[128,1536]{1,0:T(8,128)(2,1)S(1)} %split2.1), channel_id=1, source_target_pairs={{0,2},{1,3},{2,0},{3,1},{4,6},{5,7},{6,4},{7,5},{8,10},{9,11},{10,... | collective-permute-start | bytes 1179656 | tf_op jit(solution)/shard_map/ppermute | solution.py:37
  4.2 0.2 collective-permute-start
  4.4 0.0 copy-done.4
  4.4 0.1 slice_reduce_fusion.lab
  4.5 3.4 %plan.1.todo.refs_3_ = s32[488]{0:T(512)S(1)} custom-call(s32[384]{0:T(512)S(1)} %slice_reduce_fusion.lab), custom_call_target="tpu_custom_call" | custom-call | bytes 1048576 | tf_op jit(solution)/shard_map/plan/pallas_call | solution.py:389
  8.0 0.0 collective-permute-done.2.refs_1_
  8.0 0.0 copy-done.3
  8.0 0.0 copy-start
  8.0 5.0 %copy-done = bf16[1536,4608]{1,0:T(8,128)(2,1)S(1)} copy-done((bf16[1536,4608]{1,0:T(8,128)(2,1)S(1)}, bf16[1536,4608]{1,0:T(8,128)(2,1)}, u32[]{:S(2)}) %copy-start) | copy-done | bytes 14155800
  13.0 0.0 copy-start.1
  13.0 7.9 %near.1 = (s16[272,1536]{1,0:T(8,128)(2,1)}, s16[272,1536]{1,0:T(8,128)(2,1)S(1)}, bf16[256,3072]{1,0:T(8,128)(2,1)S(1)}, s32[8]{0:T(128)S(1)}) custom-call(s32[488]{0:T(512)S(1)} %plan.1.todo.refs_3_, bf16[16,64,1536]{2,1,0:T(8,128)(2,1)S(1)} %copy-done.3, bf16[128,1536]{1,0:T(8,128)(2,1)S(1)} %collective-permute-done.2.refs_1_, ...), custom_call_target="tpu_custom_call" | custom-call | flops 603979776 | bytes 4194304 | tf_op jit(solution)/shard_map/near/pallas_call | solution.py:389
  20.9 0.0 collective-permute-done.1.refs_1_
  20.9 0.0 copy-done.1
  20.9 3.4 %far2.1 = (s16[144,1536]{1,0:T(8,128)(2,1)S(1)}, bf16[128,3072]{1,0:T(8,128)(2,1)S(1)}, s32[8]{0:T(128)S(1)}) custom-call(s32[488]{0:T(512)S(1)} %plan.1.todo.refs_3_, bf16[16,64,1536]{2,1,0:T(8,128)(2,1)S(1)} %copy-done.3, bf16[128,1536]{1,0:T(8,128)(2,1)S(1)} %collective-permute-done.1.refs_1_, bf16[1536,4608]{1,0:T(8,128)(2,1)S(1)} %copy-done.1, ...), custom_call_target="tpu_custom_call" | custom-call | flops 150994944 | bytes 4194304 | tf_op jit(solution)/shard_map/far2/pallas_call | solution.py:389
  24.4 0.1 collective-permute-start.6
  24.5 0.0 collective-permute-done.refs_1_
  24.5 3.4 %far3.1 = (s16[144,1536]{1,0:T(8,128)(2,1)S(1)}, bf16[128,3072]{1,0:T(8,128)(2,1)S(1)}, s32[8]{0:T(128)S(1)}) custom-call(s32[488]{0:T(512)S(1)} %plan.1.todo.refs_3_, bf16[16,64,1536]{2,1,0:T(8,128)(2,1)S(1)} %copy-done.3, bf16[128,1536]{1,0:T(8,128)(2,1)S(1)} %collective-permute-done.refs_1_, bf16[1536,4608]{1,0:T(8,128)(2,1)S(1)} %copy-done.1, ...), custom_call_target="tpu_custom_call" | custom-call | flops 150994944 | bytes 4194304 | tf_op jit(solution)/shard_map/far3/pallas_call | solution.py:389
  27.9 2.1 %collective-permute-start.3 = (s16[144,1536]{1,0:T(8,128)(2,1)S(1)}, s16[144,1536]{1,0:T(8,128)(2,1)S(1)}, u32[]{:S(2)}, u32[]{:S(2)}) collective-permute-start(s16[144,1536]{1,0:T(8,128)(2,1)S(1)} %get-tuple-element.39), channel_id=1, source_target_pairs={{0,7},{1,6},{2,5},{3,4},{4,3},{5,2},{6,1},{7,0},{8,15},{9,14},{10,... | collective-permute-start | bytes 1327112 | tf_op jit(solution)/shard_map/ppermute | solution.py:37
  30.0 0.7 collective-permute-start.9
  30.7 1.2 %collective-permute-start.10 = (s16[272,1536]{1,0:T(8,128)(2,1)S(1)}, s16[272,1536]{1,0:T(8,128)(2,1)S(1)}, u32[]{:S(2)}, u32[]{:S(2)}) collective-permute-start(s16[272,1536]{1,0:T(8,128)(2,1)S(1)} %get-tuple-element.50), channel_id=1, source_target_pairs={{0,8},{1,9},{2,10},{3,11},{4,12},{5,13},{6,14},{7,15},{8,16},{9,17... | collective-permute-start | bytes 2506760 | tf_op jit(solution)/shard_map/ppermute | solution.py:37
  31.9 6.1 %rest2.1 = (f32[128,1536]{1,0:T(8,128)S(1)}, f32[128,1536]{1,0:T(8,128)S(1)}, s32[8]{0:T(128)S(1)}) custom-call(s32[488]{0:T(512)S(1)} %plan.1.todo.refs_3_, bf16[128,3072]{1,0:T(8,128)(2,1)S(1)} %get-tuple-element.35.refs_0_, bf16[1536,4608]{1,0:T(8,128)(2,1)S(1)} %copy-done.1, s32[8]{0:T(128)S(1)} %get-tuple-element.36.refs_2_), custom_call_target="tpu_custom_call" | custom-call | flops 301989888 | bytes 4194304 | tf_op jit(solution)/shard_map/rest2/pallas_call | solution.py:389
  37.9 17.4 %collective-permute-done.6.got_ref.one_ref = s16[144,1536]{1,0:T(8,128)(2,1)S(1)} collective-permute-done((s16[144,1536]{1,0:T(8,128)(2,1)S(1)}, s16[144,1536]{1,0:T(8,128)(2,1)S(1)}, u32[]{:S(2)}, u32[]{:S(2)}) %collective-permute-start.6) | collective-permute-done | bytes 442400 | tf_op jit(solution)/shard_map/ppermute | solution.py:37
  55.4 0.6 merge2.1
  55.9 0.1 collective-permute-start.7
  56.0 0.0 copy-start.5
  56.0 6.1 %rest3.1 = (f32[128,1536]{1,0:T(8,128)S(1)}, f32[128,1536]{1,0:T(8,128)S(1)}, s32[8]{0:T(128)S(1)}) custom-call(s32[488]{0:T(512)S(1)} %plan.1.todo.refs_3_, bf16[128,3072]{1,0:T(8,128)(2,1)S(1)} %get-tuple-element.34.refs_0_, bf16[1536,4608]{1,0:T(8,128)(2,1)S(1)} %copy-done.1, s32[8]{0:T(128)S(1)} %get-tuple-element.37.refs_2_), custom_call_target="tpu_custom_call" | custom-call | flops 301989888 | bytes 4194304 | tf_op jit(solution)/shard_map/rest3/pallas_call | solution.py:389
  62.1 1.5 %collective-permute-done.3.got_ref.one_ref = s16[144,1536]{1,0:T(8,128)(2,1)S(1)} collective-permute-done((s16[144,1536]{1,0:T(8,128)(2,1)S(1)}, s16[144,1536]{1,0:T(8,128)(2,1)S(1)}, u32[]{:S(2)}, u32[]{:S(2)}) %collective-permute-start.3) | collective-permute-done | bytes 442400 | tf_op jit(solution)/shard_map/ppermute | solution.py:37
  63.6 0.6 merge3.1
  64.2 0.1 collective-permute-start.4
  64.3 0.0 copy-done.5
  64.3 0.0 copy-start.6
  64.3 4.9 %rest1.1 = (f32[256,1536]{1,0:T(8,128)S(1)}, s32[8]{0:T(128)}) custom-call(s32[488]{0:T(512)S(1)} %plan.1.todo.refs_3_, bf16[256,3072]{1,0:T(8,128)(2,1)S(1)} %get-tuple-element.46.refs_0_, bf16[1536,4608]{1,0:T(8,128)(2,1)S(1)} %copy-done.1, s32[8]{0:T(128)S(1)} %get-tuple-element.47.refs_2_), custom_call_target="tpu_custom_call" | custom-call | flops 301989888 | bytes 4194304 | tf_op jit(solution)/shard_map/rest1/pallas_call | solution.py:389
  69.3 0.0 collective-permute-done.9.one_ref
  69.3 5.2 %collective-permute-done.10.two_ref = s16[272,1536]{1,0:T(8,128)(2,1)S(1)} collective-permute-done((s16[272,1536]{1,0:T(8,128)(2,1)S(1)}, s16[272,1536]{1,0:T(8,128)(2,1)S(1)}, u32[]{:S(2)}, u32[]{:S(2)}) %collective-permute-start.10) | collective-permute-done | bytes 835616 | tf_op jit(solution)/shard_map/ppermute | solution.py:37
  74.4 0.0 copy-done.6
  74.4 0.1 broadcast_in_dim.2.occ_ref
  74.5 1.2 %finish1.1 = (f32[256,1536]{1,0:T(8,128)S(1)}, s16[144,1536]{1,0:T(8,128)(2,1)S(1)}) custom-call(f32[256,1536]{1,0:T(8,128)S(1)} %get-tuple-element.48.mine_ref, s16[272,1536]{1,0:T(8,128)(2,1)S(1)} %collective-permute-done.9.one_ref, s16[272,1536]{1,0:T(8,128)(2,1)S(1)} %collective-permute-done.10.two_ref, f32[1,1536]{1,0:T(1,128)S(1)} %reshape.8.energy_ref, ...), custom_call_target="tpu_custom_call" | custom-call | bytes 2097152 | tf_op jit(solution)/shard_map/finish1/pallas_call | solution.py:389
  75.7 0.1 collective-permute-start.11
  75.8 8.1 %collective-permute-done.7.two_ref = s16[144,1536]{1,0:T(8,128)(2,1)S(1)} collective-permute-done((s16[144,1536]{1,0:T(8,128)(2,1)S(1)}, s16[144,1536]{1,0:T(8,128)(2,1)S(1)}, u32[]{:S(2)}, u32[]{:S(2)}) %collective-permute-start.7) | collective-permute-done | bytes 442400 | tf_op jit(solution)/shard_map/ppermute | solution.py:37
  83.9 1.2 %finish2.1 = (f32[128,1536]{1,0:T(8,128)S(1)}, s16[144,1536]{1,0:T(8,128)(2,1)S(1)}) custom-call(f32[128,1536]{1,0:T(8,128)S(1)} %get-tuple-element.42.mine_ref, s16[144,1536]{1,0:T(8,128)(2,1)S(1)} %collective-permute-done.6.got_ref.one_ref, s16[144,1536]{1,0:T(8,128)(2,1)S(1)} %collective-permute-done.7.two_ref, f32[1,1536]{1,0:T(1,128)S(1)} %reshape.8.energy_ref, ...), custom_call_target="tpu_custom_call" | custom-call | bytes 2097152 | tf_op jit(solution)/shard_map/finish2/pallas_call | solution.py:389
  85.2 0.5 collective-permute-start.8
  85.6 6.9 %collective-permute-done.4.two_ref = s16[144,1536]{1,0:T(8,128)(2,1)S(1)} collective-permute-done((s16[144,1536]{1,0:T(8,128)(2,1)S(1)}, s16[144,1536]{1,0:T(8,128)(2,1)S(1)}, u32[]{:S(2)}, u32[]{:S(2)}) %collective-permute-start.4) | collective-permute-done | bytes 442400 | tf_op jit(solution)/shard_map/ppermute | solution.py:37
  92.5 1.2 %finish3.1 = (f32[128,1536]{1,0:T(8,128)S(1)}, s16[144,1536]{1,0:T(8,128)(2,1)S(1)}) custom-call(f32[128,1536]{1,0:T(8,128)S(1)} %get-tuple-element.38.mine_ref, s16[144,1536]{1,0:T(8,128)(2,1)S(1)} %collective-permute-done.3.got_ref.one_ref, s16[144,1536]{1,0:T(8,128)(2,1)S(1)} %collective-permute-done.4.two_ref, f32[1,1536]{1,0:T(1,128)S(1)} %reshape.8.energy_ref, ...), custom_call_target="tpu_custom_call" | custom-call | bytes 2097152 | tf_op jit(solution)/shard_map/finish3/pallas_call | solution.py:389
  93.7 0.1 collective-permute-start.5
  93.8 0.0 collective-permute-done.11.got1_ref
  93.8 3.4 %own.1._ = f32[16,64,1536]{2,1,0:T(8,128)} custom-call(f32[256,1536]{1,0:T(8,128)S(1)} %get-tuple-element.51.near_ref, f32[128,1536]{1,0:T(8,128)S(1)} %get-tuple-element.52.second_ref, f32[128,1536]{1,0:T(8,128)S(1)} %get-tuple-element.53.third_ref, s16[144,1536]{1,0:T(8,128)(2,1)S(1)} %collective-permute-done.11.got1_ref), custom_call_target="tpu_custom_call" | custom-call | bytes 6291456 | tf_op jit(solution)/shard_map/own/pallas_call | solution.py:389
  97.2 0.0 collective-permute-done.8.got_ref
  97.2 1.5 %back2.1._ = f32[16,64,1536]{2,1,0:T(8,128)} custom-call(s16[144,1536]{1,0:T(8,128)(2,1)S(1)} %collective-permute-done.8.got_ref, f32[16,64,1536]{2,1,0:T(8,128)} %own.1._), custom_call_target="tpu_custom_call", output_to_operand_aliasing={{}: (1, {})} | custom-call | bytes 2097152 | tf_op jit(solution)/shard_map/back2/pallas_call | solution.py:389
  98.7 6.9 %collective-permute-done.5.got_ref = s16[144,1536]{1,0:T(8,128)(2,1)S(1)} collective-permute-done((s16[144,1536]{1,0:T(8,128)(2,1)S(1)}, s16[144,1536]{1,0:T(8,128)(2,1)S(1)}, u32[]{:S(2)}, u32[]{:S(2)}) %collective-permute-start.5) | collective-permute-done | bytes 442400 | tf_op jit(solution)/shard_map/ppermute | solution.py:37
  105.6 1.5 %back3.1 = f32[16,64,1536]{2,1,0:T(8,128)} custom-call(s16[144,1536]{1,0:T(8,128)(2,1)S(1)} %collective-permute-done.5.got_ref, f32[16,64,1536]{2,1,0:T(8,128)} %back2.1._), custom_call_target="tpu_custom_call", output_to_operand_aliasing={{}: (1, {})} | custom-call | bytes 2097152 | tf_op jit(solution)/shard_map/back3/pallas_call | solution.py:389
  (1 shorter events, 0.0 us)
Async XLA Ops:
  0.0 1.9 %copy-start.2 = (bf16[16,64,1536]{2,1,0:T(8,128)(2,1)S(1)}, bf16[16,64,1536]{2,1,0:T(8,128)(2,1)}, u32[]{:S(2)}) copy-start(bf16[16,64,1536]{2,1,0:T(8,128)(2,1)} %refs_0_.5) | copy-start | bytes 9437188
  1.9 2.5 %copy-start.4 = (s32[49152]{0:T(1024)S(1)}, s32[49152]{0:T(1024)}, u32[]{:S(2)}) copy-start(s32[49152]{0:T(1024)} %param.7) | copy-start | bytes 589828
  1.9 6.1 %copy-start.3 = (bf16[16,64,1536]{2,1,0:T(8,128)(2,1)S(1)}, bf16[16,64,1536]{2,1,0:T(8,128)(2,1)}, u32[]{:S(2)}) copy-start(bf16[16,64,1536]{2,1,0:T(8,128)(2,1)} %refs_0_.5) | copy-start | bytes 9437188
  2.2 5.8 %collective-permute-start.2 = (bf16[128,1536]{1,0:T(8,128)(2,1)S(1)}, bf16[128,1536]{1,0:T(8,128)(2,1)S(1)}, u32[]{:S(2)}, u32[]{:S(2)}) collective-permute-start(bf16[128,1536]{1,0:T(8,128)(2,1)S(1)} %get-tuple-element.31), channel_id=1, source_target_pairs={{0,1},{1,0},{2,3},{3,2},{4,5},{5,4},{6,7},{7,6},{8,9},{9,8},{10,11... | collective-permute-start | bytes 1179656 | tf_op jit(solution)/shard_map/ppermute | solution.py:37
  2.5 18.4 %collective-permute-start.1 = (bf16[128,1536]{1,0:T(8,128)(2,1)S(1)}, bf16[128,1536]{1,0:T(8,128)(2,1)S(1)}, u32[]{:S(2)}, u32[]{:S(2)}) collective-permute-start(bf16[128,1536]{1,0:T(8,128)(2,1)S(1)} %split2.1), channel_id=1, source_target_pairs={{0,2},{1,3},{2,0},{3,1},{4,6},{5,7},{6,4},{7,5},{8,10},{9,11},{10,... | collective-permute-start | bytes 1179656 | tf_op jit(solution)/shard_map/ppermute | solution.py:37
  4.2 20.3 %collective-permute-start = (bf16[128,1536]{1,0:T(8,128)(2,1)S(1)}, bf16[128,1536]{1,0:T(8,128)(2,1)S(1)}, u32[]{:S(2)}, u32[]{:S(2)}) collective-permute-start(bf16[128,1536]{1,0:T(8,128)(2,1)S(1)} %get-tuple-element.30), channel_id=1, source_target_pairs={{0,3},{1,2},{2,1},{3,0},{4,7},{5,6},{6,5},{7,4},{8,11},{9,10},{10,... | collective-permute-start | bytes 1179656 | tf_op jit(solution)/shard_map/ppermute | solution.py:37
  8.0 5.0 %copy-start = (bf16[1536,4608]{1,0:T(8,128)(2,1)S(1)}, bf16[1536,4608]{1,0:T(8,128)(2,1)}, u32[]{:S(2)}) copy-start(bf16[1536,4608]{1,0:T(8,128)(2,1)} %refs_1_.5) | copy-start | bytes 42467332
  13.0 7.9 %copy-start.1 = (bf16[1536,4608]{1,0:T(8,128)(2,1)S(1)}, bf16[1536,4608]{1,0:T(8,128)(2,1)}, u32[]{:S(2)}) copy-start(bf16[1536,4608]{1,0:T(8,128)(2,1)} %refs_1_.5) | copy-start | bytes 42467332
  24.4 31.0 %collective-permute-start.6 = (s16[144,1536]{1,0:T(8,128)(2,1)S(1)}, s16[144,1536]{1,0:T(8,128)(2,1)S(1)}, u32[]{:S(2)}, u32[]{:S(2)}) collective-permute-start(s16[144,1536]{1,0:T(8,128)(2,1)S(1)} %get-tuple-element.43), channel_id=1, source_target_pairs={{0,6},{1,7},{2,4},{3,5},{4,2},{5,3},{6,0},{7,1},{8,14},{9,15},{10,... | collective-permute-start | bytes 1327112 | tf_op jit(solution)/shard_map/ppermute | solution.py:37
  27.9 35.7 %collective-permute-start.3 = (s16[144,1536]{1,0:T(8,128)(2,1)S(1)}, s16[144,1536]{1,0:T(8,128)(2,1)S(1)}, u32[]{:S(2)}, u32[]{:S(2)}) collective-permute-start(s16[144,1536]{1,0:T(8,128)(2,1)S(1)} %get-tuple-element.39), channel_id=1, source_target_pairs={{0,7},{1,6},{2,5},{3,4},{4,3},{5,2},{6,1},{7,0},{8,15},{9,14},{10,... | collective-permute-start | bytes 1327112 | tf_op jit(solution)/shard_map/ppermute | solution.py:37
  30.0 39.3 %collective-permute-start.9 = (s16[272,1536]{1,0:T(8,128)(2,1)}, s16[272,1536]{1,0:T(8,128)(2,1)S(1)}, u32[]{:S(2)}, u32[]{:S(2)}) collective-permute-start(s16[272,1536]{1,0:T(8,128)(2,1)} %get-tuple-element.49), channel_id=1, source_target_pairs={{0,4},{1,5},{2,6},{3,7},{4,8},{5,9},{6,10},{7,11},{8,12},{9,13},{1... | collective-permute-start | bytes 2506760 | tf_op jit(solution)/shard_map/ppermute | solution.py:37
  30.7 43.8 %collective-permute-start.10 = (s16[272,1536]{1,0:T(8,128)(2,1)S(1)}, s16[272,1536]{1,0:T(8,128)(2,1)S(1)}, u32[]{:S(2)}, u32[]{:S(2)}) collective-permute-start(s16[272,1536]{1,0:T(8,128)(2,1)S(1)} %get-tuple-element.50), channel_id=1, source_target_pairs={{0,8},{1,9},{2,10},{3,11},{4,12},{5,13},{6,14},{7,15},{8,16},{9,17... | collective-permute-start | bytes 2506760 | tf_op jit(solution)/shard_map/ppermute | solution.py:37
  55.9 28.0 %collective-permute-start.7 = (s16[144,1536]{1,0:T(8,128)(2,1)S(1)}, s16[144,1536]{1,0:T(8,128)(2,1)S(1)}, u32[]{:S(2)}, u32[]{:S(2)}) collective-permute-start(s16[144,1536]{1,0:T(8,128)(2,1)S(1)} %merge2.1), channel_id=1, source_target_pairs={{0,8},{1,9},{2,10},{3,11},{4,12},{5,13},{6,14},{7,15},{8,16},{9,17... | collective-permute-start | bytes 1327112 | tf_op jit(solution)/shard_map/ppermute | solution.py:37
  56.0 8.3 %copy-start.5 = (f32[1536]{0:T(1024)S(1)}, f32[1536]{0:T(1024)}, u32[]{:S(2)}) copy-start(f32[1536]{0:T(1024)} %param.8) | copy-start | bytes 18436
  64.2 28.3 %collective-permute-start.4 = (s16[144,1536]{1,0:T(8,128)(2,1)S(1)}, s16[144,1536]{1,0:T(8,128)(2,1)S(1)}, u32[]{:S(2)}, u32[]{:S(2)}) collective-permute-start(s16[144,1536]{1,0:T(8,128)(2,1)S(1)} %merge3.1), channel_id=1, source_target_pairs={{0,8},{1,9},{2,10},{3,11},{4,12},{5,13},{6,14},{7,15},{8,16},{9,17... | collective-permute-start | bytes 1327112 | tf_op jit(solution)/shard_map/ppermute | solution.py:37
  64.3 10.1 %copy-start.6 = (f32[64]{0:T(128)S(1)}, f32[64]{0:T(128)}, u32[]{:S(2)}) copy-start(f32[64]{0:T(128)} %param.9) | copy-start | bytes 772
  75.7 18.1 %collective-permute-start.11 = (s16[144,1536]{1,0:T(8,128)(2,1)S(1)}, s16[144,1536]{1,0:T(8,128)(2,1)S(1)}, u32[]{:S(2)}, u32[]{:S(2)}) collective-permute-start(s16[144,1536]{1,0:T(8,128)(2,1)S(1)} %get-tuple-element.54), channel_id=1, source_target_pairs={{0,1},{1,0},{2,3},{3,2},{4,5},{5,4},{6,7},{7,6},{8,9},{9,8},{10,11... | collective-permute-start | bytes 1327112 | tf_op jit(solution)/shard_map/ppermute | solution.py:37
  85.2 12.0 %collective-permute-start.8 = (s16[144,1536]{1,0:T(8,128)(2,1)S(1)}, s16[144,1536]{1,0:T(8,128)(2,1)S(1)}, u32[]{:S(2)}, u32[]{:S(2)}) collective-permute-start(s16[144,1536]{1,0:T(8,128)(2,1)S(1)} %get-tuple-element.45), channel_id=1, source_target_pairs={{0,2},{1,3},{2,0},{3,1},{4,6},{5,7},{6,4},{7,5},{8,10},{9,11},{10,... | collective-permute-start | bytes 1327112 | tf_op jit(solution)/shard_map/ppermute | solution.py:37
  93.7 11.9 %collective-permute-start.5 = (s16[144,1536]{1,0:T(8,128)(2,1)S(1)}, s16[144,1536]{1,0:T(8,128)(2,1)S(1)}, u32[]{:S(2)}, u32[]{:S(2)}) collective-permute-start(s16[144,1536]{1,0:T(8,128)(2,1)S(1)} %get-tuple-element.41), channel_id=1, source_target_pairs={{0,3},{1,2},{2,1},{3,0},{4,7},{5,6},{6,5},{7,4},{8,11},{9,10},{10,... | collective-permute-start | bytes 1327112 | tf_op jit(solution)/shard_map/ppermute | solution.py:37

commit v3 on v2

v3 whole, which is shorter than its diff:
```python
import functools

import jax
import jax.numpy as jnp
from jax import lax
from jax.experimental import pallas as pl
from jax.experimental.pallas import tpu as pltpu
from jax.sharding import PartitionSpec as P

BOTH = ("blk", "occ")
BLOCKS = 32
RUN = 128
OCT = 8
G = 128
PAD = 16
LEVELS = 32000.0
STEPS = 256.0
MANY = 8
LABELS = 8
SLOTS = 160
MIB = 1024 * 1024
ANY = pl.BlockSpec(memory_space=pl.ANY)
IN_VMEM = pl.BlockSpec(memory_space=pltpu.VMEM)
IN_HBM = pl.BlockSpec(memory_space=pltpu.HBM)
IN_SMEM = pl.BlockSpec(memory_space=pltpu.SMEM)
TOKEN = jax.ShapeDtypeStruct((8,), jnp.int32)


def routes(where):
    pairs = []
    for blk in range(BLOCKS):
        for occ in range(4):
            to_blk, to_occ = where(blk, occ)
            pairs.append((blk * 4 + occ, (to_blk % BLOCKS) * 4 + to_occ))
    return pairs


def send(value, where):
    return lax.ppermute(value, BOTH, routes(where))


def place():
    k = lax.axis_index("blk")
    return k, lax.axis_index("occ"), lax.rem(k, 2)


def later(g, d):
    return lax.rem(g, 2) if d == 1 else lax.div(g, 2)


def side(g, zh, d):
    return later(g, d) if d == 1 else lax.rem(later(g, d) + zh, 2)


def apart(g, d):
    low, high = lax.rem(g, 2), lax.div(g, 2)
    low = 1 - low if d & 1 else low
    high = 1 - high if d & 2 else high
    return high * 2 + low


def encode(value, out_ref):
    rows = value.shape[0]
    most = jnp.max(jnp.abs(value), axis=0, keepdims=True)
    code = jnp.ceil(jnp.log2(jnp.maximum(most, 2.0**-120)) * STEPS)
    up = jnp.exp2(code * (-1.0 / STEPS)) * LEVELS
    coded = jnp.clip(jnp.round(value * up), -32767.0, 32767.0)
    out_ref[:rows, :] = coded.astype(jnp.int32).astype(jnp.int16)
    scale = jnp.broadcast_to(code.astype(jnp.int32), (PAD, value.shape[1]))
    out_ref[rows:, :] = scale.astype(jnp.int16)


def scales(ref):
    code = ref[ref.shape[0] - PAD :, :].astype(jnp.int32).astype(jnp.float32)[:1]
    return jnp.exp2(code * (1.0 / STEPS)) * (1.0 / LEVELS)


def codes(ref):
    return ref[: ref.shape[0] - PAD, :].astype(jnp.int32)


def decode(ref):
    return codes(ref).astype(jnp.float32) * scales(ref)


def iotas(rows, cols):
    return (
        lax.broadcasted_iota(jnp.int32, (rows, cols), 0),
        lax.broadcasted_iota(jnp.int32, (rows, cols), 1),
    )


def ones_at(where):
    return where.astype(jnp.float32).astype(jnp.bfloat16)


def flip_matrix(octet_flip):
    row, col = iotas(G, G)
    a, x, y = row >> 6, (row >> 3) & 7, row & 7
    return ones_at(col == (((a ^ octet_flip) << 6) | (y << 3) | x))


def own_pairs(cols):
    row, col = iotas(G, cols)
    q = row - 64
    octet, d, x = q >> 5, ((q >> 3) & 3) + 1, q & 7
    low = row < 64
    i = jnp.where(low, row >> 3, octet * 8 + x)
    j = jnp.where(low, 8 + (row & 7), octet * 8 + ((x + d) & 7))
    return i, j, col


def dot(a, b):
    return jnp.dot(a, b, preferred_element_type=jnp.float32)


def thirds(value):
    high = value.astype(jnp.bfloat16)
    rest = value - high.astype(jnp.float32)
    middle = rest.astype(jnp.bfloat16)
    low = (rest - middle.astype(jnp.float32)).astype(jnp.bfloat16)
    return jnp.concatenate([high, middle, low], axis=0)


def thrice(matrix):
    return jnp.concatenate([matrix, matrix, matrix], axis=1)


def slab(t_ref, group):
    return t_ref.at[:, pl.ds(pl.multiple_of(group * 16, 16), 16), :]


def half(both, s):
    parts = []
    for a in range(2):
        for x in range(OCT):
            one = both[a * OCT + x].astype(jnp.float32)
            parts.append(jnp.where((a ^ s) == 0, one[:OCT], one[OCT:]))
    return jnp.concatenate(parts, axis=0).astype(jnp.bfloat16)


def split_kernel(go, stay, own, t_ref, _, *refs):
    outs, (buf, sems) = refs[:-2], refs[-2:]
    _, g, zh = place()
    ds = sorted({*go, *stay}, reverse=True) + [0] * own
    loads = [pltpu.make_async_copy(slab(t_ref, apart(g, d) if d else g), buf.at[at], sems.at[at]) for at, d in enumerate(ds)]
    for load in loads:
        load.start()
    for load in loads:
        load.wait()
    for at, d in enumerate(go):
        outs[at][...] = half(buf[ds.index(d)], 1 - side(g, zh, d))
    for at, d in enumerate(stay):
        outs[len(go) + at][...] = half(buf[ds.index(d)], side(g, zh, d))
    if own:
        outs[-1][...] = buf[len(ds) - 1].reshape(256, buf.shape[3])


def plan_kernel(lab, todo, begins):
    k, _, _ = place()
    runs = lab.shape[0] // BLOCKS
    rows = [lab[k * runs + r] for r in range(runs)]
    for label in range(LABELS + 1):
        begins[label] = sum((row < label).astype(jnp.int32) for row in rows)
    for s in range(3):
        block = lax.rem(k + s, BLOCKS)
        base = 8 + s * SLOTS

        def column(c, count, block=block, base=base):
            label = lab[block * runs + c]

            def one(r, count):
                todo[base + count] = c * 256 + r * 16 + c
                return count + 1

            return lax.fori_loop(begins[label], begins[label + 1], one, count)

        count = lax.fori_loop(0, runs, column, jnp.int32(0))
        todo[s] = count

        def fill(at, carry, base=base, count=count):
            todo[base + at] = runs * 256 + lax.rem(todo[base + count - 1], 256)
            return carry

        lax.fori_loop(count, lax.div(count + MANY - 1, MANY) * MANY, fill, 0)


def partial_kernel(groups, offsets, after, todo, *refs):
    n = len(groups)
    if n:
        sides = []
        for d in groups:
            sides.append(refs[: 1 + (d > 0)])
            refs = refs[1 + (d > 0) :]
    else:
        lhs, *refs = refs
    v_ref, _, *refs = refs
    if after:
        _, *refs = refs
    acc, parts = refs[-2], refs[-2].shape[1] // G
    outs, refs = refs[: len(offsets) * parts], refs[len(offsets) * parts :]
    if n:
        lhs, *refs = refs
    token, vbuf, acc, sems = refs
    width = v_ref.shape[0]
    runs = width // RUN
    k, g, zh = place()
    token[0] = k

    def tile(s, entry):
        r, c = lax.rem(lax.div(entry, 16), 16), lax.rem(entry, 16)
        return v_ref.at[
            pl.ds(pl.multiple_of(r * RUN, RUN), RUN), pl.ds(pl.multiple_of(s * width + c * RUN, RUN), RUN)
        ]

    for at, (s, _) in enumerate(offsets):

        def begin(e, carry, at=at, s=s):
            source = tile(s, todo[8 + s * SLOTS + e])
            pltpu.make_async_copy(source, vbuf.at[at, e], sems.at[at]).start()
            return carry

        lax.fori_loop(0, todo[s], begin, 0)

    acc[...] = jnp.zeros_like(acc)
    for at, d in enumerate(groups):
        if d:
            s = side(g, zh, d)
            x, y = sides[at][0][...], sides[at][1][...]
            if d >= 2:
                x, y = jnp.where(zh == 1, y, x), jnp.where(zh == 1, x, y)
            y = -dot(flip_matrix(s), y)
        else:
            own = sides[at][0][...]
            i, j, col = own_pairs(256)
            x = dot(ones_at(col == i * 16 + j), own).astype(jnp.bfloat16)
            y = -dot(ones_at(col == j * 16 + i), own)
        y = y.astype(jnp.bfloat16)
        for r in range(runs):
            lhs[at * G : (at + 1) * G, 2 * r * RUN : (2 * r + 1) * RUN] = x[:, r * RUN : (r + 1) * RUN]
            lhs[at * G : (at + 1) * G, (2 * r + 1) * RUN : (2 * r + 2) * RUN] = y[:, r * RUN : (r + 1) * RUN]

    for at, (s, coded) in enumerate(offsets):

        def arrived(e, carry, at=at, s=s):
            pltpu.make_async_copy(tile(s, 0), vbuf.at[at, e], sems.at[at]).wait()
            return carry

        lax.fori_loop(0, todo[s], arrived, 0)

        def several(step, carry, at=at, s=s):
            products = []
            for u in range(MANY):
                e = step * MANY + u
                entry = todo[8 + s * SLOTS + e]
                c, r = lax.div(entry, 256), lax.rem(lax.div(entry, 16), 16)
                right = vbuf[at, jnp.minimum(e, todo[s] - 1)]
                left = lhs[:, pl.ds(pl.multiple_of(r * 2 * RUN, 2 * RUN), 2 * RUN)]
                products.append((c, dot(left, jnp.concatenate([right, right], axis=0))))
            for c, value in products:
                acc[at, :, pl.ds(pl.multiple_of(c * RUN, RUN), RUN)] += value
            return carry

        lax.fori_loop(0, lax.div(todo[s] + MANY - 1, MANY), several, 0)
        for part in range(parts):
            value = acc[at, part * G : (part + 1) * G, :width]
            if coded:
                encode(value, outs[at * parts + part])
            else:
                outs[at * parts + part][...] = value


def fetch(pairs, sems):
    copies = [pltpu.make_async_copy(a, b, sems.at[at]) for at, (a, b) in enumerate(pairs)]
    for copy in copies:
        copy.start()
    for copy in copies:
        copy.wait()


def merge_kernel(plus, mine_ref, got_ref, out_ref, buf, sems):
    fetch([(got_ref, buf)], sems)
    _, _, zh = place()
    mine = decode(mine_ref) if plus else mine_ref[...]
    encode(mine + jnp.where(zh == 0, decode(buf), 0.0), out_ref)


def finish_kernel(d, mine_ref, one_ref, two_ref, energy_ref, occ_ref, *refs):
    if d == 1:
        _, *refs = refs
    value_ref, *code_ref, one, two, sems = refs
    fetch([(one_ref, one), (two_ref, two)], sems)
    _, g, zh = place()
    if d:
        s = side(g, zh, d)
        row, col = iotas(G, 64)
        a, x, y = row >> 6, (row >> 3) & 7, row & 7
        p = apart(g, d)
        first, second = (g, p) if d == 1 else (jnp.where(zh == 1, p, g), jnp.where(zh == 1, g, p))
        i, j = a * OCT + x + first * 16, (a ^ s) * OCT + y + second * 16
    else:
        i, j, col = own_pairs(64)
        i, j = i + g * 16, j + g * 16
    pick = (col == i).astype(jnp.float32) + (col == j).astype(jnp.float32)
    sums = dot(thrice(pick.astype(jnp.bfloat16)), thirds(occ_ref[...]))[:, :1]
    first = decode(one)
    if d != 1:
        first = jnp.where(zh == 1, first, 0.0)
    value = (mine_ref[...] + first + decode(two)) / (energy_ref[...] - sums)
    value_ref[...] = value
    if d:
        encode(value, code_ref[0])


def put(out_ref, buf, value, d, w, turned, g, sems, at):
    p = apart(g, d)
    copies = []
    buf[at] = value.reshape(2, OCT, OCT, value.shape[1])
    for a in range(2):
        o = p * 2 + lax.rem(a + w + turned, 2)
        copy = pltpu.make_async_copy(
            buf.at[at, a],
            out_ref.at[a * OCT : (a + 1) * OCT, pl.ds(pl.multiple_of(o * OCT, OCT), OCT), :],
            sems.at[at, a],
        )
        copy.start()
        copies.append(copy)
    return copies


def returned(ref, d, w, zh):
    code = codes(ref)
    pieces = jnp.concatenate(
        [(code >> 8).astype(jnp.float32).astype(jnp.bfloat16), (code & 255).astype(jnp.float32).astype(jnp.bfloat16)]
    )
    flip = flip_matrix(1 - w).astype(jnp.float32)
    turned = dot(jnp.concatenate([flip * -256.0, -flip], axis=1).astype(jnp.bfloat16), pieces)
    if d == 1:
        return turned * scales(ref), 1
    return jnp.where(zh == 1, code.astype(jnp.float32), turned) * scales(ref), 1 - zh


def own_kernel(square_ref, near_ref, second_ref, third_ref, got1_ref, out_ref, got1, square, buf, sems, load_sems):
    load = pltpu.make_async_copy(got1_ref, got1, load_sems.at[0])
    load.start()
    _, g, zh = place()
    copies = []
    for at, (d, mine) in enumerate(((2, second_ref[...]), (3, third_ref[...]), (1, near_ref[...]))):
        w = later(g, d)
        if d == 1:
            copies += put(out_ref, buf, mine, d, w, 0, g, sems, at)
        else:
            turned = -dot(thrice(flip_matrix(1 - w)), thirds(mine))
            copies += put(out_ref, buf, jnp.where(zh == 1, turned, mine), d, w, zh, g, sems, at)
    row, col = iotas(256, G)
    i, j = row >> 4, row & 15
    oi, oj, xi, xj = i >> 3, j >> 3, i & 7, j & 7
    gap = (xj - xi) & 7
    up = 64 + oi * 32 + (gap - 1) * 8 + xi
    down = 64 + oi * 32 + (7 - gap) * 8 + xj
    same = oi == oj
    plus = jnp.where(same, jnp.where((gap >= 1) & (gap <= 4), up, -1), jnp.where(oi < oj, xi * 8 + xj, -1))
    minus = jnp.where(same, jnp.where(gap >= 5, down, -1), jnp.where(oi > oj, xj * 8 + xi, -1))
    pick = (col == plus).astype(jnp.float32) - (col == minus).astype(jnp.float32)
    square[...] = dot(thrice(pick.astype(jnp.bfloat16)), thirds(square_ref[...])).reshape(square.shape)
    copy = pltpu.make_async_copy(square, slab(out_ref, g), load_sems.at[1])
    copy.start()
    copies.append(copy)
    load.wait()
    w = later(g, 1)
    value, turned = returned(got1, 1, w, zh)
    copies += put(out_ref, buf, value, 1, w, turned, g, sems, 3)
    for copy in copies:
        copy.wait()


def back_kernel(d, got_ref, _, out_ref, got, buf, sems, load_sems):
    fetch([(got_ref, got)], load_sems)
    _, g, zh = place()
    w = later(g, d)
    value, turned = returned(got, d, w, zh)
    for copy in put(out_ref, buf, value, d, w, turned, g, sems, 0):
        copy.wait()


def call(kernel, name, outs, args, in_specs, out_specs, scratch=(), aliases={}, room=12):
    return pl.pallas_call(
        kernel,
        out_shape=outs,
        in_specs=in_specs,
        out_specs=out_specs,
        scratch_shapes=scratch,
        input_output_aliases=aliases,
        compiler_params=pltpu.CompilerParams(vmem_limit_bytes=room * MIB),
        cost_estimate=pl.CostEstimate(flops=0, bytes_accessed=0, transcendentals=0),
        name=name,
    )(*args)


def plain(rows, width):
    return jax.ShapeDtypeStruct((rows, width), jnp.float32)


def coded(rows, width):
    return jax.ShapeDtypeStruct((rows + PAD, width), jnp.int16)


def partials(name, groups, offsets, todo, rows, integrals, token, sides, after=None):
    width = integrals.shape[0]
    outs = [coded(G, width) if as_code else plain(G, width) for _, as_code in offsets for _ in range(rows // G)]
    if groups:
        outs.append(jax.ShapeDtypeStruct((rows, 2 * width), jnp.bfloat16))
    args = (todo, *sides, integrals, token)
    specs = [IN_SMEM] + [IN_VMEM] * len(sides) + [IN_HBM, IN_SMEM]
    if after is not None:
        args, specs = (*args, after), [*specs, ANY]
    return call(
        functools.partial(partial_kernel, groups, offsets, after is not None),
        name,
        outs + [TOKEN],
        args,
        specs,
        [IN_VMEM] * len(outs) + [IN_SMEM],
        [
            pltpu.VMEM((len(offsets), 144, RUN, RUN), jnp.bfloat16),
            pltpu.VMEM((len(offsets), rows, width + RUN), jnp.float32),
            pltpu.SemaphoreType.DMA((len(offsets),)),
        ],
        room=50,
    )


def per_device(amplitudes, integrals, pair_irrep, pair_energy, occ_energy):
    i_local, nocc, width = amplitudes.shape
    labels = pair_irrep.reshape(-1, RUN)[:, 0]
    energy = pair_energy.reshape(1, width)
    occ = jnp.broadcast_to(occ_energy[:, None], (nocc, RUN))

    def split(name, go, stay, own, token):
        slabs = len({*go, *stay}) + own
        outs = [jax.ShapeDtypeStruct((G, width), jnp.bfloat16)] * (len(go) + len(stay))
        if own:
            outs.append(jax.ShapeDtypeStruct((256, width), jnp.bfloat16))
        return call(
            functools.partial(split_kernel, go, stay, own),
            name,
            outs,
            (amplitudes, token),
            [IN_HBM, IN_SMEM],
            [IN_VMEM] * len(outs),
            [pltpu.VMEM((slabs, 16, 16, width), jnp.bfloat16), pltpu.SemaphoreType.DMA((slabs,))],
        )

    go2, go3, go1 = split("give", (2, 3, 1), (), False, jnp.zeros((8,), jnp.int32))
    got3 = send(go3, lambda b, o: (b, o ^ 3))
    got2 = send(go2, lambda b, o: (b, o ^ 2))
    got1 = send(go1, lambda b, o: (b, o ^ 1))
    (todo,) = call(
        plan_kernel,
        "plan",
        [jax.ShapeDtypeStruct((8 + 3 * SLOTS,), jnp.int32)],
        (labels,),
        [IN_SMEM],
        [IN_SMEM],
        [pltpu.SMEM((16,), jnp.int32)],
    )
    stay1, stay2, stay3, own = split("keep", (), (1, 2, 3), True, todo)

    square1, near1, square2, near2, near_rows, token = partials(
        "near", (0, 1), ((1, 1), (2, 1)), todo, 2 * G, integrals, todo, (own, stay1, got1)
    )
    near1 = send(near1, lambda b, o: (b + 1, o))
    near2 = send(near2, lambda b, o: (b + 2, o))
    square1 = send(send(square1, lambda b, o: (b, o ^ 2)), lambda b, o: (b ^ 1, o ^ 2))
    far = {}
    for d, stay, got in ((2, stay2, got2), (3, stay3, got3)):
        far1, rows, token = partials("far%d" % d, (d,), ((1, 1),), todo, G, integrals, token, (stay, got))
        far[d] = send(far1, lambda b, o, d=d: (b ^ 1, o ^ d)), rows
    base = {}
    for d in (2, 3):
        far2, far0, token = partials(
            "rest%d" % d, (), ((2, 0), (0, 0)), todo, G, integrals, token, (far[d][1],), None
        )
        base[d] = far0, far2
    square0, near0, token = partials("near0", (), ((0, 0),), todo, 2 * G, integrals, token, (near_rows,))

    onward = {}
    for d in (2, 3):
        far1, _ = far[d]
        (far2,) = call(
            functools.partial(merge_kernel, False),
            "merge%d" % d,
            [coded(G, width)],
            (base[d][1], far1),
            [IN_VMEM, ANY],
            [IN_VMEM],
            [pltpu.VMEM((G + PAD, width), jnp.int16), pltpu.SemaphoreType.DMA((1,))],
        )
        onward[d] = send(far2, lambda b, o: (b + 2, o))

    (square2,) = call(
        functools.partial(merge_kernel, True),
        "merge0",
        [coded(G, width)],
        (square2, square1),
        [IN_VMEM, ANY],
        [IN_VMEM],
        [pltpu.VMEM((G + PAD, width), jnp.int16), pltpu.SemaphoreType.DMA((1,))],
    )
    square2 = send(square2, lambda b, o: (b + 2, o))

    def finish(d, mine, one, two, *after):
        return call(
            functools.partial(finish_kernel, d),
            "finish%d" % d,
            [plain(G, width)] + [coded(G, width)] * (d > 0),
            (mine, one, two, energy, occ, *after),
            [IN_VMEM, ANY, ANY, IN_VMEM, IN_VMEM] + [ANY] * len(after),
            [IN_VMEM] * (1 + (d > 0)),
            [
                pltpu.VMEM((G + PAD, width), jnp.int16),
                pltpu.VMEM((G + PAD, width), jnp.int16),
                pltpu.SemaphoreType.DMA((2,)),
            ],
        )

    done, back = {}, {}
    for d in (2, 3):
        done[d], code = finish(d, base[d][0], far[d][0], onward[d])
        back[d] = send(code, lambda b, o, d=d: (b, o ^ d))
    (square,) = finish(0, square0, square1, square2)
    near, code = finish(1, near0, near1, near2, near0)
    back1 = send(code, lambda b, o: (b, o ^ 1))

    out = jax.ShapeDtypeStruct((i_local, nocc, width), jnp.float32)
    landed = pltpu.VMEM((G + PAD, width), jnp.int16)
    (whole,) = call(
        own_kernel,
        "own",
        [out],
        (square, near, done[2], done[3], back1),
        [IN_VMEM, IN_VMEM, IN_VMEM, IN_VMEM, ANY],
        [ANY],
        [
            landed,
            pltpu.VMEM((16, 16, width), jnp.float32),
            pltpu.VMEM((4, 2, OCT, OCT, width), jnp.float32),
            pltpu.SemaphoreType.DMA((4, 2)),
            pltpu.SemaphoreType.DMA((2,)),
        ],
        room=24,
    )
    for d in (2, 3):
        (whole,) = call(
            functools.partial(back_kernel, d),
            "back%d" % d,
            [out],
            (back[d], whole),
            [ANY, ANY],
            [ANY],
            [
                landed,
                pltpu.VMEM((1, 2, OCT, OCT, width), jnp.float32),
                pltpu.SemaphoreType.DMA((1, 2)),
                pltpu.SemaphoreType.DMA((1,)),
            ],
                aliases={1: 0},
        )
    return whole


def solution(mesh):
    placed = (P("occ", None, "blk"), P("blk", None), P(), P("blk"), P())
    return jax.shard_map(
        per_device, mesh=mesh, in_specs=placed, out_specs=P("occ", None, "blk"), check_vma=False
    )
```

time: 107 us -> 93.3 us (0.87)
  the two profiles are of different devices: /device:TPU:64 before, /device:TPU:1 now
where the time goes in v3:
time: 93.3 us; the launch traced here: 92.8 us
  Pallas kernels  42.8 us (46%)
  waiting for transfers between devices  22.8 us (24%)
  starting transfers between devices  21.9 us (23%)
  local copies, waits for them, and re-layouts  4.93 us (5%)
    pallas_call x19, Pallas kernels, call(): pl.pallas_call(kernel, out_shape=outs, in_specs=in_specs, out_specs=out_s...  42.8 us
    ppermute x15, waiting for transfers between devices, send(): return lax.ppermute(value, BOTH, routes(where))  22.8 us
    ppermute x15, starting transfers between devices, send(): return lax.ppermute(value, BOTH, routes(where))  21.9 us
    unnamed x10, local copies, waits for them, and re-layouts  3.79 us
  transfers between devices with their start and end apart: 15, of which 6 were waited for; matrix products, arithmetic and copies ran while one was open for 1% of the time, Pallas kernels for 43%

profile of v3, /device:TPU:1, one launch (start us, length us, event | category | flops | bytes accessed | tf_op | source)
XLA Modules:
  0.0 92.8 jit_solution(7320552749850274961)
XLA Ops:
  0.0 0.0 copy-start
  0.0 1.9 %copy-done = bf16[16,64,1536]{2,1,0:T(8,128)(2,1)S(1)} copy-done((bf16[16,64,1536]{2,1,0:T(8,128)(2,1)S(1)}, bf16[16,64,1536]{2,1,0:T(8,128)(2,1)}, u32[]{:S(2)}) %copy-start) | copy-done | bytes 3145752
  1.9 1.0 %give.1 = (bf16[128,1536]{1,0:T(8,128)(2,1)S(1)}, bf16[128,1536]{1,0:T(8,128)(2,1)S(1)}, bf16[128,1536]{1,0:T(8,128)(2,1)S(1)}) custom-call(bf16[16,64,1536]{2,1,0:T(8,128)(2,1)S(1)} %copy-done, s32[8]{0:T(128)S(1)} %broadcast_1__.2._), custom_call_target="tpu_custom_call" | custom-call | tf_op jit(solution)/shard_map/give/pallas_call | solution.py:387
  2.9 1.5 %collective-permute-start.2 = (bf16[128,1536]{1,0:T(8,128)(2,1)S(1)}, bf16[128,1536]{1,0:T(8,128)(2,1)S(1)}, u32[]{:S(2)}, u32[]{:S(2)}) collective-permute-start(bf16[128,1536]{1,0:T(8,128)(2,1)S(1)} %get-tuple-element.44), channel_id=1, source_target_pairs={{0,1},{1,0},{2,3},{3,2},{4,5},{5,4},{6,7},{7,6},{8,9},{9,8},{10,11... | collective-permute-start | bytes 1179656 | tf_op jit(solution)/shard_map/ppermute | solution.py:39
  4.4 1.7 %collective-permute-start.1 = (bf16[128,1536]{1,0:T(8,128)(2,1)S(1)}, bf16[128,1536]{1,0:T(8,128)(2,1)S(1)}, u32[]{:S(2)}, u32[]{:S(2)}) collective-permute-start(bf16[128,1536]{1,0:T(8,128)(2,1)S(1)} %get-tuple-element.41), channel_id=1, source_target_pairs={{0,2},{1,3},{2,0},{3,1},{4,6},{5,7},{6,4},{7,5},{8,10},{9,11},{10,... | collective-permute-start | bytes 1179656 | tf_op jit(solution)/shard_map/ppermute | solution.py:39
  6.2 0.1 collective-permute-start
  6.2 1.1 %slice_reduce_fusion.lab = s32[384]{0:T(512)S(1)} fusion(s32[384,128]{1,0:T(8,128)} %bitcast.1), kind=kLoop, calls=%fused_computation | loop fusion | bytes 3072 | tf_op jit(solution)/shard_map/slice | solution.py:435
  7.3 2.4 %plan.1._.todo.refs_4_ = s32[488]{0:T(512)S(1)} custom-call(s32[384]{0:T(512)S(1)} %slice_reduce_fusion.lab), custom_call_target="tpu_custom_call" | custom-call | tf_op jit(solution)/shard_map/plan/pallas_call | solution.py:387
  9.7 0.0 copy-start.1
  9.7 1.9 %copy-done.1 = bf16[16,64,1536]{2,1,0:T(8,128)(2,1)S(1)} copy-done((bf16[16,64,1536]{2,1,0:T(8,128)(2,1)S(1)}, bf16[16,64,1536]{2,1,0:T(8,128)(2,1)}, u32[]{:S(2)}) %copy-start.1) | copy-done | bytes 3145752
  11.6 1.1 %keep.1 = (bf16[128,1536]{1,0:T(8,128)(2,1)S(1)}, bf16[128,1536]{1,0:T(8,128)(2,1)S(1)}, bf16[128,1536]{1,0:T(8,128)(2,1)S(1)}, bf16[256,1536]{1,0:T(8,128)(2,1)S(1)}) custom-call(bf16[16,64,1536]{2,1,0:T(8,128)(2,1)S(1)} %copy-done.1, s32[488]{0:T(512)S(1)} %plan.1._.todo.refs_4_), custom_call_target="tpu_custom_call" | custom-call | tf_op jit(solution)/shard_map/keep/pallas_call | solution.py:387
  12.8 0.0 collective-permute-done.2.refs_2_
  12.8 6.4 %near.1 = (s16[144,1536]{1,0:T(8,128)(2,1)S(1)}, s16[144,1536]{1,0:T(8,128)(2,1)S(1)}, s16[144,1536]{1,0:T(8,128)(2,1)S(1)}, s16[144,1536]{1,0:T(8,128)(2,1)S(1)...) custom-call(s32[488]{0:T(512)S(1)} %plan.1._.todo.refs_4_, bf16[256,1536]{1,0:T(8,128)(2,1)S(1)} %get-tuple-element.42.refs_0_, ...), custom_call_target="tpu_custom_call" | custom-call | tf_op jit(solution)/shard_map/near/pallas_call | solution.py:387
  19.2 1.7 %collective-permute-start.9 = (s16[144,1536]{1,0:T(8,128)(2,1)S(1)}, s16[144,1536]{1,0:T(8,128)(2,1)S(1)}, u32[]{:S(2)}, u32[]{:S(2)}) collective-permute-start(s16[144,1536]{1,0:T(8,128)(2,1)S(1)} %get-tuple-element.62), channel_id=1, source_target_pairs={{0,2},{1,3},{2,0},{3,1},{4,6},{5,7},{6,4},{7,5},{8,10},{9,11},{10,... | collective-permute-start | bytes 1327112 | tf_op jit(solution)/shard_map/ppermute | solution.py:39
  20.9 0.0 collective-permute-done.1.refs_1_
  20.9 3.2 %far2.1 = (s16[144,1536]{1,0:T(8,128)(2,1)S(1)}, bf16[128,3072]{1,0:T(8,128)(2,1)S(1)}, s32[8]{0:T(128)S(1)}) custom-call(s32[488]{0:T(512)S(1)} %plan.1._.todo.refs_4_, bf16[128,1536]{1,0:T(8,128)(2,1)S(1)} %get-tuple-element.40.refs_0_, bf16[128,1536]{1,0:T(8,128)(2,1)S(1)} %collective-permute-done.1.refs_1_, bf16[1536,4608]{1,0:T(8,128)(2,1)} %refs_1_.5, ...), custom_call_target="tpu_custom_call" | custom-call | tf_op jit(solution)/shard_map/far2/pallas_call | solution.py:387
  24.2 0.8 collective-permute-start.6
  24.9 0.0 collective-permute-done.refs_1_
  24.9 3.2 %far3.1 = (s16[144,1536]{1,0:T(8,128)(2,1)S(1)}, bf16[128,3072]{1,0:T(8,128)(2,1)S(1)}, s32[8]{0:T(128)S(1)}) custom-call(s32[488]{0:T(512)S(1)} %plan.1._.todo.refs_4_, bf16[128,1536]{1,0:T(8,128)(2,1)S(1)} %get-tuple-element.38.refs_0_, bf16[128,1536]{1,0:T(8,128)(2,1)S(1)} %collective-permute-done.refs_1_, bf16[1536,4608]{1,0:T(8,128)(2,1)} %refs_1_.5, ...), custom_call_target="tpu_custom_call" | custom-call | tf_op jit(solution)/shard_map/far3/pallas_call | solution.py:387
  28.2 2.4 %collective-permute-start.3 = (s16[144,1536]{1,0:T(8,128)(2,1)S(1)}, s16[144,1536]{1,0:T(8,128)(2,1)S(1)}, u32[]{:S(2)}, u32[]{:S(2)}) collective-permute-start(s16[144,1536]{1,0:T(8,128)(2,1)S(1)} %get-tuple-element.52), channel_id=1, source_target_pairs={{0,7},{1,6},{2,5},{3,4},{4,3},{5,2},{6,1},{7,0},{8,15},{9,14},{10,... | collective-permute-start | bytes 1327112 | tf_op jit(solution)/shard_map/ppermute | solution.py:39
  30.6 0.8 collective-permute-start.12
  31.4 1.1 %collective-permute-start.13 = (s16[144,1536]{1,0:T(8,128)(2,1)S(1)}, s16[144,1536]{1,0:T(8,128)(2,1)S(1)}, u32[]{:S(2)}, u32[]{:S(2)}) collective-permute-start(s16[144,1536]{1,0:T(8,128)(2,1)S(1)} %get-tuple-element.66), channel_id=1, source_target_pairs={{0,8},{1,9},{2,10},{3,11},{4,12},{5,13},{6,14},{7,15},{8,16},{9,17... | collective-permute-start | bytes 1327112 | tf_op jit(solution)/shard_map/ppermute | solution.py:39
  32.5 4.3 %rest2.1 = (f32[128,1536]{1,0:T(8,128)S(1)}, f32[128,1536]{1,0:T(8,128)S(1)}, s32[8]{0:T(128)S(1)}) custom-call(s32[488]{0:T(512)S(1)} %plan.1._.todo.refs_4_, bf16[128,3072]{1,0:T(8,128)(2,1)S(1)} %get-tuple-element.48.refs_0_, bf16[1536,4608]{1,0:T(8,128)(2,1)} %refs_1_.5, s32[8]{0:T(128)S(1)} %get-tuple-element.49.refs_2_), custom_call_target="tpu_custom_call" | custom-call | tf_op jit(solution)/shard_map/rest2/pallas_call | solution.py:387
  36.8 0.0 collective-permute-done.9
  36.8 3.5 %collective-permute-start.10 = (s16[144,1536]{1,0:T(8,128)(2,1)S(1)}, s16[144,1536]{1,0:T(8,128)(2,1)S(1)}, u32[]{:S(2)}, u32[]{:S(2)}) collective-permute-start(s16[144,1536]{1,0:T(8,128)(2,1)S(1)} %collective-permute-done.9), channel_id=1, source_target_pairs={{0,6},{1,7},{2,4},{3,5},{4,2},{5,3},{6,0},{7,1},{8,14},{9,15},{10,... | collective-permute-start | bytes 1327112 | tf_op jit(solution)/shard_map/ppermute | solution.py:39
  40.3 3.0 %collective-permute-done.6.got_ref.one_ref = s16[144,1536]{1,0:T(8,128)(2,1)S(1)} collective-permute-done((s16[144,1536]{1,0:T(8,128)(2,1)S(1)}, s16[144,1536]{1,0:T(8,128)(2,1)S(1)}, u32[]{:S(2)}, u32[]{:S(2)}) %collective-permute-start.6) | collective-permute-done | bytes 442400 | tf_op jit(solution)/shard_map/ppermute | solution.py:39
  43.4 0.6 merge2.1
  43.9 3.9 %collective-permute-start.7 = (s16[144,1536]{1,0:T(8,128)(2,1)S(1)}, s16[144,1536]{1,0:T(8,128)(2,1)S(1)}, u32[]{:S(2)}, u32[]{:S(2)}) collective-permute-start(s16[144,1536]{1,0:T(8,128)(2,1)S(1)} %merge2.1), channel_id=1, source_target_pairs={{0,8},{1,9},{2,10},{3,11},{4,12},{5,13},{6,14},{7,15},{8,16},{9,17... | collective-permute-start | bytes 1327112 | tf_op jit(solution)/shard_map/ppermute | solution.py:39
  47.8 0.0 copy-start.3
  47.8 0.0 copy-start.2
  47.8 4.3 %rest3.1 = (f32[128,1536]{1,0:T(8,128)S(1)}, f32[128,1536]{1,0:T(8,128)S(1)}, s32[8]{0:T(128)S(1)}) custom-call(s32[488]{0:T(512)S(1)} %plan.1._.todo.refs_4_, bf16[128,3072]{1,0:T(8,128)(2,1)S(1)} %get-tuple-element.47.refs_0_, bf16[1536,4608]{1,0:T(8,128)(2,1)} %refs_1_.5, s32[8]{0:T(128)S(1)} %get-tuple-element.50.refs_2_), custom_call_target="tpu_custom_call" | custom-call | tf_op jit(solution)/shard_map/rest3/pallas_call | solution.py:387
  52.1 5.4 %collective-permute-done.3.got_ref.one_ref = s16[144,1536]{1,0:T(8,128)(2,1)S(1)} collective-permute-done((s16[144,1536]{1,0:T(8,128)(2,1)S(1)}, s16[144,1536]{1,0:T(8,128)(2,1)S(1)}, u32[]{:S(2)}, u32[]{:S(2)}) %collective-permute-start.3) | collective-permute-done | bytes 442400 | tf_op jit(solution)/shard_map/ppermute | solution.py:39
  57.5 0.6 merge3.1
  58.1 0.4 collective-permute-start.4
  58.4 0.0 copy-done.3
  58.5 0.0 copy-done.2
  58.5 0.0 copy-start.4
  58.5 3.9 %near0.1 = (f32[128,1536]{1,0:T(8,128)S(1)}, f32[128,1536]{1,0:T(8,128)S(1)}, s32[8]{0:T(128)}) custom-call(s32[488]{0:T(512)S(1)} %plan.1._.todo.refs_4_, bf16[256,3072]{1,0:T(8,128)(2,1)S(1)} %copy-done.2, bf16[1536,4608]{1,0:T(8,128)(2,1)} %refs_1_.5, s32[8]{0:T(128)S(1)} %get-tuple-element.60.refs_2_), custom_call_target="tpu_custom_call" | custom-call | tf_op jit(solution)/shard_map/near0/pallas_call | solution.py:387
  62.4 0.0 collective-permute-done.12.one_ref
  62.4 0.0 collective-permute-done.13.two_ref
  62.4 0.0 copy-done.4
  62.4 0.1 broadcast_in_dim.2.occ_ref
  62.5 1.2 %finish1.1 = (f32[128,1536]{1,0:T(8,128)S(1)}, s16[144,1536]{1,0:T(8,128)(2,1)S(1)}) custom-call(f32[128,1536]{1,0:T(8,128)S(1)} %get-tuple-element.64.mine_ref.refs_0_, s16[144,1536]{1,0:T(8,128)(2,1)S(1)} %collective-permute-done.12.one_ref, s16[144,1536]{1,0:T(8,128)(2,1)S(1)} %collective-permute-done.13.two_ref, f32[1,1536]{1,0:T(1,128)S(1)} %reshape.8.energy_ref, ...), custom_call_target="tpu_custom_call" | custom-call | tf_op jit(solution)/shard_map/finish1/pallas_call | solution.py:387
  63.7 0.1 collective-permute-start.14
  63.8 1.4 %collective-permute-done.10.got_ref.one_ref = s16[144,1536]{1,0:T(8,128)(2,1)S(1)} collective-permute-done((s16[144,1536]{1,0:T(8,128)(2,1)S(1)}, s16[144,1536]{1,0:T(8,128)(2,1)S(1)}, u32[]{:S(2)}, u32[]{:S(2)}) %collective-permute-start.10) | collective-permute-done | bytes 442400 | tf_op jit(solution)/shard_map/ppermute | solution.py:39
  65.2 0.6 merge0.1
  65.8 2.6 %collective-permute-start.11 = (s16[144,1536]{1,0:T(8,128)(2,1)S(1)}, s16[144,1536]{1,0:T(8,128)(2,1)S(1)}, u32[]{:S(2)}, u32[]{:S(2)}) collective-permute-start(s16[144,1536]{1,0:T(8,128)(2,1)S(1)} %merge0.1), channel_id=1, source_target_pairs={{0,8},{1,9},{2,10},{3,11},{4,12},{5,13},{6,14},{7,15},{8,16},{9,17... | collective-permute-start | bytes 1327112 | tf_op jit(solution)/shard_map/ppermute | solution.py:39
  68.5 0.0 collective-permute-done.7.two_ref
  68.5 1.2 %finish2.1 = (f32[128,1536]{1,0:T(8,128)S(1)}, s16[144,1536]{1,0:T(8,128)(2,1)S(1)}) custom-call(f32[128,1536]{1,0:T(8,128)S(1)} %get-tuple-element.55.mine_ref, s16[144,1536]{1,0:T(8,128)(2,1)S(1)} %collective-permute-done.6.got_ref.one_ref, s16[144,1536]{1,0:T(8,128)(2,1)S(1)} %collective-permute-done.7.two_ref, f32[1,1536]{1,0:T(1,128)S(1)} %reshape.8.energy_ref, ...), custom_call_target="tpu_custom_call" | custom-call | tf_op jit(solution)/shard_map/finish2/pallas_call | solution.py:387
  69.7 0.8 collective-permute-start.8
  70.5 1.9 %collective-permute-done.4.two_ref = s16[144,1536]{1,0:T(8,128)(2,1)S(1)} collective-permute-done((s16[144,1536]{1,0:T(8,128)(2,1)S(1)}, s16[144,1536]{1,0:T(8,128)(2,1)S(1)}, u32[]{:S(2)}, u32[]{:S(2)}) %collective-permute-start.4) | collective-permute-done | bytes 442400 | tf_op jit(solution)/shard_map/ppermute | solution.py:39
  72.4 1.2 %finish3.1 = (f32[128,1536]{1,0:T(8,128)S(1)}, s16[144,1536]{1,0:T(8,128)(2,1)S(1)}) custom-call(f32[128,1536]{1,0:T(8,128)S(1)} %get-tuple-element.51.mine_ref, s16[144,1536]{1,0:T(8,128)(2,1)S(1)} %collective-permute-done.3.got_ref.one_ref, s16[144,1536]{1,0:T(8,128)(2,1)S(1)} %collective-permute-done.4.two_ref, f32[1,1536]{1,0:T(1,128)S(1)} %reshape.8.energy_ref, ...), custom_call_target="tpu_custom_call" | custom-call | tf_op jit(solution)/shard_map/finish3/pallas_call | solution.py:387
  73.6 0.5 collective-permute-start.5
  74.1 7.1 %collective-permute-done.11.two_ref = s16[144,1536]{1,0:T(8,128)(2,1)S(1)} collective-permute-done((s16[144,1536]{1,0:T(8,128)(2,1)S(1)}, s16[144,1536]{1,0:T(8,128)(2,1)S(1)}, u32[]{:S(2)}, u32[]{:S(2)}) %collective-permute-start.11) | collective-permute-done | bytes 442400 | tf_op jit(solution)/shard_map/ppermute | solution.py:39
  81.1 1.0 %finish0.1.square_ref = f32[128,1536]{1,0:T(8,128)S(1)} custom-call(f32[128,1536]{1,0:T(8,128)S(1)} %get-tuple-element.61.mine_ref, s16[144,1536]{1,0:T(8,128)(2,1)S(1)} %collective-permute-done.10.got_ref.one_ref, s16[144,1536]{1,0:T(8,128)(2,1)S(1)} %collective-permute-done.11.two_ref, f32[1,1536]{1,0:T(1,128)S(1)} %reshape.8.energy_ref, ...), custom_call_target="tpu_custom_call" | custom-call | tf_op jit(solution)/shard_map/finish0/pallas_call | solution.py:387
  82.2 0.0 collective-permute-done.14.got1_ref
  82.2 3.4 %own.1._ = f32[16,64,1536]{2,1,0:T(8,128)} custom-call(f32[128,1536]{1,0:T(8,128)S(1)} %finish0.1.square_ref, f32[128,1536]{1,0:T(8,128)S(1)} %get-tuple-element.67.near_ref, f32[128,1536]{1,0:T(8,128)S(1)} %get-tuple-element.68.second_ref, f32[128,1536]{1,0:T(8,128)S(1)} %get-tuple-element.69.third_ref, s16[144,1536]{1,0:T(8,128)(2,1)S(1)} %collective-permute-done.14.got1_ref), custom_call_target="tpu_custom_call" | custom-call | tf_op jit(solution)/shard_map/own/pallas_call | solution.py:387
  85.6 0.0 collective-permute-done.8.got_ref
  85.6 1.5 %back2.1._ = f32[16,64,1536]{2,1,0:T(8,128)} custom-call(s16[144,1536]{1,0:T(8,128)(2,1)S(1)} %collective-permute-done.8.got_ref, f32[16,64,1536]{2,1,0:T(8,128)} %own.1._), custom_call_target="tpu_custom_call", output_to_operand_aliasing={{}: (1, {})} | custom-call | tf_op jit(solution)/shard_map/back2/pallas_call | solution.py:387
  87.1 4.0 %collective-permute-done.5.got_ref = s16[144,1536]{1,0:T(8,128)(2,1)S(1)} collective-permute-done((s16[144,1536]{1,0:T(8,128)(2,1)S(1)}, s16[144,1536]{1,0:T(8,128)(2,1)S(1)}, u32[]{:S(2)}, u32[]{:S(2)}) %collective-permute-start.5) | collective-permute-done | bytes 442400 | tf_op jit(solution)/shard_map/ppermute | solution.py:39
  91.1 1.5 %back3.1 = f32[16,64,1536]{2,1,0:T(8,128)} custom-call(s16[144,1536]{1,0:T(8,128)(2,1)S(1)} %collective-permute-done.5.got_ref, f32[16,64,1536]{2,1,0:T(8,128)} %back2.1._), custom_call_target="tpu_custom_call", output_to_operand_aliasing={{}: (1, {})} | custom-call | tf_op jit(solution)/shard_map/back3/pallas_call | solution.py:387
  (2 shorter events, 0.0 us)
Async XLA Ops:
  0.0 1.9 %copy-start = (bf16[16,64,1536]{2,1,0:T(8,128)(2,1)S(1)}, bf16[16,64,1536]{2,1,0:T(8,128)(2,1)}, u32[]{:S(2)}) copy-start(bf16[16,64,1536]{2,1,0:T(8,128)(2,1)} %t_ref.3) | copy-start | bytes 9437188
  2.9 9.8 %collective-permute-start.2 = (bf16[128,1536]{1,0:T(8,128)(2,1)S(1)}, bf16[128,1536]{1,0:T(8,128)(2,1)S(1)}, u32[]{:S(2)}, u32[]{:S(2)}) collective-permute-start(bf16[128,1536]{1,0:T(8,128)(2,1)S(1)} %get-tuple-element.44), channel_id=1, source_target_pairs={{0,1},{1,0},{2,3},{3,2},{4,5},{5,4},{6,7},{7,6},{8,9},{9,8},{10,11... | collective-permute-start | bytes 1179656 | tf_op jit(solution)/shard_map/ppermute | solution.py:39
  4.4 16.5 %collective-permute-start.1 = (bf16[128,1536]{1,0:T(8,128)(2,1)S(1)}, bf16[128,1536]{1,0:T(8,128)(2,1)S(1)}, u32[]{:S(2)}, u32[]{:S(2)}) collective-permute-start(bf16[128,1536]{1,0:T(8,128)(2,1)S(1)} %get-tuple-element.41), channel_id=1, source_target_pairs={{0,2},{1,3},{2,0},{3,1},{4,6},{5,7},{6,4},{7,5},{8,10},{9,11},{10,... | collective-permute-start | bytes 1179656 | tf_op jit(solution)/shard_map/ppermute | solution.py:39
  6.2 18.8 %collective-permute-start = (bf16[128,1536]{1,0:T(8,128)(2,1)S(1)}, bf16[128,1536]{1,0:T(8,128)(2,1)S(1)}, u32[]{:S(2)}, u32[]{:S(2)}) collective-permute-start(bf16[128,1536]{1,0:T(8,128)(2,1)S(1)} %get-tuple-element.39), channel_id=1, source_target_pairs={{0,3},{1,2},{2,1},{3,0},{4,7},{5,6},{6,5},{7,4},{8,11},{9,10},{10,... | collective-permute-start | bytes 1179656 | tf_op jit(solution)/shard_map/ppermute | solution.py:39
  9.7 1.9 %copy-start.1 = (bf16[16,64,1536]{2,1,0:T(8,128)(2,1)S(1)}, bf16[16,64,1536]{2,1,0:T(8,128)(2,1)}, u32[]{:S(2)}) copy-start(bf16[16,64,1536]{2,1,0:T(8,128)(2,1)} %t_ref.3) | copy-start | bytes 9437188
  19.2 17.6 %collective-permute-start.9 = (s16[144,1536]{1,0:T(8,128)(2,1)S(1)}, s16[144,1536]{1,0:T(8,128)(2,1)S(1)}, u32[]{:S(2)}, u32[]{:S(2)}) collective-permute-start(s16[144,1536]{1,0:T(8,128)(2,1)S(1)} %get-tuple-element.62), channel_id=1, source_target_pairs={{0,2},{1,3},{2,0},{3,1},{4,6},{5,7},{6,4},{7,5},{8,10},{9,11},{10,... | collective-permute-start | bytes 1327112 | tf_op jit(solution)/shard_map/ppermute | solution.py:39
  24.2 19.2 %collective-permute-start.6 = (s16[144,1536]{1,0:T(8,128)(2,1)S(1)}, s16[144,1536]{1,0:T(8,128)(2,1)S(1)}, u32[]{:S(2)}, u32[]{:S(2)}) collective-permute-start(s16[144,1536]{1,0:T(8,128)(2,1)S(1)} %get-tuple-element.56), channel_id=1, source_target_pairs={{0,6},{1,7},{2,4},{3,5},{4,2},{5,3},{6,0},{7,1},{8,14},{9,15},{10,... | collective-permute-start | bytes 1327112 | tf_op jit(solution)/shard_map/ppermute | solution.py:39
  28.2 29.3 %collective-permute-start.3 = (s16[144,1536]{1,0:T(8,128)(2,1)S(1)}, s16[144,1536]{1,0:T(8,128)(2,1)S(1)}, u32[]{:S(2)}, u32[]{:S(2)}) collective-permute-start(s16[144,1536]{1,0:T(8,128)(2,1)S(1)} %get-tuple-element.52), channel_id=1, source_target_pairs={{0,7},{1,6},{2,5},{3,4},{4,3},{5,2},{6,1},{7,0},{8,15},{9,14},{10,... | collective-permute-start | bytes 1327112 | tf_op jit(solution)/shard_map/ppermute | solution.py:39
  30.6 31.8 %collective-permute-start.12 = (s16[144,1536]{1,0:T(8,128)(2,1)S(1)}, s16[144,1536]{1,0:T(8,128)(2,1)S(1)}, u32[]{:S(2)}, u32[]{:S(2)}) collective-permute-start(s16[144,1536]{1,0:T(8,128)(2,1)S(1)} %get-tuple-element.65), channel_id=1, source_target_pairs={{0,4},{1,5},{2,6},{3,7},{4,8},{5,9},{6,10},{7,11},{8,12},{9,13},{1... | collective-permute-start | bytes 1327112 | tf_op jit(solution)/shard_map/ppermute | solution.py:39
  31.4 31.0 %collective-permute-start.13 = (s16[144,1536]{1,0:T(8,128)(2,1)S(1)}, s16[144,1536]{1,0:T(8,128)(2,1)S(1)}, u32[]{:S(2)}, u32[]{:S(2)}) collective-permute-start(s16[144,1536]{1,0:T(8,128)(2,1)S(1)} %get-tuple-element.66), channel_id=1, source_target_pairs={{0,8},{1,9},{2,10},{3,11},{4,12},{5,13},{6,14},{7,15},{8,16},{9,17... | collective-permute-start | bytes 1327112 | tf_op jit(solution)/shard_map/ppermute | solution.py:39
  36.8 28.4 %collective-permute-start.10 = (s16[144,1536]{1,0:T(8,128)(2,1)S(1)}, s16[144,1536]{1,0:T(8,128)(2,1)S(1)}, u32[]{:S(2)}, u32[]{:S(2)}) collective-permute-start(s16[144,1536]{1,0:T(8,128)(2,1)S(1)} %collective-permute-done.9), channel_id=1, source_target_pairs={{0,6},{1,7},{2,4},{3,5},{4,2},{5,3},{6,0},{7,1},{8,14},{9,15},{10,... | collective-permute-start | bytes 1327112 | tf_op jit(solution)/shard_map/ppermute | solution.py:39
  43.9 24.5 %collective-permute-start.7 = (s16[144,1536]{1,0:T(8,128)(2,1)S(1)}, s16[144,1536]{1,0:T(8,128)(2,1)S(1)}, u32[]{:S(2)}, u32[]{:S(2)}) collective-permute-start(s16[144,1536]{1,0:T(8,128)(2,1)S(1)} %merge2.1), channel_id=1, source_target_pairs={{0,8},{1,9},{2,10},{3,11},{4,12},{5,13},{6,14},{7,15},{8,16},{9,17... | collective-permute-start | bytes 1327112 | tf_op jit(solution)/shard_map/ppermute | solution.py:39
  47.8 10.6 %copy-start.3 = (f32[1536]{0:T(1024)S(1)}, f32[1536]{0:T(1024)}, u32[]{:S(2)}) copy-start(f32[1536]{0:T(1024)} %param.8) | copy-start | bytes 18436
  47.8 10.7 %copy-start.2 = (bf16[256,3072]{1,0:T(8,128)(2,1)S(1)}, bf16[256,3072]{1,0:T(8,128)(2,1)}, u32[]{:S(2)}) copy-start(bf16[256,3072]{1,0:T(8,128)(2,1)} %get-tuple-element.59.refs_0_) | copy-start | bytes 4718596
  58.1 14.4 %collective-permute-start.4 = (s16[144,1536]{1,0:T(8,128)(2,1)S(1)}, s16[144,1536]{1,0:T(8,128)(2,1)S(1)}, u32[]{:S(2)}, u32[]{:S(2)}) collective-permute-start(s16[144,1536]{1,0:T(8,128)(2,1)S(1)} %merge3.1), channel_id=1, source_target_pairs={{0,8},{1,9},{2,10},{3,11},{4,12},{5,13},{6,14},{7,15},{8,16},{9,17... | collective-permute-start | bytes 1327112 | tf_op jit(solution)/shard_map/ppermute | solution.py:39
  58.5 3.9 %copy-start.4 = (f32[64]{0:T(128)S(1)}, f32[64]{0:T(128)}, u32[]{:S(2)}) copy-start(f32[64]{0:T(128)} %param.9) | copy-start | bytes 772
  63.7 18.5 %collective-permute-start.14 = (s16[144,1536]{1,0:T(8,128)(2,1)S(1)}, s16[144,1536]{1,0:T(8,128)(2,1)S(1)}, u32[]{:S(2)}, u32[]{:S(2)}) collective-permute-start(s16[144,1536]{1,0:T(8,128)(2,1)S(1)} %get-tuple-element.70), channel_id=1, source_target_pairs={{0,1},{1,0},{2,3},{3,2},{4,5},{5,4},{6,7},{7,6},{8,9},{9,8},{10,11... | collective-permute-start | bytes 1327112 | tf_op jit(solution)/shard_map/ppermute | solution.py:39
  65.8 15.3 %collective-permute-start.11 = (s16[144,1536]{1,0:T(8,128)(2,1)S(1)}, s16[144,1536]{1,0:T(8,128)(2,1)S(1)}, u32[]{:S(2)}, u32[]{:S(2)}) collective-permute-start(s16[144,1536]{1,0:T(8,128)(2,1)S(1)} %merge0.1), channel_id=1, source_target_pairs={{0,8},{1,9},{2,10},{3,11},{4,12},{5,13},{6,14},{7,15},{8,16},{9,17... | collective-permute-start | bytes 1327112 | tf_op jit(solution)/shard_map/ppermute | solution.py:39
  69.7 15.9 %collective-permute-start.8 = (s16[144,1536]{1,0:T(8,128)(2,1)S(1)}, s16[144,1536]{1,0:T(8,128)(2,1)S(1)}, u32[]{:S(2)}, u32[]{:S(2)}) collective-permute-start(s16[144,1536]{1,0:T(8,128)(2,1)S(1)} %get-tuple-element.58), channel_id=1, source_target_pairs={{0,2},{1,3},{2,0},{3,1},{4,6},{5,7},{6,4},{7,5},{8,10},{9,11},{10,... | collective-permute-start | bytes 1327112 | tf_op jit(solution)/shard_map/ppermute | solution.py:39
  73.6 17.5 %collective-permute-start.5 = (s16[144,1536]{1,0:T(8,128)(2,1)S(1)}, s16[144,1536]{1,0:T(8,128)(2,1)S(1)}, u32[]{:S(2)}, u32[]{:S(2)}) collective-permute-start(s16[144,1536]{1,0:T(8,128)(2,1)S(1)} %get-tuple-element.54), channel_id=1, source_target_pairs={{0,3},{1,2},{2,1},{3,0},{4,7},{5,6},{6,5},{7,4},{8,11},{9,10},{10,... | collective-permute-start | bytes 1327112 | tf_op jit(solution)/shard_map/ppermute | solution.py:39

commit v4 on v3

--- a/solution.py
+++ b/solution.py
@@ -12,11 +12,12 @@
 RUN = 128
 OCT = 8
 G = 128
-PAD = 16
+PAD = 8
 LEVELS = 32000.0
 STEPS = 256.0
 MANY = 8
 LABELS = 8
+ORDER = (0, 2, 3)
 SLOTS = 160
 MIB = 1024 * 1024
 ANY = pl.BlockSpec(memory_space=pl.ANY)
@@ -285,11 +286,7 @@
     encode(mine + jnp.where(zh == 0, decode(buf), 0.0), out_ref)
 
 
-def finish_kernel(d, mine_ref, one_ref, two_ref, energy_ref, occ_ref, *refs):
-    if d == 1:
-        _, *refs = refs
-    value_ref, *code_ref, one, two, sems = refs
-    fetch([(one_ref, one), (two_ref, two)], sems)
+def finished(d, mine, one, two, energy, occ):
     _, g, zh = place()
     if d:
         s = side(g, zh, d)
@@ -302,14 +299,17 @@
         i, j, col = own_pairs(64)
         i, j = i + g * 16, j + g * 16
     pick = (col == i).astype(jnp.float32) + (col == j).astype(jnp.float32)
-    sums = dot(thrice(pick.astype(jnp.bfloat16)), thirds(occ_ref[...]))[:, :1]
-    first = decode(one)
+    sums = dot(thrice(pick.astype(jnp.bfloat16)), thirds(occ))[:, :1]
     if d != 1:
-        first = jnp.where(zh == 1, first, 0.0)
-    value = (mine_ref[...] + first + decode(two)) / (energy_ref[...] - sums)
+        one = jnp.where(zh == 1, one, 0.0)
+    return (mine + one + two) / (energy - sums)
+
+
+def finish_kernel(d, mine_ref, one_ref, two_ref, energy_ref, occ_ref, value_ref, code_ref, one, two, sems):
+    fetch([(one_ref, one), (two_ref, two)], sems)
+    value = finished(d, mine_ref[...], decode(one), decode(two), energy_ref[...], occ_ref[...])
     value_ref[...] = value
-    if d:
-        encode(value, code_ref[0])
+    encode(value, code_ref)
 
 
 def put(out_ref, buf, value, d, w, turned, g, sems, at):
@@ -340,7 +340,7 @@
     return jnp.where(zh == 1, code.astype(jnp.float32), turned) * scales(ref), 1 - zh
 
 
-def own_kernel(square_ref, near_ref, second_ref, third_ref, got1_ref, out_ref, got1, square, buf, sems, load_sems):
+def own_kernel(near_ref, second_ref, third_ref, got1_ref, out_ref, got1, buf, sems, load_sems):
     load = pltpu.make_async_copy(got1_ref, got1, load_sems.at[0])
     load.start()
     _, g, zh = place()
@@ -352,6 +352,18 @@
         else:
             turned = -dot(thrice(flip_matrix(1 - w)), thirds(mine))
             copies += put(out_ref, buf, jnp.where(zh == 1, turned, mine), d, w, zh, g, sems, at)
+    load.wait()
+    w = later(g, 1)
+    value, turned = returned(got1, 1, w, zh)
+    copies += put(out_ref, buf, value, 1, w, turned, g, sems, 3)
+    for copy in copies:
+        copy.wait()
+
+
+def square_kernel(mine_ref, one_ref, two_ref, energy_ref, occ_ref, _, out_ref, one, two, square, sems):
+    fetch([(one_ref, one), (two_ref, two)], sems)
+    _, g, _ = place()
+    value = finished(0, mine_ref[...], decode(one), decode(two), energy_ref[...], occ_ref[...])
     row, col = iotas(256, G)
     i, j = row >> 4, row & 15
     oi, oj, xi, xj = i >> 3, j >> 3, i & 7, j & 7
@@ -362,16 +374,8 @@
     plus = jnp.where(same, jnp.where((gap >= 1) & (gap <= 4), up, -1), jnp.where(oi < oj, xi * 8 + xj, -1))
     minus = jnp.where(same, jnp.where(gap >= 5, down, -1), jnp.where(oi > oj, xj * 8 + xi, -1))
     pick = (col == plus).astype(jnp.float32) - (col == minus).astype(jnp.float32)
-    square[...] = dot(thrice(pick.astype(jnp.bfloat16)), thirds(square_ref[...])).reshape(square.shape)
-    copy = pltpu.make_async_copy(square, slab(out_ref, g), load_sems.at[1])
-    copy.start()
-    copies.append(copy)
-    load.wait()
-    w = later(g, 1)
-    value, turned = returned(got1, 1, w, zh)
-    copies += put(out_ref, buf, value, 1, w, turned, g, sems, 3)
-    for copy in copies:
-        copy.wait()
+    square[...] = dot(thrice(pick.astype(jnp.bfloat16)), thirds(value)).reshape(square.shape)
+    fetch([(square, slab(out_ref, g))], sems)
 
 
 def back_kernel(d, got_ref, _, out_ref, got, buf, sems, load_sems):
@@ -464,7 +468,7 @@
         [IN_SMEM],
         [pltpu.SMEM((16,), jnp.int32)],
     )
-    stay1, stay2, stay3, own = split("keep", (), (1, 2, 3), True, todo)
+    stay1, stay2, stay3, own = split("keep", (), (1, 2, 3), True, jnp.zeros((8,), jnp.int32))
 
     square1, near1, square2, near2, near_rows, token = partials(
         "near", (0, 1), ((1, 1), (2, 1)), todo, 2 * G, integrals, todo, (own, stay1, got1)
@@ -509,48 +513,55 @@
     )
     square2 = send(square2, lambda b, o: (b + 2, o))
 
-    def finish(d, mine, one, two, *after):
+    landed = pltpu.VMEM((G + PAD, width), jnp.int16)
+
+    def finish(d, mine, one, two):
         return call(
             functools.partial(finish_kernel, d),
             "finish%d" % d,
-            [plain(G, width)] + [coded(G, width)] * (d > 0),
-            (mine, one, two, energy, occ, *after),
-            [IN_VMEM, ANY, ANY, IN_VMEM, IN_VMEM] + [ANY] * len(after),
-            [IN_VMEM] * (1 + (d > 0)),
-            [
-                pltpu.VMEM((G + PAD, width), jnp.int16),
-                pltpu.VMEM((G + PAD, width), jnp.int16),
-                pltpu.SemaphoreType.DMA((2,)),
-            ],
+            [plain(G, width), coded(G, width)],
+            (mine, one, two, energy, occ),
+            [IN_VMEM, ANY, ANY, IN_VMEM, IN_VMEM],
+            [IN_VMEM] * 2,
+            [landed, landed, pltpu.SemaphoreType.DMA((2,))],
         )
 
     done, back = {}, {}
     for d in (2, 3):
         done[d], code = finish(d, base[d][0], far[d][0], onward[d])
         back[d] = send(code, lambda b, o, d=d: (b, o ^ d))
-    (square,) = finish(0, square0, square1, square2)
-    near, code = finish(1, near0, near1, near2, near0)
+    near, code = finish(1, near0, near1, near2)
     back1 = send(code, lambda b, o: (b, o ^ 1))
 
     out = jax.ShapeDtypeStruct((i_local, nocc, width), jnp.float32)
-    landed = pltpu.VMEM((G + PAD, width), jnp.int16)
     (whole,) = call(
         own_kernel,
         "own",
         [out],
-        (square, near, done[2], done[3], back1),
-        [IN_VMEM, IN_VMEM, IN_VMEM, IN_VMEM, ANY],
+        (near, done[2], done[3], back1),
+        [IN_VMEM, IN_VMEM, IN_VMEM, ANY],
         [ANY],
         [
             landed,
-            pltpu.VMEM((16, 16, width), jnp.float32),
             pltpu.VMEM((4, 2, OCT, OCT, width), jnp.float32),
             pltpu.SemaphoreType.DMA((4, 2)),
-            pltpu.SemaphoreType.DMA((2,)),
+            pltpu.SemaphoreType.DMA((1,)),
         ],
         room=24,
     )
-    for d in (2, 3):
+    for d in ORDER:
+        if d == 0:
+            (whole,) = call(
+                square_kernel,
+                "square",
+                [out],
+                (square0, square1, square2, energy, occ, whole),
+                [IN_VMEM, ANY, ANY, IN_VMEM, IN_VMEM, ANY],
+                [ANY],
+                [landed, landed, pltpu.VMEM((16, 16, width), jnp.float32), pltpu.SemaphoreType.DMA((2,))],
+                aliases={5: 0},
+            )
+            continue
         (whole,) = call(
             functools.partial(back_kernel, d),
             "back%d" % d,
@@ -564,7 +575,7 @@
                 pltpu.SemaphoreType.DMA((1, 2)),
                 pltpu.SemaphoreType.DMA((1,)),
             ],
-                aliases={1: 0},
+            aliases={1: 0},
         )
     return whole
 

time: 93.3 us -> 86.4 us (0.926); the launches traced: 92.8 us -> 84.9 us
  starting transfers between devices: 21.9 us -> 18.4 us
  waiting for transfers between devices: 22.8 us -> 19.8 us
  local copies, waits for them, and re-layouts: 4.93 us -> 2.13 us
  Pallas kernels: 42.8 us -> 44.1 us
    ppermute x15, starting transfers between devices: 21.9 us -> 18.4 us  [send(): return lax.ppermute(value, BOTH, routes(where))]
    ppermute x15, waiting for transfers between devices: 22.8 us -> 19.8 us  [send(): return lax.ppermute(value, BOTH, routes(where))]
    unnamed x10, local copies, waits for them, and re-layouts: 3.79 us -> 1.91 us
    pallas_call x19, Pallas kernels: 42.8 us -> 44.1 us  [call(): pl.pallas_call(kernel, out_shape=outs, in_specs=in_specs, out_specs=out_s...]
  transfers between devices with their start and end apart: 15 -> 15, of which waited for: 6 -> 5; matrix products, arithmetic and copies ran while one was open for 1% -> 0% of each run, Pallas kernels for 43% -> 49%
where the time goes in v4:
time: 86.4 us; the launch traced here: 84.9 us
  Pallas kernels  44.1 us (51%)
  waiting for transfers between devices  19.8 us (23%)
  starting transfers between devices  18.4 us (21%)
  local copies, waits for them, and re-layouts  2.13 us (2%)
    pallas_call x19, Pallas kernels, call(): pl.pallas_call(kernel, out_shape=outs, in_specs=in_specs, out_specs=out_s...  44.1 us
    ppermute x15, waiting for transfers between devices, send(): return lax.ppermute(value, BOTH, routes(where))  19.8 us
    ppermute x15, starting transfers between devices, send(): return lax.ppermute(value, BOTH, routes(where))  18.4 us
    unnamed x10, local copies, waits for them, and re-layouts  1.91 us
  transfers between devices with their start and end apart: 15, of which 5 were waited for; matrix products, arithmetic and copies ran while one was open for 0% of the time, Pallas kernels for 49%

profile of v4, /device:TPU:1, one launch (start us, length us, event | category | flops | bytes accessed | tf_op | source)
XLA Modules:
  0.0 84.9 jit_solution(6754852978812387513)
XLA Ops:
  0.0 0.0 copy-start
  0.0 1.9 %copy-done = bf16[16,64,1536]{2,1,0:T(8,128)(2,1)S(1)} copy-done((bf16[16,64,1536]{2,1,0:T(8,128)(2,1)S(1)}, bf16[16,64,1536]{2,1,0:T(8,128)(2,1)}, u32[]{:S(2)}) %copy-start) | copy-done | bytes 3145752
  1.9 0.0 copy-start.2
  1.9 1.0 %give.1 = (bf16[128,1536]{1,0:T(8,128)(2,1)S(1)}, bf16[128,1536]{1,0:T(8,128)(2,1)S(1)}, bf16[128,1536]{1,0:T(8,128)(2,1)S(1)}) custom-call(bf16[16,64,1536]{2,1,0:T(8,128)(2,1)S(1)} %copy-done, s32[8]{0:T(128)S(1)} %broadcast_1__.2._), custom_call_target="tpu_custom_call" | custom-call | tf_op jit(solution)/shard_map/give/pallas_call | solution.py:391
  2.9 1.5 %collective-permute-start.2 = (bf16[128,1536]{1,0:T(8,128)(2,1)S(1)}, bf16[128,1536]{1,0:T(8,128)(2,1)S(1)}, u32[]{:S(2)}, u32[]{:S(2)}) collective-permute-start(bf16[128,1536]{1,0:T(8,128)(2,1)S(1)} %get-tuple-element.44), channel_id=1, source_target_pairs={{0,1},{1,0},{2,3},{3,2},{4,5},{5,4},{6,7},{7,6},{8,9},{9,8},{10,11... | collective-permute-start | bytes 1179656 | tf_op jit(solution)/shard_map/ppermute | solution.py:40
  4.4 1.7 %collective-permute-start.1 = (bf16[128,1536]{1,0:T(8,128)(2,1)S(1)}, bf16[128,1536]{1,0:T(8,128)(2,1)S(1)}, u32[]{:S(2)}, u32[]{:S(2)}) collective-permute-start(bf16[128,1536]{1,0:T(8,128)(2,1)S(1)} %get-tuple-element.41), channel_id=1, source_target_pairs={{0,2},{1,3},{2,0},{3,1},{4,6},{5,7},{6,4},{7,5},{8,10},{9,11},{10,... | collective-permute-start | bytes 1179656 | tf_op jit(solution)/shard_map/ppermute | solution.py:40
  6.2 0.1 collective-permute-start
  6.2 1.1 %keep.1 = (bf16[128,1536]{1,0:T(8,128)(2,1)S(1)}, bf16[128,1536]{1,0:T(8,128)(2,1)S(1)}, bf16[128,1536]{1,0:T(8,128)(2,1)S(1)}, bf16[256,1536]{1,0:T(8,128)(2,1)S(1)}) custom-call(bf16[16,64,1536]{2,1,0:T(8,128)(2,1)S(1)} %copy-done, s32[8]{0:T(128)S(1)} %broadcast_1__.2._), custom_call_target="tpu_custom_call" | custom-call | tf_op jit(solution)/shard_map/keep/pallas_call | solution.py:391
  7.3 0.0 copy-done.2
  7.3 0.1 slice_reduce_fusion.lab
  7.5 2.5 %plan.1.todo.refs_4_ = s32[488]{0:T(512)S(1)} custom-call(s32[384]{0:T(512)S(1)} %slice_reduce_fusion.lab), custom_call_target="tpu_custom_call" | custom-call | tf_op jit(solution)/shard_map/plan/pallas_call | solution.py:391
  10.0 0.0 collective-permute-done.2.refs_2_
  10.0 6.4 %near.1 = (s16[136,1536]{1,0:T(8,128)(2,1)S(1)}, s16[136,1536]{1,0:T(8,128)(2,1)S(1)}, s16[136,1536]{1,0:T(8,128)(2,1)S(1)}, s16[136,1536]{1,0:T(8,128)(2,1)S(1)...) custom-call(s32[488]{0:T(512)S(1)} %plan.1.todo.refs_4_, bf16[256,1536]{1,0:T(8,128)(2,1)S(1)} %get-tuple-element.42.refs_0_, ...), custom_call_target="tpu_custom_call" | custom-call | tf_op jit(solution)/shard_map/near/pallas_call | solution.py:391
  16.4 1.7 %collective-permute-start.9 = (s16[136,1536]{1,0:T(8,128)(2,1)S(1)}, s16[136,1536]{1,0:T(8,128)(2,1)S(1)}, u32[]{:S(2)}, u32[]{:S(2)}) collective-permute-start(s16[136,1536]{1,0:T(8,128)(2,1)S(1)} %get-tuple-element.62), channel_id=1, source_target_pairs={{0,2},{1,3},{2,0},{3,1},{4,6},{5,7},{6,4},{7,5},{8,10},{9,11},{10,... | collective-permute-start | bytes 1253384 | tf_op jit(solution)/shard_map/ppermute | solution.py:40
  18.1 0.0 collective-permute-done.1.refs_1_
  18.1 3.1 %far2.1 = (s16[136,1536]{1,0:T(8,128)(2,1)S(1)}, bf16[128,3072]{1,0:T(8,128)(2,1)S(1)}, s32[8]{0:T(128)S(1)}) custom-call(s32[488]{0:T(512)S(1)} %plan.1.todo.refs_4_, bf16[128,1536]{1,0:T(8,128)(2,1)S(1)} %get-tuple-element.40.refs_0_, bf16[128,1536]{1,0:T(8,128)(2,1)S(1)} %collective-permute-done.1.refs_1_, bf16[1536,4608]{1,0:T(8,128)(2,1)} %refs_1_.5, ...), custom_call_target="tpu_custom_call" | custom-call | tf_op jit(solution)/shard_map/far2/pallas_call | solution.py:391
  21.3 1.3 %collective-permute-start.6 = (s16[136,1536]{1,0:T(8,128)(2,1)S(1)}, s16[136,1536]{1,0:T(8,128)(2,1)S(1)}, u32[]{:S(2)}, u32[]{:S(2)}) collective-permute-start(s16[136,1536]{1,0:T(8,128)(2,1)S(1)} %get-tuple-element.56), channel_id=1, source_target_pairs={{0,6},{1,7},{2,4},{3,5},{4,2},{5,3},{6,0},{7,1},{8,14},{9,15},{10,... | collective-permute-start | bytes 1253384 | tf_op jit(solution)/shard_map/ppermute | solution.py:40
  22.6 1.7 %collective-permute-done.refs_1_ = bf16[128,1536]{1,0:T(8,128)(2,1)S(1)} collective-permute-done((bf16[128,1536]{1,0:T(8,128)(2,1)S(1)}, bf16[128,1536]{1,0:T(8,128)(2,1)S(1)}, u32[]{:S(2)}, u32[]{:S(2)}) %collective-permute-start) | collective-permute-done | bytes 393248 | tf_op jit(solution)/shard_map/ppermute | solution.py:40
  24.2 3.2 %far3.1 = (s16[136,1536]{1,0:T(8,128)(2,1)S(1)}, bf16[128,3072]{1,0:T(8,128)(2,1)S(1)}, s32[8]{0:T(128)S(1)}) custom-call(s32[488]{0:T(512)S(1)} %plan.1.todo.refs_4_, bf16[128,1536]{1,0:T(8,128)(2,1)S(1)} %get-tuple-element.38.refs_0_, bf16[128,1536]{1,0:T(8,128)(2,1)S(1)} %collective-permute-done.refs_1_, bf16[1536,4608]{1,0:T(8,128)(2,1)} %refs_1_.5, ...), custom_call_target="tpu_custom_call" | custom-call | tf_op jit(solution)/shard_map/far3/pallas_call | solution.py:391
  27.4 3.1 %collective-permute-start.3 = (s16[136,1536]{1,0:T(8,128)(2,1)S(1)}, s16[136,1536]{1,0:T(8,128)(2,1)S(1)}, u32[]{:S(2)}, u32[]{:S(2)}) collective-permute-start(s16[136,1536]{1,0:T(8,128)(2,1)S(1)} %get-tuple-element.52), channel_id=1, source_target_pairs={{0,7},{1,6},{2,5},{3,4},{4,3},{5,2},{6,1},{7,0},{8,15},{9,14},{10,... | collective-permute-start | bytes 1253384 | tf_op jit(solution)/shard_map/ppermute | solution.py:40
  30.5 0.6 collective-permute-start.12
  31.1 1.7 %collective-permute-start.13 = (s16[136,1536]{1,0:T(8,128)(2,1)S(1)}, s16[136,1536]{1,0:T(8,128)(2,1)S(1)}, u32[]{:S(2)}, u32[]{:S(2)}) collective-permute-start(s16[136,1536]{1,0:T(8,128)(2,1)S(1)} %get-tuple-element.66), channel_id=1, source_target_pairs={{0,8},{1,9},{2,10},{3,11},{4,12},{5,13},{6,14},{7,15},{8,16},{9,17... | collective-permute-start | bytes 1253384 | tf_op jit(solution)/shard_map/ppermute | solution.py:40
  32.8 4.6 %rest2.1 = (f32[128,1536]{1,0:T(8,128)S(1)}, f32[128,1536]{1,0:T(8,128)S(1)}, s32[8]{0:T(128)S(1)}) custom-call(s32[488]{0:T(512)S(1)} %plan.1.todo.refs_4_, bf16[128,3072]{1,0:T(8,128)(2,1)S(1)} %get-tuple-element.48.refs_0_, bf16[1536,4608]{1,0:T(8,128)(2,1)} %refs_1_.5, s32[8]{0:T(128)S(1)} %get-tuple-element.49.refs_2_), custom_call_target="tpu_custom_call" | custom-call | tf_op jit(solution)/shard_map/rest2/pallas_call | solution.py:391
  37.4 0.0 collective-permute-done.9
  37.4 2.0 %collective-permute-start.10 = (s16[136,1536]{1,0:T(8,128)(2,1)S(1)}, s16[136,1536]{1,0:T(8,128)(2,1)S(1)}, u32[]{:S(2)}, u32[]{:S(2)}) collective-permute-start(s16[136,1536]{1,0:T(8,128)(2,1)S(1)} %collective-permute-done.9), channel_id=1, source_target_pairs={{0,6},{1,7},{2,4},{3,5},{4,2},{5,3},{6,0},{7,1},{8,14},{9,15},{10,... | collective-permute-start | bytes 1253384 | tf_op jit(solution)/shard_map/ppermute | solution.py:40
  39.4 0.0 collective-permute-done.6.got_ref.one_ref
  39.4 0.5 merge2.1
  40.0 1.0 %collective-permute-start.7 = (s16[136,1536]{1,0:T(8,128)(2,1)S(1)}, s16[136,1536]{1,0:T(8,128)(2,1)S(1)}, u32[]{:S(2)}, u32[]{:S(2)}) collective-permute-start(s16[136,1536]{1,0:T(8,128)(2,1)S(1)} %merge2.1), channel_id=1, source_target_pairs={{0,8},{1,9},{2,10},{3,11},{4,12},{5,13},{6,14},{7,15},{8,16},{9,17... | collective-permute-start | bytes 1253384 | tf_op jit(solution)/shard_map/ppermute | solution.py:40
  40.9 0.0 copy-start.3
  40.9 0.0 copy-start.1
  40.9 4.6 %rest3.1 = (f32[128,1536]{1,0:T(8,128)S(1)}, f32[128,1536]{1,0:T(8,128)S(1)}, s32[8]{0:T(128)S(1)}) custom-call(s32[488]{0:T(512)S(1)} %plan.1.todo.refs_4_, bf16[128,3072]{1,0:T(8,128)(2,1)S(1)} %get-tuple-element.47.refs_0_, bf16[1536,4608]{1,0:T(8,128)(2,1)} %refs_1_.5, s32[8]{0:T(128)S(1)} %get-tuple-element.50.refs_2_), custom_call_target="tpu_custom_call" | custom-call | tf_op jit(solution)/shard_map/rest3/pallas_call | solution.py:391
  45.6 7.5 %collective-permute-done.3.got_ref.one_ref = s16[136,1536]{1,0:T(8,128)(2,1)S(1)} collective-permute-done((s16[136,1536]{1,0:T(8,128)(2,1)S(1)}, s16[136,1536]{1,0:T(8,128)(2,1)S(1)}, u32[]{:S(2)}, u32[]{:S(2)}) %collective-permute-start.3) | collective-permute-done | bytes 417824 | tf_op jit(solution)/shard_map/ppermute | solution.py:40
  53.0 0.5 merge3.1
  53.6 0.1 collective-permute-start.4
  53.6 0.0 copy-done.3
  53.7 0.0 copy-done.1
  53.7 0.0 copy-start.4
  53.7 4.4 %near0.1 = (f32[128,1536]{1,0:T(8,128)S(1)}, f32[128,1536]{1,0:T(8,128)S(1)}, s32[8]{0:T(128)}) custom-call(s32[488]{0:T(512)S(1)} %plan.1.todo.refs_4_, bf16[256,3072]{1,0:T(8,128)(2,1)S(1)} %copy-done.1, bf16[1536,4608]{1,0:T(8,128)(2,1)} %refs_1_.5, s32[8]{0:T(128)S(1)} %get-tuple-element.60.refs_2_), custom_call_target="tpu_custom_call" | custom-call | tf_op jit(solution)/shard_map/near0/pallas_call | solution.py:391
  58.1 0.0 collective-permute-done.12.one_ref
  58.1 0.0 collective-permute-done.13.two_ref
  58.1 0.0 copy-done.4
  58.1 0.1 broadcast_in_dim.2.occ_ref
  58.2 1.1 %finish1.1 = (f32[128,1536]{1,0:T(8,128)S(1)}, s16[136,1536]{1,0:T(8,128)(2,1)S(1)}) custom-call(f32[128,1536]{1,0:T(8,128)S(1)} %get-tuple-element.64.mine_ref, s16[136,1536]{1,0:T(8,128)(2,1)S(1)} %collective-permute-done.12.one_ref, s16[136,1536]{1,0:T(8,128)(2,1)S(1)} %collective-permute-done.13.two_ref, f32[1,1536]{1,0:T(1,128)S(1)} %reshape.8.energy_ref, ...), custom_call_target="tpu_custom_call" | custom-call | tf_op jit(solution)/shard_map/finish1/pallas_call | solution.py:391
  59.3 1.0 %collective-permute-start.14 = (s16[136,1536]{1,0:T(8,128)(2,1)S(1)}, s16[136,1536]{1,0:T(8,128)(2,1)S(1)}, u32[]{:S(2)}, u32[]{:S(2)}) collective-permute-start(s16[136,1536]{1,0:T(8,128)(2,1)S(1)} %get-tuple-element.70), channel_id=1, source_target_pairs={{0,1},{1,0},{2,3},{3,2},{4,5},{5,4},{6,7},{7,6},{8,9},{9,8},{10,11... | collective-permute-start | bytes 1253384 | tf_op jit(solution)/shard_map/ppermute | solution.py:40
  60.3 0.0 collective-permute-done.10.got_ref.one_ref
  60.3 0.6 merge0.1
  60.9 0.8 collective-permute-start.11
  61.7 0.0 collective-permute-done.7.two_ref
  61.7 1.2 %finish2.1 = (f32[128,1536]{1,0:T(8,128)S(1)}, s16[136,1536]{1,0:T(8,128)(2,1)S(1)}) custom-call(f32[128,1536]{1,0:T(8,128)S(1)} %get-tuple-element.55.mine_ref, s16[136,1536]{1,0:T(8,128)(2,1)S(1)} %collective-permute-done.6.got_ref.one_ref, s16[136,1536]{1,0:T(8,128)(2,1)S(1)} %collective-permute-done.7.two_ref, f32[1,1536]{1,0:T(1,128)S(1)} %reshape.8.energy_ref, ...), custom_call_target="tpu_custom_call" | custom-call | tf_op jit(solution)/shard_map/finish2/pallas_call | solution.py:391
  62.9 0.6 collective-permute-start.8
  63.4 4.4 %collective-permute-done.4.two_ref = s16[136,1536]{1,0:T(8,128)(2,1)S(1)} collective-permute-done((s16[136,1536]{1,0:T(8,128)(2,1)S(1)}, s16[136,1536]{1,0:T(8,128)(2,1)S(1)}, u32[]{:S(2)}, u32[]{:S(2)}) %collective-permute-start.4) | collective-permute-done | bytes 417824 | tf_op jit(solution)/shard_map/ppermute | solution.py:40
  67.8 1.1 %finish3.1 = (f32[128,1536]{1,0:T(8,128)S(1)}, s16[136,1536]{1,0:T(8,128)(2,1)S(1)}) custom-call(f32[128,1536]{1,0:T(8,128)S(1)} %get-tuple-element.51.mine_ref, s16[136,1536]{1,0:T(8,128)(2,1)S(1)} %collective-permute-done.3.got_ref.one_ref, s16[136,1536]{1,0:T(8,128)(2,1)S(1)} %collective-permute-done.4.two_ref, f32[1,1536]{1,0:T(1,128)S(1)} %reshape.8.energy_ref, ...), custom_call_target="tpu_custom_call" | custom-call | tf_op jit(solution)/shard_map/finish3/pallas_call | solution.py:391
  69.0 1.4 %collective-permute-start.5 = (s16[136,1536]{1,0:T(8,128)(2,1)S(1)}, s16[136,1536]{1,0:T(8,128)(2,1)S(1)}, u32[]{:S(2)}, u32[]{:S(2)}) collective-permute-start(s16[136,1536]{1,0:T(8,128)(2,1)S(1)} %get-tuple-element.54), channel_id=1, source_target_pairs={{0,3},{1,2},{2,1},{3,0},{4,7},{5,6},{6,5},{7,4},{8,11},{9,10},{10,... | collective-permute-start | bytes 1253384 | tf_op jit(solution)/shard_map/ppermute | solution.py:40
  70.4 0.0 collective-permute-done.14.got1_ref
  70.4 2.4 %own.1._ = f32[16,64,1536]{2,1,0:T(8,128)} custom-call(f32[128,1536]{1,0:T(8,128)S(1)} %get-tuple-element.67.near_ref, f32[128,1536]{1,0:T(8,128)S(1)} %get-tuple-element.68.second_ref, f32[128,1536]{1,0:T(8,128)S(1)} %get-tuple-element.69.third_ref, s16[136,1536]{1,0:T(8,128)(2,1)S(1)} %collective-permute-done.14.got1_ref), custom_call_target="tpu_custom_call" | custom-call | tf_op jit(solution)/shard_map/own/pallas_call | solution.py:391
  72.7 3.7 %collective-permute-done.11.two_ref = s16[136,1536]{1,0:T(8,128)(2,1)S(1)} collective-permute-done((s16[136,1536]{1,0:T(8,128)(2,1)S(1)}, s16[136,1536]{1,0:T(8,128)(2,1)S(1)}, u32[]{:S(2)}, u32[]{:S(2)}) %collective-permute-start.11) | collective-permute-done | bytes 417824 | tf_op jit(solution)/shard_map/ppermute | solution.py:40
  76.5 2.7 %square.1._ = f32[16,64,1536]{2,1,0:T(8,128)} custom-call(f32[128,1536]{1,0:T(8,128)S(1)} %get-tuple-element.61.mine_ref, s16[136,1536]{1,0:T(8,128)(2,1)S(1)} %collective-permute-done.10.got_ref.one_ref, s16[136,1536]{1,0:T(8,128)(2,1)S(1)} %collective-permute-done.11.two_ref, f32[1,1536]{1,0:T(1,128)S(1)} %reshape.8.energy_ref, ...), custom_call_target="tpu_custom_call", output_to_operand_aliasing={{}: (5, {})} | custom-call | tf_op jit(solution)/shard_map/square/pallas_call | solution.py:391
  79.2 0.0 collective-permute-done.8.got_ref
  79.2 1.5 %back2.1._ = f32[16,64,1536]{2,1,0:T(8,128)} custom-call(s16[136,1536]{1,0:T(8,128)(2,1)S(1)} %collective-permute-done.8.got_ref, f32[16,64,1536]{2,1,0:T(8,128)} %square.1._), custom_call_target="tpu_custom_call", output_to_operand_aliasing={{}: (1, {})} | custom-call | tf_op jit(solution)/shard_map/back2/pallas_call | solution.py:391
  80.7 2.5 %collective-permute-done.5.got_ref = s16[136,1536]{1,0:T(8,128)(2,1)S(1)} collective-permute-done((s16[136,1536]{1,0:T(8,128)(2,1)S(1)}, s16[136,1536]{1,0:T(8,128)(2,1)S(1)}, u32[]{:S(2)}, u32[]{:S(2)}) %collective-permute-start.5) | collective-permute-done | bytes 417824 | tf_op jit(solution)/shard_map/ppermute | solution.py:40
  83.3 1.5 %back3.1 = f32[16,64,1536]{2,1,0:T(8,128)} custom-call(s16[136,1536]{1,0:T(8,128)(2,1)S(1)} %collective-permute-done.5.got_ref, f32[16,64,1536]{2,1,0:T(8,128)} %back2.1._), custom_call_target="tpu_custom_call", output_to_operand_aliasing={{}: (1, {})} | custom-call | tf_op jit(solution)/shard_map/back3/pallas_call | solution.py:391
  (2 shorter events, 0.0 us)
Async XLA Ops:
  0.0 1.9 %copy-start = (bf16[16,64,1536]{2,1,0:T(8,128)(2,1)S(1)}, bf16[16,64,1536]{2,1,0:T(8,128)(2,1)}, u32[]{:S(2)}) copy-start(bf16[16,64,1536]{2,1,0:T(8,128)(2,1)} %t_ref.3) | copy-start | bytes 9437188
  1.9 5.4 %copy-start.2 = (s32[49152]{0:T(1024)S(1)}, s32[49152]{0:T(1024)}, u32[]{:S(2)}) copy-start(s32[49152]{0:T(1024)} %param.7) | copy-start | bytes 589828
  2.9 7.1 %collective-permute-start.2 = (bf16[128,1536]{1,0:T(8,128)(2,1)S(1)}, bf16[128,1536]{1,0:T(8,128)(2,1)S(1)}, u32[]{:S(2)}, u32[]{:S(2)}) collective-permute-start(bf16[128,1536]{1,0:T(8,128)(2,1)S(1)} %get-tuple-element.44), channel_id=1, source_target_pairs={{0,1},{1,0},{2,3},{3,2},{4,5},{5,4},{6,7},{7,6},{8,9},{9,8},{10,11... | collective-permute-start | bytes 1179656 | tf_op jit(solution)/shard_map/ppermute | solution.py:40
  4.4 13.7 %collective-permute-start.1 = (bf16[128,1536]{1,0:T(8,128)(2,1)S(1)}, bf16[128,1536]{1,0:T(8,128)(2,1)S(1)}, u32[]{:S(2)}, u32[]{:S(2)}) collective-permute-start(bf16[128,1536]{1,0:T(8,128)(2,1)S(1)} %get-tuple-element.41), channel_id=1, source_target_pairs={{0,2},{1,3},{2,0},{3,1},{4,6},{5,7},{6,4},{7,5},{8,10},{9,11},{10,... | collective-permute-start | bytes 1179656 | tf_op jit(solution)/shard_map/ppermute | solution.py:40
  6.2 18.1 %collective-permute-start = (bf16[128,1536]{1,0:T(8,128)(2,1)S(1)}, bf16[128,1536]{1,0:T(8,128)(2,1)S(1)}, u32[]{:S(2)}, u32[]{:S(2)}) collective-permute-start(bf16[128,1536]{1,0:T(8,128)(2,1)S(1)} %get-tuple-element.39), channel_id=1, source_target_pairs={{0,3},{1,2},{2,1},{3,0},{4,7},{5,6},{6,5},{7,4},{8,11},{9,10},{10,... | collective-permute-start | bytes 1179656 | tf_op jit(solution)/shard_map/ppermute | solution.py:40
  16.4 21.0 %collective-permute-start.9 = (s16[136,1536]{1,0:T(8,128)(2,1)S(1)}, s16[136,1536]{1,0:T(8,128)(2,1)S(1)}, u32[]{:S(2)}, u32[]{:S(2)}) collective-permute-start(s16[136,1536]{1,0:T(8,128)(2,1)S(1)} %get-tuple-element.62), channel_id=1, source_target_pairs={{0,2},{1,3},{2,0},{3,1},{4,6},{5,7},{6,4},{7,5},{8,10},{9,11},{10,... | collective-permute-start | bytes 1253384 | tf_op jit(solution)/shard_map/ppermute | solution.py:40
  21.3 18.1 %collective-permute-start.6 = (s16[136,1536]{1,0:T(8,128)(2,1)S(1)}, s16[136,1536]{1,0:T(8,128)(2,1)S(1)}, u32[]{:S(2)}, u32[]{:S(2)}) collective-permute-start(s16[136,1536]{1,0:T(8,128)(2,1)S(1)} %get-tuple-element.56), channel_id=1, source_target_pairs={{0,6},{1,7},{2,4},{3,5},{4,2},{5,3},{6,0},{7,1},{8,14},{9,15},{10,... | collective-permute-start | bytes 1253384 | tf_op jit(solution)/shard_map/ppermute | solution.py:40
  27.4 25.6 %collective-permute-start.3 = (s16[136,1536]{1,0:T(8,128)(2,1)S(1)}, s16[136,1536]{1,0:T(8,128)(2,1)S(1)}, u32[]{:S(2)}, u32[]{:S(2)}) collective-permute-start(s16[136,1536]{1,0:T(8,128)(2,1)S(1)} %get-tuple-element.52), channel_id=1, source_target_pairs={{0,7},{1,6},{2,5},{3,4},{4,3},{5,2},{6,1},{7,0},{8,15},{9,14},{10,... | collective-permute-start | bytes 1253384 | tf_op jit(solution)/shard_map/ppermute | solution.py:40
  30.5 27.6 %collective-permute-start.12 = (s16[136,1536]{1,0:T(8,128)(2,1)S(1)}, s16[136,1536]{1,0:T(8,128)(2,1)S(1)}, u32[]{:S(2)}, u32[]{:S(2)}) collective-permute-start(s16[136,1536]{1,0:T(8,128)(2,1)S(1)} %get-tuple-element.65), channel_id=1, source_target_pairs={{0,4},{1,5},{2,6},{3,7},{4,8},{5,9},{6,10},{7,11},{8,12},{9,13},{1... | collective-permute-start | bytes 1253384 | tf_op jit(solution)/shard_map/ppermute | solution.py:40
  31.1 27.0 %collective-permute-start.13 = (s16[136,1536]{1,0:T(8,128)(2,1)S(1)}, s16[136,1536]{1,0:T(8,128)(2,1)S(1)}, u32[]{:S(2)}, u32[]{:S(2)}) collective-permute-start(s16[136,1536]{1,0:T(8,128)(2,1)S(1)} %get-tuple-element.66), channel_id=1, source_target_pairs={{0,8},{1,9},{2,10},{3,11},{4,12},{5,13},{6,14},{7,15},{8,16},{9,17... | collective-permute-start | bytes 1253384 | tf_op jit(solution)/shard_map/ppermute | solution.py:40
  37.4 22.9 %collective-permute-start.10 = (s16[136,1536]{1,0:T(8,128)(2,1)S(1)}, s16[136,1536]{1,0:T(8,128)(2,1)S(1)}, u32[]{:S(2)}, u32[]{:S(2)}) collective-permute-start(s16[136,1536]{1,0:T(8,128)(2,1)S(1)} %collective-permute-done.9), channel_id=1, source_target_pairs={{0,6},{1,7},{2,4},{3,5},{4,2},{5,3},{6,0},{7,1},{8,14},{9,15},{10,... | collective-permute-start | bytes 1253384 | tf_op jit(solution)/shard_map/ppermute | solution.py:40
  40.0 21.7 %collective-permute-start.7 = (s16[136,1536]{1,0:T(8,128)(2,1)S(1)}, s16[136,1536]{1,0:T(8,128)(2,1)S(1)}, u32[]{:S(2)}, u32[]{:S(2)}) collective-permute-start(s16[136,1536]{1,0:T(8,128)(2,1)S(1)} %merge2.1), channel_id=1, source_target_pairs={{0,8},{1,9},{2,10},{3,11},{4,12},{5,13},{6,14},{7,15},{8,16},{9,17... | collective-permute-start | bytes 1253384 | tf_op jit(solution)/shard_map/ppermute | solution.py:40
  40.9 12.7 %copy-start.3 = (f32[1536]{0:T(1024)S(1)}, f32[1536]{0:T(1024)}, u32[]{:S(2)}) copy-start(f32[1536]{0:T(1024)} %param.8) | copy-start | bytes 18436
  40.9 12.8 %copy-start.1 = (bf16[256,3072]{1,0:T(8,128)(2,1)S(1)}, bf16[256,3072]{1,0:T(8,128)(2,1)}, u32[]{:S(2)}) copy-start(bf16[256,3072]{1,0:T(8,128)(2,1)} %get-tuple-element.59.refs_0_) | copy-start | bytes 4718596
  53.6 14.3 %collective-permute-start.4 = (s16[136,1536]{1,0:T(8,128)(2,1)S(1)}, s16[136,1536]{1,0:T(8,128)(2,1)S(1)}, u32[]{:S(2)}, u32[]{:S(2)}) collective-permute-start(s16[136,1536]{1,0:T(8,128)(2,1)S(1)} %merge3.1), channel_id=1, source_target_pairs={{0,8},{1,9},{2,10},{3,11},{4,12},{5,13},{6,14},{7,15},{8,16},{9,17... | collective-permute-start | bytes 1253384 | tf_op jit(solution)/shard_map/ppermute | solution.py:40
  53.7 4.4 %copy-start.4 = (f32[64]{0:T(128)S(1)}, f32[64]{0:T(128)}, u32[]{:S(2)}) copy-start(f32[64]{0:T(128)} %param.9) | copy-start | bytes 772
  59.3 11.1 %collective-permute-start.14 = (s16[136,1536]{1,0:T(8,128)(2,1)S(1)}, s16[136,1536]{1,0:T(8,128)(2,1)S(1)}, u32[]{:S(2)}, u32[]{:S(2)}) collective-permute-start(s16[136,1536]{1,0:T(8,128)(2,1)S(1)} %get-tuple-element.70), channel_id=1, source_target_pairs={{0,1},{1,0},{2,3},{3,2},{4,5},{5,4},{6,7},{7,6},{8,9},{9,8},{10,11... | collective-permute-start | bytes 1253384 | tf_op jit(solution)/shard_map/ppermute | solution.py:40
  60.9 15.6 %collective-permute-start.11 = (s16[136,1536]{1,0:T(8,128)(2,1)S(1)}, s16[136,1536]{1,0:T(8,128)(2,1)S(1)}, u32[]{:S(2)}, u32[]{:S(2)}) collective-permute-start(s16[136,1536]{1,0:T(8,128)(2,1)S(1)} %merge0.1), channel_id=1, source_target_pairs={{0,8},{1,9},{2,10},{3,11},{4,12},{5,13},{6,14},{7,15},{8,16},{9,17... | collective-permute-start | bytes 1253384 | tf_op jit(solution)/shard_map/ppermute | solution.py:40
  62.9 16.4 %collective-permute-start.8 = (s16[136,1536]{1,0:T(8,128)(2,1)S(1)}, s16[136,1536]{1,0:T(8,128)(2,1)S(1)}, u32[]{:S(2)}, u32[]{:S(2)}) collective-permute-start(s16[136,1536]{1,0:T(8,128)(2,1)S(1)} %get-tuple-element.58), channel_id=1, source_target_pairs={{0,2},{1,3},{2,0},{3,1},{4,6},{5,7},{6,4},{7,5},{8,10},{9,11},{10,... | collective-permute-start | bytes 1253384 | tf_op jit(solution)/shard_map/ppermute | solution.py:40
  69.0 14.3 %collective-permute-start.5 = (s16[136,1536]{1,0:T(8,128)(2,1)S(1)}, s16[136,1536]{1,0:T(8,128)(2,1)S(1)}, u32[]{:S(2)}, u32[]{:S(2)}) collective-permute-start(s16[136,1536]{1,0:T(8,128)(2,1)S(1)} %get-tuple-element.54), channel_id=1, source_target_pairs={{0,3},{1,2},{2,1},{3,0},{4,7},{5,6},{6,5},{7,4},{8,11},{9,10},{10,... | collective-permute-start | bytes 1253384 | tf_op jit(solution)/shard_map/ppermute | solution.py:40

commit v5 on v4

--- a/solution.py
+++ b/solution.py
@@ -15,7 +15,7 @@
 PAD = 8
 LEVELS = 32000.0
 STEPS = 256.0
-MANY = 8
+MANY = 4
 LABELS = 8
 ORDER = (0, 2, 3)
 SLOTS = 160

time: 86.4 us -> 87.9 us (1.017)
  Pallas kernels: 44.1 us -> 50.7 us
  starting transfers between devices: 18.4 us -> 14.2 us
    pallas_call x19, Pallas kernels: 44.1 us -> 50.7 us  [call(): pl.pallas_call(kernel, out_shape=outs, in_specs=in_specs, out_specs=out_s...]
    ppermute x15, starting transfers between devices: 18.4 us -> 14.2 us  [send(): return lax.ppermute(value, BOTH, routes(where))]
  transfers between devices with their start and end apart: 15 -> 15, of which waited for: 5 -> 5; matrix products, arithmetic and copies ran while one was open for 0% -> 0% of each run, Pallas kernels for 49% -> 55%
where the time goes in v5:
time: 87.9 us; the launch traced here: 87.2 us
  Pallas kernels  50.7 us (58%)
  waiting for transfers between devices  19.9 us (23%)
  starting transfers between devices  14.2 us (16%)
  local copies, waits for them, and re-layouts  2.13 us (2%)
    pallas_call x19, Pallas kernels, call(): pl.pallas_call(kernel, out_shape=outs, in_specs=in_specs, out_specs=out_s...  50.7 us
    ppermute x15, waiting for transfers between devices, send(): return lax.ppermute(value, BOTH, routes(where))  19.9 us
    ppermute x15, starting transfers between devices, send(): return lax.ppermute(value, BOTH, routes(where))  14.2 us
    unnamed x10, local copies, waits for them, and re-layouts  1.91 us
  transfers between devices with their start and end apart: 15, of which 5 were waited for; matrix products, arithmetic and copies ran while one was open for 0% of the time, Pallas kernels for 55%

profile of v5, /device:TPU:1, one launch (start us, length us, event | category | flops | bytes accessed | tf_op | source)
XLA Modules:
  0.0 87.2 jit_solution(5065673460054882775)
XLA Ops:
  0.0 0.0 copy-start
  0.0 1.9 %copy-done = bf16[16,64,1536]{2,1,0:T(8,128)(2,1)S(1)} copy-done((bf16[16,64,1536]{2,1,0:T(8,128)(2,1)S(1)}, bf16[16,64,1536]{2,1,0:T(8,128)(2,1)}, u32[]{:S(2)}) %copy-start) | copy-done | bytes 3145752
  1.9 0.0 copy-start.2
  1.9 1.0 %give.1 = (bf16[128,1536]{1,0:T(8,128)(2,1)S(1)}, bf16[128,1536]{1,0:T(8,128)(2,1)S(1)}, bf16[128,1536]{1,0:T(8,128)(2,1)S(1)}) custom-call(bf16[16,64,1536]{2,1,0:T(8,128)(2,1)S(1)} %copy-done, s32[8]{0:T(128)S(1)} %broadcast_1__.2._), custom_call_target="tpu_custom_call" | custom-call | tf_op jit(solution)/shard_map/give/pallas_call | solution.py:391
  2.9 1.5 %collective-permute-start.2 = (bf16[128,1536]{1,0:T(8,128)(2,1)S(1)}, bf16[128,1536]{1,0:T(8,128)(2,1)S(1)}, u32[]{:S(2)}, u32[]{:S(2)}) collective-permute-start(bf16[128,1536]{1,0:T(8,128)(2,1)S(1)} %get-tuple-element.44), channel_id=1, source_target_pairs={{0,1},{1,0},{2,3},{3,2},{4,5},{5,4},{6,7},{7,6},{8,9},{9,8},{10,11... | collective-permute-start | bytes 1179656 | tf_op jit(solution)/shard_map/ppermute | solution.py:40
  4.4 1.7 %collective-permute-start.1 = (bf16[128,1536]{1,0:T(8,128)(2,1)S(1)}, bf16[128,1536]{1,0:T(8,128)(2,1)S(1)}, u32[]{:S(2)}, u32[]{:S(2)}) collective-permute-start(bf16[128,1536]{1,0:T(8,128)(2,1)S(1)} %get-tuple-element.41), channel_id=1, source_target_pairs={{0,2},{1,3},{2,0},{3,1},{4,6},{5,7},{6,4},{7,5},{8,10},{9,11},{10,... | collective-permute-start | bytes 1179656 | tf_op jit(solution)/shard_map/ppermute | solution.py:40
  6.2 0.1 collective-permute-start
  6.2 1.1 %keep.1 = (bf16[128,1536]{1,0:T(8,128)(2,1)S(1)}, bf16[128,1536]{1,0:T(8,128)(2,1)S(1)}, bf16[128,1536]{1,0:T(8,128)(2,1)S(1)}, bf16[256,1536]{1,0:T(8,128)(2,1)S(1)}) custom-call(bf16[16,64,1536]{2,1,0:T(8,128)(2,1)S(1)} %copy-done, s32[8]{0:T(128)S(1)} %broadcast_1__.2._), custom_call_target="tpu_custom_call" | custom-call | tf_op jit(solution)/shard_map/keep/pallas_call | solution.py:391
  7.3 0.0 copy-done.2
  7.3 0.1 slice_reduce_fusion.lab
  7.5 2.6 %plan.1.todo.refs_4_ = s32[488]{0:T(512)S(1)} custom-call(s32[384]{0:T(512)S(1)} %slice_reduce_fusion.lab), custom_call_target="tpu_custom_call" | custom-call | tf_op jit(solution)/shard_map/plan/pallas_call | solution.py:391
  10.1 0.0 collective-permute-done.2.refs_2_
  10.1 7.6 %near.1 = (s16[136,1536]{1,0:T(8,128)(2,1)S(1)}, s16[136,1536]{1,0:T(8,128)(2,1)S(1)}, s16[136,1536]{1,0:T(8,128)(2,1)S(1)}, s16[136,1536]{1,0:T(8,128)(2,1)S(1)...) custom-call(s32[488]{0:T(512)S(1)} %plan.1.todo.refs_4_, bf16[256,1536]{1,0:T(8,128)(2,1)S(1)} %get-tuple-element.42.refs_0_, ...), custom_call_target="tpu_custom_call" | custom-call | tf_op jit(solution)/shard_map/near/pallas_call | solution.py:391
  17.7 1.7 %collective-permute-start.9 = (s16[136,1536]{1,0:T(8,128)(2,1)S(1)}, s16[136,1536]{1,0:T(8,128)(2,1)S(1)}, u32[]{:S(2)}, u32[]{:S(2)}) collective-permute-start(s16[136,1536]{1,0:T(8,128)(2,1)S(1)} %get-tuple-element.62), channel_id=1, source_target_pairs={{0,2},{1,3},{2,0},{3,1},{4,6},{5,7},{6,4},{7,5},{8,10},{9,11},{10,... | collective-permute-start | bytes 1253384 | tf_op jit(solution)/shard_map/ppermute | solution.py:40
  19.4 0.0 collective-permute-done.1.refs_1_
  19.4 3.7 %far2.1 = (s16[136,1536]{1,0:T(8,128)(2,1)S(1)}, bf16[128,3072]{1,0:T(8,128)(2,1)S(1)}, s32[8]{0:T(128)S(1)}) custom-call(s32[488]{0:T(512)S(1)} %plan.1.todo.refs_4_, bf16[128,1536]{1,0:T(8,128)(2,1)S(1)} %get-tuple-element.40.refs_0_, bf16[128,1536]{1,0:T(8,128)(2,1)S(1)} %collective-permute-done.1.refs_1_, bf16[1536,4608]{1,0:T(8,128)(2,1)} %refs_1_.5, ...), custom_call_target="tpu_custom_call" | custom-call | tf_op jit(solution)/shard_map/far2/pallas_call | solution.py:391
  23.1 0.1 collective-permute-start.6
  23.2 1.0 %collective-permute-done.refs_1_ = bf16[128,1536]{1,0:T(8,128)(2,1)S(1)} collective-permute-done((bf16[128,1536]{1,0:T(8,128)(2,1)S(1)}, bf16[128,1536]{1,0:T(8,128)(2,1)S(1)}, u32[]{:S(2)}, u32[]{:S(2)}) %collective-permute-start) | collective-permute-done | bytes 393248 | tf_op jit(solution)/shard_map/ppermute | solution.py:40
  24.2 3.7 %far3.1 = (s16[136,1536]{1,0:T(8,128)(2,1)S(1)}, bf16[128,3072]{1,0:T(8,128)(2,1)S(1)}, s32[8]{0:T(128)S(1)}) custom-call(s32[488]{0:T(512)S(1)} %plan.1.todo.refs_4_, bf16[128,1536]{1,0:T(8,128)(2,1)S(1)} %get-tuple-element.38.refs_0_, bf16[128,1536]{1,0:T(8,128)(2,1)S(1)} %collective-permute-done.refs_1_, bf16[1536,4608]{1,0:T(8,128)(2,1)} %refs_1_.5, ...), custom_call_target="tpu_custom_call" | custom-call | tf_op jit(solution)/shard_map/far3/pallas_call | solution.py:391
  27.9 2.9 %collective-permute-start.3 = (s16[136,1536]{1,0:T(8,128)(2,1)S(1)}, s16[136,1536]{1,0:T(8,128)(2,1)S(1)}, u32[]{:S(2)}, u32[]{:S(2)}) collective-permute-start(s16[136,1536]{1,0:T(8,128)(2,1)S(1)} %get-tuple-element.52), channel_id=1, source_target_pairs={{0,7},{1,6},{2,5},{3,4},{4,3},{5,2},{6,1},{7,0},{8,15},{9,14},{10,... | collective-permute-start | bytes 1253384 | tf_op jit(solution)/shard_map/ppermute | solution.py:40
  30.8 0.6 collective-permute-start.12
  31.4 1.2 %collective-permute-start.13 = (s16[136,1536]{1,0:T(8,128)(2,1)S(1)}, s16[136,1536]{1,0:T(8,128)(2,1)S(1)}, u32[]{:S(2)}, u32[]{:S(2)}) collective-permute-start(s16[136,1536]{1,0:T(8,128)(2,1)S(1)} %get-tuple-element.66), channel_id=1, source_target_pairs={{0,8},{1,9},{2,10},{3,11},{4,12},{5,13},{6,14},{7,15},{8,16},{9,17... | collective-permute-start | bytes 1253384 | tf_op jit(solution)/shard_map/ppermute | solution.py:40
  32.7 6.3 %rest2.1 = (f32[128,1536]{1,0:T(8,128)S(1)}, f32[128,1536]{1,0:T(8,128)S(1)}, s32[8]{0:T(128)S(1)}) custom-call(s32[488]{0:T(512)S(1)} %plan.1.todo.refs_4_, bf16[128,3072]{1,0:T(8,128)(2,1)S(1)} %get-tuple-element.48.refs_0_, bf16[1536,4608]{1,0:T(8,128)(2,1)} %refs_1_.5, s32[8]{0:T(128)S(1)} %get-tuple-element.49.refs_2_), custom_call_target="tpu_custom_call" | custom-call | tf_op jit(solution)/shard_map/rest2/pallas_call | solution.py:391
  39.0 0.0 collective-permute-done.9
  39.0 1.0 %collective-permute-start.10 = (s16[136,1536]{1,0:T(8,128)(2,1)S(1)}, s16[136,1536]{1,0:T(8,128)(2,1)S(1)}, u32[]{:S(2)}, u32[]{:S(2)}) collective-permute-start(s16[136,1536]{1,0:T(8,128)(2,1)S(1)} %collective-permute-done.9), channel_id=1, source_target_pairs={{0,6},{1,7},{2,4},{3,5},{4,2},{5,3},{6,0},{7,1},{8,14},{9,15},{10,... | collective-permute-start | bytes 1253384 | tf_op jit(solution)/shard_map/ppermute | solution.py:40
  40.1 0.0 collective-permute-done.6.got_ref.one_ref
  40.1 0.5 merge2.1
  40.6 1.4 %collective-permute-start.7 = (s16[136,1536]{1,0:T(8,128)(2,1)S(1)}, s16[136,1536]{1,0:T(8,128)(2,1)S(1)}, u32[]{:S(2)}, u32[]{:S(2)}) collective-permute-start(s16[136,1536]{1,0:T(8,128)(2,1)S(1)} %merge2.1), channel_id=1, source_target_pairs={{0,8},{1,9},{2,10},{3,11},{4,12},{5,13},{6,14},{7,15},{8,16},{9,17... | collective-permute-start | bytes 1253384 | tf_op jit(solution)/shard_map/ppermute | solution.py:40
  42.1 0.0 copy-start.3
  42.1 0.0 copy-start.1
  42.1 6.3 %rest3.1 = (f32[128,1536]{1,0:T(8,128)S(1)}, f32[128,1536]{1,0:T(8,128)S(1)}, s32[8]{0:T(128)S(1)}) custom-call(s32[488]{0:T(512)S(1)} %plan.1.todo.refs_4_, bf16[128,3072]{1,0:T(8,128)(2,1)S(1)} %get-tuple-element.47.refs_0_, bf16[1536,4608]{1,0:T(8,128)(2,1)} %refs_1_.5, s32[8]{0:T(128)S(1)} %get-tuple-element.50.refs_2_), custom_call_target="tpu_custom_call" | custom-call | tf_op jit(solution)/shard_map/rest3/pallas_call | solution.py:391
  48.4 6.4 %collective-permute-done.3.got_ref.one_ref = s16[136,1536]{1,0:T(8,128)(2,1)S(1)} collective-permute-done((s16[136,1536]{1,0:T(8,128)(2,1)S(1)}, s16[136,1536]{1,0:T(8,128)(2,1)S(1)}, u32[]{:S(2)}, u32[]{:S(2)}) %collective-permute-start.3) | collective-permute-done | bytes 417824 | tf_op jit(solution)/shard_map/ppermute | solution.py:40
  54.8 0.5 merge3.1
  55.4 0.1 collective-permute-start.4
  55.5 0.0 copy-done.3
  55.5 0.0 copy-done.1
  55.5 0.0 copy-start.4
  55.5 5.2 %near0.1 = (f32[128,1536]{1,0:T(8,128)S(1)}, f32[128,1536]{1,0:T(8,128)S(1)}, s32[8]{0:T(128)}) custom-call(s32[488]{0:T(512)S(1)} %plan.1.todo.refs_4_, bf16[256,3072]{1,0:T(8,128)(2,1)S(1)} %copy-done.1, bf16[1536,4608]{1,0:T(8,128)(2,1)} %refs_1_.5, s32[8]{0:T(128)S(1)} %get-tuple-element.60.refs_2_), custom_call_target="tpu_custom_call" | custom-call | tf_op jit(solution)/shard_map/near0/pallas_call | solution.py:391
  60.7 0.0 collective-permute-done.12.one_ref
  60.7 0.0 collective-permute-done.13.two_ref
  60.7 0.0 copy-done.4
  60.7 0.1 broadcast_in_dim.2.occ_ref
  60.8 1.1 %finish1.1 = (f32[128,1536]{1,0:T(8,128)S(1)}, s16[136,1536]{1,0:T(8,128)(2,1)S(1)}) custom-call(f32[128,1536]{1,0:T(8,128)S(1)} %get-tuple-element.64.mine_ref, s16[136,1536]{1,0:T(8,128)(2,1)S(1)} %collective-permute-done.12.one_ref, s16[136,1536]{1,0:T(8,128)(2,1)S(1)} %collective-permute-done.13.two_ref, f32[1,1536]{1,0:T(1,128)S(1)} %reshape.8.energy_ref, ...), custom_call_target="tpu_custom_call" | custom-call | tf_op jit(solution)/shard_map/finish1/pallas_call | solution.py:391
  61.9 0.1 collective-permute-start.14
  62.0 0.0 collective-permute-done.10.got_ref.one_ref
  62.0 0.6 merge0.1
  62.7 1.4 %collective-permute-start.11 = (s16[136,1536]{1,0:T(8,128)(2,1)S(1)}, s16[136,1536]{1,0:T(8,128)(2,1)S(1)}, u32[]{:S(2)}, u32[]{:S(2)}) collective-permute-start(s16[136,1536]{1,0:T(8,128)(2,1)S(1)} %merge0.1), channel_id=1, source_target_pairs={{0,8},{1,9},{2,10},{3,11},{4,12},{5,13},{6,14},{7,15},{8,16},{9,17... | collective-permute-start | bytes 1253384 | tf_op jit(solution)/shard_map/ppermute | solution.py:40
  64.1 0.0 collective-permute-done.7.two_ref
  64.1 1.2 %finish2.1 = (f32[128,1536]{1,0:T(8,128)S(1)}, s16[136,1536]{1,0:T(8,128)(2,1)S(1)}) custom-call(f32[128,1536]{1,0:T(8,128)S(1)} %get-tuple-element.55.mine_ref, s16[136,1536]{1,0:T(8,128)(2,1)S(1)} %collective-permute-done.6.got_ref.one_ref, s16[136,1536]{1,0:T(8,128)(2,1)S(1)} %collective-permute-done.7.two_ref, f32[1,1536]{1,0:T(1,128)S(1)} %reshape.8.energy_ref, ...), custom_call_target="tpu_custom_call" | custom-call | tf_op jit(solution)/shard_map/finish2/pallas_call | solution.py:391
  65.2 0.1 collective-permute-start.8
  65.3 4.3 %collective-permute-done.4.two_ref = s16[136,1536]{1,0:T(8,128)(2,1)S(1)} collective-permute-done((s16[136,1536]{1,0:T(8,128)(2,1)S(1)}, s16[136,1536]{1,0:T(8,128)(2,1)S(1)}, u32[]{:S(2)}, u32[]{:S(2)}) %collective-permute-start.4) | collective-permute-done | bytes 417824 | tf_op jit(solution)/shard_map/ppermute | solution.py:40
  69.6 1.1 %finish3.1 = (f32[128,1536]{1,0:T(8,128)S(1)}, s16[136,1536]{1,0:T(8,128)(2,1)S(1)}) custom-call(f32[128,1536]{1,0:T(8,128)S(1)} %get-tuple-element.51.mine_ref, s16[136,1536]{1,0:T(8,128)(2,1)S(1)} %collective-permute-done.3.got_ref.one_ref, s16[136,1536]{1,0:T(8,128)(2,1)S(1)} %collective-permute-done.4.two_ref, f32[1,1536]{1,0:T(1,128)S(1)} %reshape.8.energy_ref, ...), custom_call_target="tpu_custom_call" | custom-call | tf_op jit(solution)/shard_map/finish3/pallas_call | solution.py:391
  70.8 0.2 collective-permute-start.5
  70.9 0.0 collective-permute-done.14.got1_ref
  70.9 2.4 %own.1._ = f32[16,64,1536]{2,1,0:T(8,128)} custom-call(f32[128,1536]{1,0:T(8,128)S(1)} %get-tuple-element.67.near_ref, f32[128,1536]{1,0:T(8,128)S(1)} %get-tuple-element.68.second_ref, f32[128,1536]{1,0:T(8,128)S(1)} %get-tuple-element.69.third_ref, s16[136,1536]{1,0:T(8,128)(2,1)S(1)} %collective-permute-done.14.got1_ref), custom_call_target="tpu_custom_call" | custom-call | tf_op jit(solution)/shard_map/own/pallas_call | solution.py:391
  73.3 4.7 %collective-permute-done.11.two_ref = s16[136,1536]{1,0:T(8,128)(2,1)S(1)} collective-permute-done((s16[136,1536]{1,0:T(8,128)(2,1)S(1)}, s16[136,1536]{1,0:T(8,128)(2,1)S(1)}, u32[]{:S(2)}, u32[]{:S(2)}) %collective-permute-start.11) | collective-permute-done | bytes 417824 | tf_op jit(solution)/shard_map/ppermute | solution.py:40
  78.0 2.7 %square.1._ = f32[16,64,1536]{2,1,0:T(8,128)} custom-call(f32[128,1536]{1,0:T(8,128)S(1)} %get-tuple-element.61.mine_ref, s16[136,1536]{1,0:T(8,128)(2,1)S(1)} %collective-permute-done.10.got_ref.one_ref, s16[136,1536]{1,0:T(8,128)(2,1)S(1)} %collective-permute-done.11.two_ref, f32[1,1536]{1,0:T(1,128)S(1)} %reshape.8.energy_ref, ...), custom_call_target="tpu_custom_call", output_to_operand_aliasing={{}: (5, {})} | custom-call | tf_op jit(solution)/shard_map/square/pallas_call | solution.py:391
  80.8 0.0 collective-permute-done.8.got_ref
  80.8 1.5 %back2.1._ = f32[16,64,1536]{2,1,0:T(8,128)} custom-call(s16[136,1536]{1,0:T(8,128)(2,1)S(1)} %collective-permute-done.8.got_ref, f32[16,64,1536]{2,1,0:T(8,128)} %square.1._), custom_call_target="tpu_custom_call", output_to_operand_aliasing={{}: (1, {})} | custom-call | tf_op jit(solution)/shard_map/back2/pallas_call | solution.py:391
  82.3 3.4 %collective-permute-done.5.got_ref = s16[136,1536]{1,0:T(8,128)(2,1)S(1)} collective-permute-done((s16[136,1536]{1,0:T(8,128)(2,1)S(1)}, s16[136,1536]{1,0:T(8,128)(2,1)S(1)}, u32[]{:S(2)}, u32[]{:S(2)}) %collective-permute-start.5) | collective-permute-done | bytes 417824 | tf_op jit(solution)/shard_map/ppermute | solution.py:40
  85.6 1.5 %back3.1 = f32[16,64,1536]{2,1,0:T(8,128)} custom-call(s16[136,1536]{1,0:T(8,128)(2,1)S(1)} %collective-permute-done.5.got_ref, f32[16,64,1536]{2,1,0:T(8,128)} %back2.1._), custom_call_target="tpu_custom_call", output_to_operand_aliasing={{}: (1, {})} | custom-call | tf_op jit(solution)/shard_map/back3/pallas_call | solution.py:391
  (2 shorter events, 0.0 us)
Async XLA Ops:
  0.0 1.9 %copy-start = (bf16[16,64,1536]{2,1,0:T(8,128)(2,1)S(1)}, bf16[16,64,1536]{2,1,0:T(8,128)(2,1)}, u32[]{:S(2)}) copy-start(bf16[16,64,1536]{2,1,0:T(8,128)(2,1)} %t_ref.3) | copy-start | bytes 9437188
  1.9 5.4 %copy-start.2 = (s32[49152]{0:T(1024)S(1)}, s32[49152]{0:T(1024)}, u32[]{:S(2)}) copy-start(s32[49152]{0:T(1024)} %param.7) | copy-start | bytes 589828
  2.9 7.1 %collective-permute-start.2 = (bf16[128,1536]{1,0:T(8,128)(2,1)S(1)}, bf16[128,1536]{1,0:T(8,128)(2,1)S(1)}, u32[]{:S(2)}, u32[]{:S(2)}) collective-permute-start(bf16[128,1536]{1,0:T(8,128)(2,1)S(1)} %get-tuple-element.44), channel_id=1, source_target_pairs={{0,1},{1,0},{2,3},{3,2},{4,5},{5,4},{6,7},{7,6},{8,9},{9,8},{10,11... | collective-permute-start | bytes 1179656 | tf_op jit(solution)/shard_map/ppermute | solution.py:40
  4.4 15.0 %collective-permute-start.1 = (bf16[128,1536]{1,0:T(8,128)(2,1)S(1)}, bf16[128,1536]{1,0:T(8,128)(2,1)S(1)}, u32[]{:S(2)}, u32[]{:S(2)}) collective-permute-start(bf16[128,1536]{1,0:T(8,128)(2,1)S(1)} %get-tuple-element.41), channel_id=1, source_target_pairs={{0,2},{1,3},{2,0},{3,1},{4,6},{5,7},{6,4},{7,5},{8,10},{9,11},{10,... | collective-permute-start | bytes 1179656 | tf_op jit(solution)/shard_map/ppermute | solution.py:40
  6.2 18.1 %collective-permute-start = (bf16[128,1536]{1,0:T(8,128)(2,1)S(1)}, bf16[128,1536]{1,0:T(8,128)(2,1)S(1)}, u32[]{:S(2)}, u32[]{:S(2)}) collective-permute-start(bf16[128,1536]{1,0:T(8,128)(2,1)S(1)} %get-tuple-element.39), channel_id=1, source_target_pairs={{0,3},{1,2},{2,1},{3,0},{4,7},{5,6},{6,5},{7,4},{8,11},{9,10},{10,... | collective-permute-start | bytes 1179656 | tf_op jit(solution)/shard_map/ppermute | solution.py:40
  17.7 21.4 %collective-permute-start.9 = (s16[136,1536]{1,0:T(8,128)(2,1)S(1)}, s16[136,1536]{1,0:T(8,128)(2,1)S(1)}, u32[]{:S(2)}, u32[]{:S(2)}) collective-permute-start(s16[136,1536]{1,0:T(8,128)(2,1)S(1)} %get-tuple-element.62), channel_id=1, source_target_pairs={{0,2},{1,3},{2,0},{3,1},{4,6},{5,7},{6,4},{7,5},{8,10},{9,11},{10,... | collective-permute-start | bytes 1253384 | tf_op jit(solution)/shard_map/ppermute | solution.py:40
  23.1 17.0 %collective-permute-start.6 = (s16[136,1536]{1,0:T(8,128)(2,1)S(1)}, s16[136,1536]{1,0:T(8,128)(2,1)S(1)}, u32[]{:S(2)}, u32[]{:S(2)}) collective-permute-start(s16[136,1536]{1,0:T(8,128)(2,1)S(1)} %get-tuple-element.56), channel_id=1, source_target_pairs={{0,6},{1,7},{2,4},{3,5},{4,2},{5,3},{6,0},{7,1},{8,14},{9,15},{10,... | collective-permute-start | bytes 1253384 | tf_op jit(solution)/shard_map/ppermute | solution.py:40
  27.9 26.9 %collective-permute-start.3 = (s16[136,1536]{1,0:T(8,128)(2,1)S(1)}, s16[136,1536]{1,0:T(8,128)(2,1)S(1)}, u32[]{:S(2)}, u32[]{:S(2)}) collective-permute-start(s16[136,1536]{1,0:T(8,128)(2,1)S(1)} %get-tuple-element.52), channel_id=1, source_target_pairs={{0,7},{1,6},{2,5},{3,4},{4,3},{5,2},{6,1},{7,0},{8,15},{9,14},{10,... | collective-permute-start | bytes 1253384 | tf_op jit(solution)/shard_map/ppermute | solution.py:40
  30.8 29.9 %collective-permute-start.12 = (s16[136,1536]{1,0:T(8,128)(2,1)S(1)}, s16[136,1536]{1,0:T(8,128)(2,1)S(1)}, u32[]{:S(2)}, u32[]{:S(2)}) collective-permute-start(s16[136,1536]{1,0:T(8,128)(2,1)S(1)} %get-tuple-element.65), channel_id=1, source_target_pairs={{0,4},{1,5},{2,6},{3,7},{4,8},{5,9},{6,10},{7,11},{8,12},{9,13},{1... | collective-permute-start | bytes 1253384 | tf_op jit(solution)/shard_map/ppermute | solution.py:40
  31.4 29.3 %collective-permute-start.13 = (s16[136,1536]{1,0:T(8,128)(2,1)S(1)}, s16[136,1536]{1,0:T(8,128)(2,1)S(1)}, u32[]{:S(2)}, u32[]{:S(2)}) collective-permute-start(s16[136,1536]{1,0:T(8,128)(2,1)S(1)} %get-tuple-element.66), channel_id=1, source_target_pairs={{0,8},{1,9},{2,10},{3,11},{4,12},{5,13},{6,14},{7,15},{8,16},{9,17... | collective-permute-start | bytes 1253384 | tf_op jit(solution)/shard_map/ppermute | solution.py:40
  39.0 23.0 %collective-permute-start.10 = (s16[136,1536]{1,0:T(8,128)(2,1)S(1)}, s16[136,1536]{1,0:T(8,128)(2,1)S(1)}, u32[]{:S(2)}, u32[]{:S(2)}) collective-permute-start(s16[136,1536]{1,0:T(8,128)(2,1)S(1)} %collective-permute-done.9), channel_id=1, source_target_pairs={{0,6},{1,7},{2,4},{3,5},{4,2},{5,3},{6,0},{7,1},{8,14},{9,15},{10,... | collective-permute-start | bytes 1253384 | tf_op jit(solution)/shard_map/ppermute | solution.py:40
  40.6 23.4 %collective-permute-start.7 = (s16[136,1536]{1,0:T(8,128)(2,1)S(1)}, s16[136,1536]{1,0:T(8,128)(2,1)S(1)}, u32[]{:S(2)}, u32[]{:S(2)}) collective-permute-start(s16[136,1536]{1,0:T(8,128)(2,1)S(1)} %merge2.1), channel_id=1, source_target_pairs={{0,8},{1,9},{2,10},{3,11},{4,12},{5,13},{6,14},{7,15},{8,16},{9,17... | collective-permute-start | bytes 1253384 | tf_op jit(solution)/shard_map/ppermute | solution.py:40
  42.1 13.4 %copy-start.3 = (f32[1536]{0:T(1024)S(1)}, f32[1536]{0:T(1024)}, u32[]{:S(2)}) copy-start(f32[1536]{0:T(1024)} %param.8) | copy-start | bytes 18436
  42.1 13.4 %copy-start.1 = (bf16[256,3072]{1,0:T(8,128)(2,1)S(1)}, bf16[256,3072]{1,0:T(8,128)(2,1)}, u32[]{:S(2)}) copy-start(bf16[256,3072]{1,0:T(8,128)(2,1)} %get-tuple-element.59.refs_0_) | copy-start | bytes 4718596
  55.4 14.2 %collective-permute-start.4 = (s16[136,1536]{1,0:T(8,128)(2,1)S(1)}, s16[136,1536]{1,0:T(8,128)(2,1)S(1)}, u32[]{:S(2)}, u32[]{:S(2)}) collective-permute-start(s16[136,1536]{1,0:T(8,128)(2,1)S(1)} %merge3.1), channel_id=1, source_target_pairs={{0,8},{1,9},{2,10},{3,11},{4,12},{5,13},{6,14},{7,15},{8,16},{9,17... | collective-permute-start | bytes 1253384 | tf_op jit(solution)/shard_map/ppermute | solution.py:40
  55.5 5.2 %copy-start.4 = (f32[64]{0:T(128)S(1)}, f32[64]{0:T(128)}, u32[]{:S(2)}) copy-start(f32[64]{0:T(128)} %param.9) | copy-start | bytes 772
  61.9 9.0 %collective-permute-start.14 = (s16[136,1536]{1,0:T(8,128)(2,1)S(1)}, s16[136,1536]{1,0:T(8,128)(2,1)S(1)}, u32[]{:S(2)}, u32[]{:S(2)}) collective-permute-start(s16[136,1536]{1,0:T(8,128)(2,1)S(1)} %get-tuple-element.70), channel_id=1, source_target_pairs={{0,1},{1,0},{2,3},{3,2},{4,5},{5,4},{6,7},{7,6},{8,9},{9,8},{10,11... | collective-permute-start | bytes 1253384 | tf_op jit(solution)/shard_map/ppermute | solution.py:40
  62.7 15.4 %collective-permute-start.11 = (s16[136,1536]{1,0:T(8,128)(2,1)S(1)}, s16[136,1536]{1,0:T(8,128)(2,1)S(1)}, u32[]{:S(2)}, u32[]{:S(2)}) collective-permute-start(s16[136,1536]{1,0:T(8,128)(2,1)S(1)} %merge0.1), channel_id=1, source_target_pairs={{0,8},{1,9},{2,10},{3,11},{4,12},{5,13},{6,14},{7,15},{8,16},{9,17... | collective-permute-start | bytes 1253384 | tf_op jit(solution)/shard_map/ppermute | solution.py:40
  65.2 15.5 %collective-permute-start.8 = (s16[136,1536]{1,0:T(8,128)(2,1)S(1)}, s16[136,1536]{1,0:T(8,128)(2,1)S(1)}, u32[]{:S(2)}, u32[]{:S(2)}) collective-permute-start(s16[136,1536]{1,0:T(8,128)(2,1)S(1)} %get-tuple-element.58), channel_id=1, source_target_pairs={{0,2},{1,3},{2,0},{3,1},{4,6},{5,7},{6,4},{7,5},{8,10},{9,11},{10,... | collective-permute-start | bytes 1253384 | tf_op jit(solution)/shard_map/ppermute | solution.py:40
  70.8 14.9 %collective-permute-start.5 = (s16[136,1536]{1,0:T(8,128)(2,1)S(1)}, s16[136,1536]{1,0:T(8,128)(2,1)S(1)}, u32[]{:S(2)}, u32[]{:S(2)}) collective-permute-start(s16[136,1536]{1,0:T(8,128)(2,1)S(1)} %get-tuple-element.54), channel_id=1, source_target_pairs={{0,3},{1,2},{2,1},{3,0},{4,7},{5,6},{6,5},{7,4},{8,11},{9,10},{10,... | collective-permute-start | bytes 1253384 | tf_op jit(solution)/shard_map/ppermute | solution.py:40
